TPU v7x, 32 devices: a whole 2x2x4 slice. The times are simulated.
32 devices in a mesh: res: 8 (over y, x, core), tp: 4 (over z).
Axes of the slice: x: 2, y: 2, z: 4, core: 2. Of those that a mesh axis runs over, the one named last changes fastest.
Arguments:
- node_feats: bfloat16 [2, 4096, 512], P(None, ('res', 'tp')), may hold values from -6 to 6
- edge_feats: bfloat16 [2, 4096, 60, 192], P(None, ('res', 'tp')), may hold values from -6 to 6
- slot_index: int32 [2, 4096, 60], P(None, ('res', 'tp')), may hold values from 0 to 511, as said below
- send_rows: int32 [2, 32, 32, 16], P(None, ('res', 'tp')), may hold values from 0 to 127, as said below
- res_mask: int32 [2, 4096], P(None, ('res', 'tp')), may hold values 0 or 1
- chain_ids: int32 [2, 4096], P(None, ('res', 'tp')), may hold values from 0 to 15, never falling along the last dimension, each value on 1 to 512 neighbouring positions
- node_upstream: bfloat16 [2, 4096, 512], P(None, ('res', 'tp')), may hold values from -6 to 6
- edge_upstream: bfloat16 [2, 4096, 60, 192], P(None, ('res', 'tp')), may hold values from -6 to 6
- message_square: float32 [4, 512, 512], P(None, 'tp'), may hold values from -0.25 to 0.25
- message_edge: float32 [192, 512], P('tp'), may hold values from -0.4375 to 0.4375
- expand_weight: float32 [512, 2048], P('tp'), may hold values from -0.25 to 0.25
- contract_weight: float32 [2048, 512], P('tp'), may hold values from -0.125 to 0.125
- edge_input: float32 [2, 512, 192], P(None, 'tp'), may hold values from -0.25 to 0.25
- edge_square: float32 [3, 192, 192], P(None, 'tp'), may hold values from -0.4375 to 0.4375
- gains_biases: float32 [8256], P('tp')
- message_square_first: float32 [4, 512, 512], P(None, 'tp'), may hold values from -0.0034179688 to 0.0034179688
- message_edge_first: float32 [192, 512], P('tp'), may hold values from -0.00048828125 to 0.00048828125
- expand_weight_first: float32 [512, 2048], P('tp'), may hold values from -0.0034179688 to 0.0034179688
- contract_weight_first: float32 [2048, 512], P('tp'), may hold values from -0.0034179688 to 0.0034179688
- edge_input_first: float32 [2, 512, 192], P(None, 'tp'), may hold values from -0.0034179688 to 0.0034179688
- edge_square_first: float32 [3, 192, 192], P(None, 'tp'), may hold values from -0.0034179688 to 0.0034179688
- gains_biases_first: float32 [8256], P('tp'), may hold values from -0.009765625 to 0.009765625
- message_square_second: float32 [4, 512, 512], P(None, 'tp'), may hold values from 2.8093928e-07 to 1.1237571e-06
- message_edge_second: float32 [192, 512], P('tp'), may hold values from 3.9019343e-09 to 1.5607737e-08
- expand_weight_second: float32 [512, 2048], P('tp'), may hold values from 2.8093928e-07 to 1.1237571e-06
- contract_weight_second: float32 [2048, 512], P('tp'), may hold values from 2.8093928e-07 to 1.1237571e-06
- edge_input_second: float32 [2, 512, 192], P(None, 'tp'), may hold values from 2.8093928e-07 to 1.1237571e-06
- edge_square_second: float32 [3, 192, 192], P(None, 'tp'), may hold values from 2.8093928e-07 to 1.1237571e-06
- gains_biases_second: float32 [8256], P('tp'), may hold values from 2.5284535e-06 to 1.0113814e-05
Outputs:
- node_out: float32 [2, 4096, 512], P(None, ('res', 'tp'))
- edge_out: float32 [2, 4096, 60, 192], P(None, ('res', 'tp'))
- node_grad: float32 [2, 4096, 512], P(None, ('res', 'tp'))
- edge_grad: float32 [2, 4096, 60, 192], P(None, ('res', 'tp'))
- grad_norm: float32 [1], replicated
- new_message_square: float32 [4, 512, 512], P(None, 'tp')
- new_message_edge: float32 [192, 512], P('tp')
- new_expand_weight: float32 [512, 2048], P('tp')
- new_contract_weight: float32 [2048, 512], P('tp')
- new_edge_input: float32 [2, 512, 192], P(None, 'tp')
- new_edge_square: float32 [3, 192, 192], P(None, 'tp')
- new_gains_biases: float32 [8256], P('tp')
- new_message_square_first: float32 [4, 512, 512], P(None, 'tp')
- new_message_edge_first: float32 [192, 512], P('tp')
- new_expand_weight_first: float32 [512, 2048], P('tp')
- new_contract_weight_first: float32 [2048, 512], P('tp')
- new_edge_input_first: float32 [2, 512, 192], P(None, 'tp')
- new_edge_square_first: float32 [3, 192, 192], P(None, 'tp')
- new_gains_biases_first: float32 [8256], P('tp')
- new_message_square_second: float32 [4, 512, 512], P(None, 'tp')
- new_message_edge_second: float32 [192, 512], P('tp')
- new_expand_weight_second: float32 [512, 2048], P('tp')
- new_contract_weight_second: float32 [2048, 512], P('tp')
- new_edge_input_second: float32 [2, 512, 192], P(None, 'tp')
- new_edge_square_second: float32 [3, 192, 192], P(None, 'tp')
- new_gains_biases_second: float32 [8256], P('tp')
Inputs may be any that keep to these rules, and one draw needn't show every extreme that they name: slot_index = s * 16 + c names the row send_rows[m, s, d, c] of device s, d being the device of the edge's residue. `send_rows`: the 16 rows that one device sends to one device are distinct. `chain_ids`: ids never fall along the residues of a micro-batch.
All inputs are finite; a program needn't handle non-finite values. No bound on the sum of `res_mask` on one device may be relied on, other than what follows from the above.
Results may differ from a plain program's by a relative error of at most 0.012.
The roundings to bfloat16 on the way count: a program that leaves them out, or rounds other values in their place, can miss the bound.
Values may be sent and summed in bfloat16 or wider, within the bound.
A program may use at most 384 MiB of HBM per device.

v0:
```python
import jax
import jax.numpy as jnp
from jax import lax
from jax.sharding import PartitionSpec as P

D = 512
E = 192
F = 2048
STEP = 5


norm_eps = 1e-05
learn_rate = 0.03
vector_rate = 0.25
beta_first = 0.5
beta_second = 0.5
adam_eps = 1e-08
decay_rate = 0.01
clip_norm = 1.0


def layer_norm(values, gain_row, shift_row):
    centred = values - jnp.mean(values, axis=-1, keepdims=True)
    spread = jnp.mean(centred * centred, axis=-1, keepdims=True)
    return centred * lax.rsqrt(spread + norm_eps) * gain_row + shift_row


def gelu_back(pre_act, upstream):
    return jax.vjp(jax.nn.gelu, pre_act)[1](upstream)[0]


def mix(left, weight):
    return jnp.einsum("nkd,dh->nkh", left, weight, preferred_element_type=jnp.float32)


def mix_back(upstream, weight):
    return jnp.einsum("nkh,dh->nkd", upstream, weight, preferred_element_type=jnp.float32)


def weight_grad(left, upstream):
    return jnp.einsum("nkd,nkh->dh", left, upstream, preferred_element_type=jnp.float32)


def exact_dot(left, right):
    return jnp.dot(left, right, precision=lax.Precision.HIGHEST)


def fetch_tags(tag_local, row_index):
    res_count = lax.axis_size("res")
    tp_count = lax.axis_size("tp")
    outgoing = tag_local[row_index].reshape(res_count, tp_count, row_index.shape[1])
    arrived = lax.all_to_all(
        lax.all_to_all(outgoing, "res", split_axis=0, concat_axis=0, tiled=True),
        "tp",
        split_axis=1,
        concat_axis=1,
        tiled=True,
    )
    return arrived.reshape(-1)


def fetch_rows(local_rows, row_index):
    res_count = lax.axis_size("res")
    tp_count = lax.axis_size("tp")
    width = local_rows.shape[1]
    outgoing = local_rows[row_index].reshape(res_count, tp_count, row_index.shape[1], width)
    arrived = lax.all_to_all(
        lax.all_to_all(outgoing, "res", split_axis=0, concat_axis=0, tiled=True),
        "tp",
        split_axis=1,
        concat_axis=1,
        tiled=True,
    )
    return arrived.reshape(-1, width)


def fetch_projected(local_rows, row_index):
    res_count = lax.axis_size("res")
    tp_count = lax.axis_size("tp")
    width = local_rows.shape[1]
    outgoing = local_rows[row_index].reshape(res_count, tp_count, row_index.shape[1], width)
    arrived = lax.all_to_all(
        lax.all_to_all(outgoing, "res", split_axis=0, concat_axis=0, tiled=True),
        "tp",
        split_axis=1,
        concat_axis=1,
        tiled=True,
    )
    return arrived.reshape(-1, width)


def return_grads(neigh_grad, slot_index, row_index, local_count):
    res_count = lax.axis_size("res")
    tp_count = lax.axis_size("tp")
    capacity = row_index.shape[1]
    width = neigh_grad.shape[2]
    table_grad = jnp.zeros((res_count * tp_count * capacity, width), jnp.float32)
    table_grad = table_grad.at[slot_index.reshape(-1)].add(neigh_grad.reshape(-1, width))
    incoming = lax.all_to_all(
        lax.all_to_all(
            table_grad.reshape(res_count, tp_count, capacity, width),
            "res",
            split_axis=0,
            concat_axis=0,
            tiled=True,
        ),
        "tp",
        split_axis=1,
        concat_axis=1,
        tiled=True,
    )
    local_grad = jnp.zeros((local_count, width), jnp.float32)
    return local_grad.at[row_index.reshape(-1)].add(incoming.reshape(-1, width))


def return_sums(neigh_grad, slot_index, row_index, local_count):
    res_count = lax.axis_size("res")
    tp_count = lax.axis_size("tp")
    capacity = row_index.shape[1]
    width = neigh_grad.shape[2]
    table_grad = jnp.zeros((res_count * tp_count * capacity, width), jnp.float32)
    table_grad = table_grad.at[slot_index.reshape(-1)].add(neigh_grad.reshape(-1, width))
    incoming = lax.all_to_all(
        lax.all_to_all(
            table_grad.reshape(res_count, tp_count, capacity, width),
            "res",
            split_axis=0,
            concat_axis=0,
            tiled=True,
        ),
        "tp",
        split_axis=1,
        concat_axis=1,
        tiled=True,
    )
    local_grad = jnp.zeros((local_count, width), jnp.float32)
    return local_grad.at[row_index.reshape(-1)].add(incoming.reshape(-1, width))


def run_batch(
    weights,
    node_feats,
    edge_feats,
    slot_index,
    row_index,
    res_mask,
    chain_ids,
    node_upstream,
    edge_upstream,
):
    square, edge_proj, expand_weight, contract_weight, edge_proj_in, edge_sq, vector = weights
    vector_float = vector.astype(jnp.float32)
    node_rows = vector_float[: 11 * D].reshape(11, D)
    expand_bias = vector_float[11 * D : 11 * D + F]
    edge_bias = vector_float[11 * D + F :].reshape(3, E)
    local_count = node_feats.shape[0]
    tag_local = res_mask * (chain_ids + 1)
    tag_table = fetch_tags(tag_local, row_index)
    tag_neigh = tag_table[slot_index]
    edge_valid = ((res_mask[:, None] > 0) & (tag_neigh > 0)).astype(jnp.float32)
    same_chain = (tag_neigh == chain_ids[:, None] + 1).astype(jnp.float32)
    neigh_count = jnp.maximum(jnp.sum(edge_valid, axis=1), 1.0)
    values_in = node_feats.astype(jnp.float32)
    norm_first, first_back = jax.vjp(layer_norm, values_in, node_rows[0], node_rows[1])
    first_low = norm_first.astype(jnp.bfloat16)
    self_term = jnp.dot(first_low, square[0], preferred_element_type=jnp.float32) + node_rows[6]
    first_neigh = fetch_rows(first_low, row_index)[slot_index]
    pre_one = (
        self_term[:, None, :]
        + mix(first_neigh, square[1])
        + mix(edge_feats, edge_proj)
        + same_chain[:, :, None] * node_rows[7]
    )
    act_one = jax.nn.gelu(pre_one).astype(jnp.bfloat16)
    pre_two = mix(act_one, square[2]) + node_rows[8]
    act_two = jax.nn.gelu(pre_two).astype(jnp.bfloat16)
    message = mix(act_two, square[3]) + node_rows[9]
    mixed_rows = (
        values_in + jnp.sum(edge_valid[:, :, None] * message, axis=1) / neigh_count[:, None]
    )
    norm_second, second_back = jax.vjp(layer_norm, mixed_rows, node_rows[2], node_rows[3])
    second_low = norm_second.astype(jnp.bfloat16)
    expand_pre = (
        jnp.dot(second_low, expand_weight, preferred_element_type=jnp.float32) + expand_bias
    )
    expand_act = jax.nn.gelu(expand_pre).astype(jnp.bfloat16)
    node_out = (
        mixed_rows
        + jnp.dot(expand_act, contract_weight, preferred_element_type=jnp.float32)
        + node_rows[10]
    )
    norm_third, third_back = jax.vjp(layer_norm, node_out, node_rows[4], node_rows[5])
    third_low = norm_third.astype(jnp.bfloat16)
    edge_self = (
        jnp.dot(third_low, edge_proj_in[0], preferred_element_type=jnp.float32) + edge_bias[0]
    )
    projected_local = jnp.dot(third_low, edge_proj_in[1], preferred_element_type=jnp.float32)
    neigh_term = fetch_projected(projected_local, row_index)[slot_index]
    edge_pre_one = edge_self[:, None, :] + neigh_term + mix(edge_feats, edge_sq[0])
    edge_act_one = jax.nn.gelu(edge_pre_one).astype(jnp.bfloat16)
    edge_pre_two = mix(edge_act_one, edge_sq[1]) + edge_bias[1]
    edge_act_two = jax.nn.gelu(edge_pre_two).astype(jnp.bfloat16)
    edge_delta = mix(edge_act_two, edge_sq[2]) + edge_bias[2]
    edge_out = edge_feats.astype(jnp.float32) + edge_valid[:, :, None] * edge_delta
    node_up = node_upstream.astype(jnp.float32)
    edge_up = edge_upstream.astype(jnp.float32)
    grad_delta = (edge_valid[:, :, None] * edge_up).astype(jnp.bfloat16)
    grad_vthird = weight_grad(edge_act_two, grad_delta)
    grad_dthird = jnp.sum(grad_delta.astype(jnp.float32), axis=(0, 1))
    grad_edge_two = gelu_back(edge_pre_two, mix_back(grad_delta, edge_sq[2])).astype(jnp.bfloat16)
    grad_vsecond = weight_grad(edge_act_one, grad_edge_two)
    grad_dsecond = jnp.sum(grad_edge_two.astype(jnp.float32), axis=(0, 1))
    grad_edge_one = gelu_back(edge_pre_one, mix_back(grad_edge_two, edge_sq[1])).astype(
        jnp.bfloat16
    )
    grad_vedge = weight_grad(edge_feats, grad_edge_one)
    grad_edge_self = jnp.sum(grad_edge_one.astype(jnp.float32), axis=1)
    grad_dfirst = jnp.sum(grad_edge_self, axis=0)
    grad_vself = exact_dot(third_low.astype(jnp.float32).T, grad_edge_self)
    grad_third = exact_dot(grad_edge_self, edge_proj_in[0].astype(jnp.float32).T)
    grad_edges = edge_up + mix_back(grad_edge_one, edge_sq[0])
    row_sums = return_sums(grad_edge_one.astype(jnp.float32), slot_index, row_index, local_count)
    grad_vneigh = exact_dot(third_low.astype(jnp.float32).T, row_sums)
    grad_third = grad_third + exact_dot(row_sums, edge_proj_in[1].astype(jnp.float32).T)
    grad_out_norm, grad_gain_three, grad_shift_three = third_back(grad_third)
    grad_node_out = node_up + grad_out_norm
    grad_contract_in = grad_node_out.astype(jnp.bfloat16)
    grad_contract = jnp.dot(expand_act.T, grad_contract_in, preferred_element_type=jnp.float32)
    grad_cfive = jnp.sum(grad_contract_in.astype(jnp.float32), axis=0)
    grad_expand_pre = gelu_back(
        expand_pre, jnp.dot(grad_contract_in, contract_weight.T, preferred_element_type=jnp.float32)
    ).astype(jnp.bfloat16)
    grad_expand = jnp.dot(second_low.T, grad_expand_pre, preferred_element_type=jnp.float32)
    grad_cfour = jnp.sum(grad_expand_pre.astype(jnp.float32), axis=0)
    grad_mixed_norm, grad_gain_two, grad_shift_two = second_back(
        jnp.dot(grad_expand_pre, expand_weight.T, preferred_element_type=jnp.float32)
    )
    grad_mixed = grad_node_out + grad_mixed_norm
    grad_message = (
        edge_valid[:, :, None] * (grad_mixed / neigh_count[:, None])[:, None, :]
    ).astype(jnp.bfloat16)
    grad_wthird = weight_grad(act_two, grad_message)
    grad_cthree = jnp.sum(grad_message.astype(jnp.float32), axis=(0, 1))
    grad_pre_two = gelu_back(pre_two, mix_back(grad_message, square[3])).astype(jnp.bfloat16)
    grad_wsecond = weight_grad(act_one, grad_pre_two)
    grad_ctwo = jnp.sum(grad_pre_two.astype(jnp.float32), axis=(0, 1))
    grad_pre_one = gelu_back(pre_one, mix_back(grad_pre_two, square[2])).astype(jnp.bfloat16)
    grad_wedge = weight_grad(edge_feats, grad_pre_one)
    grad_wneigh = weight_grad(first_neigh, grad_pre_one)
    grad_chain = jnp.sum(same_chain[:, :, None] * grad_pre_one.astype(jnp.float32), axis=(0, 1))
    grad_self_term = jnp.sum(grad_pre_one.astype(jnp.float32), axis=1)
    grad_cone = jnp.sum(grad_self_term, axis=0)
    grad_wself = exact_dot(first_low.astype(jnp.float32).T, grad_self_term)
    grad_first = exact_dot(grad_self_term, square[0].astype(jnp.float32).T)
    grad_edges = grad_edges + mix_back(grad_pre_one, edge_proj)
    grad_first = grad_first + return_grads(
        mix_back(grad_pre_one, square[1]), slot_index, row_index, local_count
    )
    grad_in_norm, grad_gain_one, grad_shift_one = first_back(grad_first)
    grad_nodes = grad_mixed + grad_in_norm
    node_vectors = jnp.stack(
        [
            grad_gain_one,
            grad_shift_one,
            grad_gain_two,
            grad_shift_two,
            grad_gain_three,
            grad_shift_three,
            grad_cone,
            grad_chain,
            grad_ctwo,
            grad_cthree,
            grad_cfive,
        ]
    )
    vector_grad = jnp.concatenate(
        [node_vectors.reshape(-1), grad_cfour, grad_dfirst, grad_dsecond, grad_dthird]
    )
    local_grads = (
        jnp.stack([grad_wself, grad_wneigh, grad_wsecond, grad_wthird]),
        grad_wedge,
        grad_expand,
        grad_contract,
        jnp.stack([grad_vself, grad_vneigh]),
        jnp.stack([grad_vedge, grad_vsecond, grad_vthird]),
        vector_grad,
    )
    return (node_out, edge_out, grad_nodes, grad_edges, local_grads)


def add_parts(left_parts, right_parts):
    if left_parts is None:
        return right_parts
    return tuple((left_item + right_item for left_item, right_item in zip(left_parts, right_parts)))


def shards(
    node_feats,
    edge_feats,
    slot_index,
    send_rows,
    res_mask,
    chain_ids,
    node_upstream,
    edge_upstream,
    message_square,
    message_edge,
    expand_weight,
    contract_weight,
    edge_input,
    edge_square,
    gains_biases,
    message_square_first,
    message_edge_first,
    expand_weight_first,
    contract_weight_first,
    edge_input_first,
    edge_square_first,
    gains_biases_first,
    message_square_second,
    message_edge_second,
    expand_weight_second,
    contract_weight_second,
    edge_input_second,
    edge_square_second,
    gains_biases_second,
):
    masters = (
        message_square,
        message_edge,
        expand_weight,
        contract_weight,
        edge_input,
        edge_square,
        gains_biases,
    )
    firsts = (
        message_square_first,
        message_edge_first,
        expand_weight_first,
        contract_weight_first,
        edge_input_first,
        edge_square_first,
        gains_biases_first,
    )
    seconds = (
        message_square_second,
        message_edge_second,
        expand_weight_second,
        contract_weight_second,
        edge_input_second,
        edge_square_second,
        gains_biases_second,
    )
    node_outs, edge_outs, node_grads, edge_grads = ([], [], [], [])
    shard_total = None
    for batch_index in range(node_feats.shape[0]):
        gathered = (
            lax.all_gather(message_square.astype(jnp.bfloat16), "tp", axis=1, tiled=True),
            lax.all_gather(message_edge.astype(jnp.bfloat16), "tp", axis=0, tiled=True),
            lax.all_gather(expand_weight.astype(jnp.bfloat16), "tp", axis=0, tiled=True),
            lax.all_gather(contract_weight.astype(jnp.bfloat16), "tp", axis=0, tiled=True),
            lax.all_gather(edge_input.astype(jnp.bfloat16), "tp", axis=1, tiled=True),
            lax.all_gather(edge_square.astype(jnp.bfloat16), "tp", axis=1, tiled=True),
            lax.all_gather(gains_biases.astype(jnp.bfloat16), "tp", axis=0, tiled=True),
        )
        node_out, edge_out, grad_nodes, grad_edges, local_grads = run_batch(
            gathered,
            node_feats[batch_index],
            edge_feats[batch_index],
            slot_index[batch_index],
            send_rows[batch_index, 0],
            res_mask[batch_index],
            chain_ids[batch_index],
            node_upstream[batch_index],
            edge_upstream[batch_index],
        )
        node_outs.append(node_out)
        edge_outs.append(edge_out)
        node_grads.append(grad_nodes)
        edge_grads.append(grad_edges)
        shard_total = add_parts(
            shard_total,
            lax.psum(
                (
                    lax.psum_scatter(local_grads[0], "tp", scatter_dimension=1, tiled=True),
                    lax.psum_scatter(local_grads[1], "tp", scatter_dimension=0, tiled=True),
                    lax.psum_scatter(local_grads[2], "tp", scatter_dimension=0, tiled=True),
                    lax.psum_scatter(local_grads[3], "tp", scatter_dimension=0, tiled=True),
                    lax.psum_scatter(local_grads[4], "tp", scatter_dimension=1, tiled=True),
                    lax.psum_scatter(local_grads[5], "tp", scatter_dimension=1, tiled=True),
                    lax.psum_scatter(local_grads[6], "tp", scatter_dimension=0, tiled=True),
                ),
                "res",
            ),
        )
    square_sum = jnp.zeros((), jnp.float32)
    for grad_part in shard_total:
        square_sum = square_sum + jnp.sum(grad_part * grad_part)
    grad_norm = jnp.sqrt(lax.psum(square_sum, "tp"))
    clip_scale = clip_norm / jnp.maximum(grad_norm, clip_norm)
    first_fix = 1.0 - beta_first**STEP
    second_fix = 1.0 - beta_second**STEP
    decays = (decay_rate, decay_rate, decay_rate, decay_rate, decay_rate, decay_rate, 0.0)
    step_rates = (
        learn_rate,
        learn_rate,
        learn_rate,
        learn_rate,
        learn_rate,
        learn_rate,
        vector_rate,
    )
    new_weights, new_firsts, new_seconds = ([], [], [])
    for master, first_moment, second_moment, grad_part, decay_now, rate_now in zip(
        masters, firsts, seconds, shard_total, decays, step_rates
    ):
        clipped = grad_part * clip_scale
        first_new = beta_first * first_moment + (1.0 - beta_first) * clipped
        second_new = beta_second * second_moment + (1.0 - beta_second) * clipped * clipped
        step_size = first_new / first_fix / (jnp.sqrt(second_new / second_fix) + adam_eps)
        new_weights.append(master - rate_now * (step_size + decay_now * master))
        new_firsts.append(first_new)
        new_seconds.append(second_new)
    return (
        jnp.stack(node_outs),
        jnp.stack(edge_outs),
        jnp.stack(node_grads),
        jnp.stack(edge_grads),
        grad_norm.reshape(1),
        new_weights[0],
        new_weights[1],
        new_weights[2],
        new_weights[3],
        new_weights[4],
        new_weights[5],
        new_weights[6],
        new_firsts[0],
        new_firsts[1],
        new_firsts[2],
        new_firsts[3],
        new_firsts[4],
        new_firsts[5],
        new_firsts[6],
        new_seconds[0],
        new_seconds[1],
        new_seconds[2],
        new_seconds[3],
        new_seconds[4],
        new_seconds[5],
        new_seconds[6],
    )


def solution(mesh):
    placed = (
        P(None, ("res", "tp"), None),
        P(None, ("res", "tp"), None, None),
        P(None, ("res", "tp"), None),
        P(None, ("res", "tp"), None, None),
        P(None, ("res", "tp")),
        P(None, ("res", "tp")),
        P(None, ("res", "tp"), None),
        P(None, ("res", "tp"), None, None),
        P(None, "tp", None),
        P("tp", None),
        P("tp", None),
        P("tp", None),
        P(None, "tp", None),
        P(None, "tp", None),
        P("tp"),
        P(None, "tp", None),
        P("tp", None),
        P("tp", None),
        P("tp", None),
        P(None, "tp", None),
        P(None, "tp", None),
        P("tp"),
        P(None, "tp", None),
        P("tp", None),
        P("tp", None),
        P("tp", None),
        P(None, "tp", None),
        P(None, "tp", None),
        P("tp"),
    )
    return jax.shard_map(
        shards,
        mesh=mesh,
        in_specs=placed,
        out_specs=(
            P(None, ("res", "tp"), None),
            P(None, ("res", "tp"), None, None),
            P(None, ("res", "tp"), None),
            P(None, ("res", "tp"), None, None),
            P(),
            P(None, "tp", None),
            P("tp", None),
            P("tp", None),
            P("tp", None),
            P(None, "tp", None),
            P(None, "tp", None),
            P("tp"),
            P(None, "tp", None),
            P("tp", None),
            P("tp", None),
            P("tp", None),
            P(None, "tp", None),
            P(None, "tp", None),
            P("tp"),
            P(None, "tp", None),
            P("tp", None),
            P("tp", None),
            P("tp", None),
            P(None, "tp", None),
            P(None, "tp", None),
            P("tp"),
        ),
        check_vma=False,
    )
```

profile of v0, /device:TPU:0, one launch (start us, length us, event | category | flops | bytes accessed | tf_op | source)
XLA Modules:
  0.0 1396.8 jit_solution(7868334822839587192)
XLA Ops:
  24.2 20.3 %all-reduce = bf16[8256]{0:T(1024)(128)(2,1)S(1)} all-reduce(bf16[8256]{0:T(1024)(128)(2,1)S(1)} %dynamic-update-slice), channel_id=1, replica_groups=mesh['res'=8,'tp'=4] {'tp'}, use_global_device_ids=true, to_apply=%add | all-reduce | flops 8256 | bytes 33024
  94.4 15.3 %all_gather.30 = bf16[192,512]{1,0:T(8,128)(2,1)S(1)} all-gather(bf16[48,512]{1,0:T(8,128)(2,1)S(1)} %convert_element_type.299), channel_id=1, replica_groups=mesh['res'=8,'tp'=4] {'tp'}, dimensions={0}, use_global_device_ids=true | all-gather | bytes 245760 | tf_op jit(solution)/shard_map/all_gather | solution.py:360
  109.7 14.7 %all_gather.33 = bf16[2,512,192]{1,2,0:T(8,128)(2,1)} all-gather(bf16[2,128,192]{1,2,0:T(8,128)(2,1)S(1)} %convert_element_type.320), channel_id=1, replica_groups=mesh['res'=8,'tp'=4] {'tp'}, dimensions={1}, use_global_device_ids=true | all-gather | bytes 491520 | tf_op jit(solution)/shard_map/all_gather | solution.py:363
  134.1 45.2 %gather_fusion.1 = s32[7680]{0:T(1024)S(1)} fusion(s32[512]{0:T(512)S(1)} %reshape.780, s32[8192]{0:T(1024)S(1)} %pad_clamp_fusion.1), kind=kCustom, calls=%fused_computation.1 | custom fusion | bytes 92160 | tf_op jit(solution)/shard_map/gather | solution.py:159
  179.4 45.2 %gather_fusion.5 = s32[7680]{0:T(1024)S(1)} fusion(s32[512]{0:T(512)S(1)} %reshape.784, s32[8192]{0:T(1024)S(1)} %pad_clamp_fusion), kind=kCustom, calls=%fused_computation.5 | custom fusion | bytes 92160 | tf_op jit(solution)/shard_map/gather | solution.py:159
  233.5 22.1 %gather_fusion.7 = bf16[7680,512]{1,0:T(8,128)(2,1)} fusion(bf16[512,512]{1,0:T(8,128)(2,1)S(1)} %bitcast.522, s32[8192]{0:T(1024)S(1)} %pad_clamp_fusion), kind=kCustom, calls=%fused_computation.7 | custom fusion | bytes 15759360 | tf_op jit(solution)/shard_map/gather | solution.py:167
  255.6 11.1 reshape.877
  266.6 12.9 copy.396
  279.5 22.2 %gather_fusion.3 = bf16[7680,512]{1,0:T(8,128)(2,1)} fusion(bf16[512,512]{1,0:T(8,128)(2,1)S(1)} %bitcast.523, s32[8192]{0:T(1024)S(1)} %pad_clamp_fusion.1), kind=kCustom, calls=%fused_computation.3 | custom fusion | bytes 15759360 | tf_op jit(solution)/shard_map/gather | solution.py:167
  301.8 11.1 reshape.845
  312.8 13.0 copy.393
  334.0 9.8 multiply_add_fusion.1
  352.0 9.9 multiply_add_fusion
  361.9 12.2 fusion.185
  374.1 25.4 %multiply_convert_fusion.4 = (bf16[128,60,512]{2,0,1:T(8,128)(2,1)}, bf16[128,60,512]{2,0,1:T(8,128)(2,1)}, f32[128,60,512]{2,0,1:T(8,128)}) fusion(f32[512]{0:T(512)S(1)} %copy-done.191, f32[128,60,512]{2,0,1:T(8,128)} %fusion.185, bf16[4,512,512]{2,1,0:T(8,128)(2,1)S(1)} %copy-done.30, f32[128,60,512]{2,0,1:T(8,128)} %multiply_add_fusion.1), kind=kOutput, calls=%fused_computation.75 | convolution fusion | flops 4140564480 | bytes 63440896 | tf_op jit(solution)/shard_map/nkd,dh->nkh/dot_general | solution.py:33
  428.3 14.8 %all_gather.34 = bf16[3,192,192]{2,1,0:T(8,128)(2,1)S(1)} all-gather(bf16[3,48,192]{2,1,0:T(8,128)(2,1)S(1)} %convert_element_type.321), channel_id=1, replica_groups=mesh['res'=8,'tp'=4] {'tp'}, dimensions={1}, use_global_device_ids=true | all-gather | bytes 276480 | tf_op jit(solution)/shard_map/all_gather | solution.py:364
  466.9 9.5 all-to-all-done.9
  481.1 18.9 %gather_fusion.9 = f32[7680,192]{1,0:T(8,128)} fusion(f32[512,192]{1,0:T(8,128)S(1)} %bitcast.520, s32[8192]{0:T(1024)S(1)} %pad_clamp_fusion.1), kind=kCustom, calls=%fused_computation.9 | custom fusion | bytes 11827200 | tf_op jit(solution)/shard_map/gather | solution.py:198
  500.0 9.2 reshape.893
  545.0 19.1 %gather_fusion.11 = f32[7680,192]{1,0:T(8,128)} fusion(f32[512,192]{1,0:T(8,128)S(1)} %bitcast.521, s32[8192]{0:T(1024)S(1)} %copy-done.69), kind=kCustom, calls=%fused_computation.11 | custom fusion | bytes 11827200 | tf_op jit(solution)/shard_map/gather | solution.py:198
  564.1 9.2 reshape.909
  612.3 9.2 reshape.952
  621.5 42.9 %scatter_custom_fusion.4 = f32[512,192]{1,0:T(8,128)} fusion(s32[7680]{0:T(1024)} %fusion.263, f32[7680,192]{1,0:T(8,128)} %reshape.952, f32[]{:T(128)} %constant.52.clone.1), kind=kCustom, calls=%fused_computation.357 | custom fusion | flops 1474560 | bytes 393728 | tf_op jit(solution)/shard_map/scatter-add | solution.py:122
  683.0 9.2 reshape.920
  692.2 42.7 %scatter_custom_fusion = f32[512,192]{1,0:T(8,128)} fusion(s32[7680]{0:T(1024)} %fusion.262, f32[7680,192]{1,0:T(8,128)} %reshape.920, f32[]{:T(128)} %constant.52.clone.1), kind=kCustom, calls=%fused_computation.359 | custom fusion | flops 1474560 | bytes 393728 | tf_op jit(solution)/shard_map/scatter-add | solution.py:122
  780.4 11.4 all-to-all-done.13
  818.4 16.2 %convert_reduce_fusion.7 = (f32[512]{0:T(512)}, bf16[128,60,512]{2,0,1:T(8,128)(2,1)S(1)}) fusion(f32[128,60,512]{2,0,1:T(8,128)S(1)} %bitcast.577, f32[512]{0:T(512)S(1)} %copy-done.192, bf16[4,512,512]{2,1,0:T(8,128)(2,1)S(1)} %copy-done.31, f32[128,512]{1,0:T(8,128)S(1)} %get-tuple-element.248, f32[128,60]{0,1:T(8,128)S(1)} %copy-done.104), kind=kOutput, calls=%fused_computation.67 | convolution fusion | flops 4124835328 | bytes 24416256 | tf_op jit(solution)/shard_map/nkh,dh->nkd/dot_general | solution.py:37
  837.8 10.1 convolution_bitcast_fusion.4
  847.9 19.1 %fusion.28 = (f32[512]{0:T(512)}, f32[512]{0:T(512)}, f32[128,512]{1,0:T(8,128)S(1)}, bf16[128,60,512]{2,0,1:T(8,128)(2,1)S(1)}) fusion(f32[128,60]{0,1:T(8,128)S(1)} %copy-done.116, f32[128,60,512]{2,0,1:T(8,128)} %multiply_add_fusion.1, bf16[128,60,512]{2,0,1:T(8,128)(2,1)} %copy-done.222, bf16[4,512,512]{2,1,0:T(8,128)(2,1)S(1)} %copy-done.31), kind=kOutput, calls=%fused_computation.62 | convolution fusion | flops 4124769280 | bytes 32280576 | tf_op jit(solution)/shard_map/nkh,dh->nkd/dot_general | solution.py:37
  874.5 19.0 %convert_reduce_fusion.5 = (f32[512]{0:T(512)}, bf16[128,60,512]{2,0,1:T(8,128)(2,1)}) fusion(f32[128,60,512]{2,0,1:T(8,128)} %fusion.185, f32[512]{0:T(512)S(1)} %copy-done.192, bf16[4,512,512]{2,1,0:T(8,128)(2,1)S(1)} %copy-done.31, f32[128,512]{1,0:T(8,128)S(1)} %get-tuple-element.247, f32[128,60]{0,1:T(8,128)S(1)} %copy-done.101), kind=kOutput, calls=%fused_computation.65 | convolution fusion | flops 4124835328 | bytes 24416256 | tf_op jit(solution)/shard_map/nkh,dh->nkd/dot_general | solution.py:37
  893.6 12.3 convolution_bitcast_fusion.2
  905.9 19.1 %fusion.29 = (f32[512]{0:T(512)}, f32[512]{0:T(512)}, f32[128,512]{1,0:T(8,128)}, bf16[128,60,512]{2,0,1:T(8,128)(2,1)S(1)}) fusion(f32[128,60]{0,1:T(8,128)S(1)} %copy-done.114, f32[128,60,512]{2,0,1:T(8,128)} %multiply_add_fusion, bf16[128,60,512]{2,0,1:T(8,128)(2,1)} %get-tuple-element.313, bf16[4,512,512]{2,1,0:T(8,128)(2,1)S(1)} %copy-done.31), kind=kOutput, calls=%fused_computation.63 | convolution fusion | flops 4124769280 | bytes 32280576 | tf_op jit(solution)/shard_map/nkh,dh->nkd/dot_general | solution.py:37
  966.9 9.4 add_bitcast_fusion.1
  984.6 11.3 copy.388
  995.9 11.2 copy.378
  1007.1 11.1 dot_general.272
  1018.2 11.2 dot_general.261
  1029.4 11.1 fusion.177
  1040.5 47.1 %scatter_custom_fusion.2 = f32[512,512]{1,0:T(8,128)} fusion(s32[7680]{0:T(1024)} %fusion.262, f32[7680,512]{1,0:T(8,128)} %fusion.177, f32[]{:T(128)} %constant.52.clone.1), kind=kCustom, calls=%fused_computation.283 | custom fusion | flops 3932160 | bytes 1049088 | tf_op jit(solution)/shard_map/scatter-add | solution.py:98
  1092.3 11.2 fusion.175
  1103.5 47.1 %scatter_custom_fusion.6 = f32[512,512]{1,0:T(8,128)} fusion(s32[7680]{0:T(1024)} %fusion.263, f32[7680,512]{1,0:T(8,128)} %fusion.175, f32[]{:T(128)} %constant.52.clone.1), kind=kCustom, calls=%fused_computation.281 | custom fusion | flops 3932160 | bytes 1049088 | tf_op jit(solution)/shard_map/scatter-add | solution.py:98
  1154.9 10.6 pad_maximum_fusion
  1193.6 37.0 %all-to-all-done.15 = f32[8,4,16,512]{3,2,0,1:T(8,128)} async-done(((f32[8,4,16,512]{3,2,0,1:T(8,128)}), f32[8,4,16,512]{3,2,0,1:T(8,128)}, u32[]{:S(2)}, u32[]{:S(2)}) %all-to-all-start.15) | async-done | bytes 1048608 | tf_op jit(solution)/shard_map/all_to_all | solution.py:99
  1243.1 8.7 pad_maximum_fusion.1
  1270.0 17.5 %all-reduce.2 = f32[8256]{0:T(1024)S(1)} all-reduce(f32[8256]{0:T(1024)S(1)} %add.914), channel_id=15, replica_groups=mesh['res'=8,'tp'=4] {'tp'}, use_global_device_ids=true, to_apply=%region_85.0.clone | all-reduce | flops 8256 | bytes 66048
  1287.5 22.5 %psum.126 = f32[2064]{0:T(1024)S(1)} all-reduce(f32[2064]{0:T(1024)S(1)} %dynamic-slice.4), channel_id=1, replica_groups=mesh['res'=8,'tp'=4] {'res'}, use_global_device_ids=true, to_apply=%region_86.0 | all-reduce | flops 2064 | bytes 16512 | tf_op jit(solution)/shard_map/psum | solution.py:384
  1311.8 30.0 %all-reduce.9.cloned.1.call-done = (f32[4,128,512]{2,1,0:T(8,128)}, f32[48,512]{1,0:T(8,128)}, f32[128,2048]{1,0:T(8,128)}, f32[512,512]{1,0:T(8,128)}, f32[2,128,192]{1,2,0:T(8,128)}, /*index=5*/f32[3,48,192]{2,1,0:T(8,128)}) async-done(((f32[4,128,512]{2,1,0:T(8,128)}, f32[48,512]{1,0:T(8,128)}, f32[128,2048]{1,0:T(8,128)}, f32[512,512]{1,0:T(8,128)}, f32[2,128,192]{1,2,0:T(8,128)}, ...) | async-done | bytes 3551248 | tf_op jit(solution)/shard_map/psum | solution.py:384
  1359.3 12.4 psum.119
  (782 shorter events, 478.7 us)
Async XLA Ops:
  7.2 318.6 %all-gather.4.cloned.1.call-start = ((), (), s32[]{:S(2)}) async-start(), calls=%async_computation.25 | async-start | bytes 2621440 | tf_op jit(solution)/shard_map/all_gather | solution.py:359
  9.4 402.8 %all-gather.6.cloned.1.call-start = ((), (), s32[]{:S(2)}) async-start(), calls=%async_computation.26 | async-start | bytes 2621440 | tf_op jit(solution)/shard_map/all_gather | solution.py:361
  12.4 68.3 %copy-start.87 = (s32[1024]{0:T(1024)}, s32[1024]{0:T(1024)S(1)}, u32[]{:S(2)}) copy-start(s32[1024]{0:T(1024)S(1)} %pad_clamp_fusion.3) | copy-start | bytes 12292
  17.3 32.3 %all-to-all-start = ((s32[8,4,16]{2,1,0:T(4,128)}), s32[8,4,16]{2,1,0:T(4,128)S(1)}, u32[]{:S(2)}, u32[]{:S(2)}) async-start(s32[8,4,16]{2,1,0:T(4,128)} %reshape.779), calls=%async_computation | async-start | bytes 32768 | tf_op jit(solution)/shard_map/all_to_all | solution.py:53
  44.5 48.1 %copy-start.112 = (bf16[8256]{0:T(1024)(128)(2,1)}, bf16[8256]{0:T(1024)(128)(2,1)S(1)}, u32[]{:S(2)}) copy-start(bf16[8256]{0:T(1024)(128)(2,1)S(1)} %all-reduce) | copy-start | bytes 49540
  44.6 281.2 %copy-start.134 = (f32[128]{0:T(128)}, f32[128]{0:T(128)S(1)}, u32[]{:S(2)}) copy-start(f32[128]{0:T(128)S(1)} %get-tuple-element.319) | copy-start | bytes 1540
  44.6 299.2 %copy-start.132 = (f32[128]{0:T(128)}, f32[128]{0:T(128)S(1)}, u32[]{:S(2)}) copy-start(f32[128]{0:T(128)S(1)} %get-tuple-element.318) | copy-start | bytes 1540
  45.5 298.3 %copy-start.123 = (f32[512]{0:T(512)}, f32[512]{0:T(512)S(1)}, u32[]{:S(2)}) copy-start(f32[512]{0:T(512)S(1)} %get-tuple-element.269) | copy-start | bytes 6148
  49.6 8.8 all-to-all-start.4
  53.7 272.2 %copy-start.173 = (f32[128]{0:T(128)}, f32[128]{0:T(128)S(1)}, u32[]{:S(2)}) copy-start(f32[128]{0:T(128)S(1)} %fusion.267) | copy-start | bytes 1540
  58.4 8.7 all-to-all-start.1
  61.6 282.2 %copy-start.175 = (f32[128]{0:T(128)}, f32[128]{0:T(128)S(1)}, u32[]{:S(2)}) copy-start(f32[128]{0:T(128)S(1)} %fusion.269) | copy-start | bytes 1540
  67.1 8.8 all-to-all-start.5
  73.2 51.2 %copy-start.181 = (s32[2,128]{1,0:T(2,128)S(1)}, s32[2,128]{1,0:T(2,128)}, u32[]{:S(2)}) copy-start(s32[2,128]{1,0:T(2,128)} %param.33) | copy-start | bytes 3076
  75.9 13.2 all-to-all-start.6
  79.4 51.2 %copy-start.182 = (s32[2,128]{1,0:T(2,128)S(1)}, s32[2,128]{1,0:T(2,128)}, u32[]{:S(2)}) copy-start(s32[2,128]{1,0:T(2,128)} %param.34) | copy-start | bytes 3076
  79.4 336.0 %all-gather.8.cloned.1.call-start = ((), (), s32[]{:S(2)}) async-start(), calls=%async_computation.27 | async-start | bytes 2621440 | tf_op jit(solution)/shard_map/all_gather | solution.py:362
  89.1 36.1 %all-to-all-start.2 = ((bf16[8,4,16,512]{3,2,1,0:T(8,128)(2,1)}), bf16[8,4,16,512]{3,2,1,0:T(8,128)(2,1)S(1)}, u32[]{:S(2)}, u32[]{:S(2)}) async-start(bf16[8,4,16,512]{3,2,1,0:T(8,128)(2,1)} %bitcast.8), calls=%async_computation.2 | async-start | bytes 1048576 | tf_op jit(solution)/shard_map/all_to_all | solution.py:68
  109.7 242.3 %copy-start.28 = (bf16[192,512]{1,0:T(8,128)(2,1)}, bf16[192,512]{1,0:T(8,128)(2,1)S(1)}, u32[]{:S(2)}) copy-start(bf16[192,512]{1,0:T(8,128)(2,1)S(1)} %all_gather.30) | copy-start | bytes 589828
  125.2 100.4 %all-to-all-start.7 = ((bf16[8,4,16,512]{3,2,0,1:T(8,128)(2,1)}), bf16[8,4,16,512]{3,2,0,1:T(8,128)(2,1)S(1)}, u32[]{:S(2)}, u32[]{:S(2)}) async-start(bf16[8,4,16,512]{3,2,0,1:T(8,128)(2,1)} %copy.356), calls=%async_computation.7 | async-start | bytes 1048576 | tf_op jit(solution)/shard_map/all_to_all | solution.py:67
  130.6 102.9 %copy-start.68 = (s32[8192]{0:T(1024)}, s32[8192]{0:T(1024)S(1)}, u32[]{:S(2)}) copy-start(s32[8192]{0:T(1024)S(1)} %pad_clamp_fusion) | copy-start | bytes 98308
  225.6 53.9 %all-to-all-start.3 = ((bf16[8,4,16,512]{3,2,0,1:T(8,128)(2,1)}), bf16[8,4,16,512]{3,2,0,1:T(8,128)(2,1)S(1)}, u32[]{:S(2)}, u32[]{:S(2)}) async-start(bf16[8,4,16,512]{3,2,0,1:T(8,128)(2,1)} %copy.347), calls=%async_computation.3 | async-start | bytes 1048576 | tf_op jit(solution)/shard_map/all_to_all | solution.py:67
  231.6 120.3 %copy-start.113 = (f32[128,60]{0,1:T(8,128)}, f32[128,60]{0,1:T(8,128)S(1)}, u32[]{:S(2)}) copy-start(f32[128,60]{0,1:T(8,128)S(1)} %copy.359) | copy-start | bytes 92164
  231.7 102.3 %copy-start.115 = (f32[128,60]{0,1:T(8,128)}, f32[128,60]{0,1:T(8,128)S(1)}, u32[]{:S(2)}) copy-start(f32[128,60]{0,1:T(8,128)S(1)} %copy.350) | copy-start | bytes 92164
  423.4 22.2 %all-to-all-start.8 = ((f32[8,4,16,192]{3,2,1,0:T(8,128)}), f32[8,4,16,192]{3,2,1,0:T(8,128)S(1)}, u32[]{:S(2)}, u32[]{:S(2)}) async-start(f32[8,4,16,192]{3,2,1,0:T(8,128)} %bitcast.31), calls=%async_computation.8 | async-start | bytes 1048576 | tf_op jit(solution)/shard_map/all_to_all | solution.py:83
  443.1 85.1 %copy-start.65 = (bf16[3,192,192]{2,1,0:T(8,128)(2,1)}, bf16[3,192,192]{2,1,0:T(8,128)(2,1)S(1)}, u32[]{:S(2)}) copy-start(bf16[3,192,192]{2,1,0:T(8,128)(2,1)S(1)} %all_gather.34) | copy-start | bytes 663556
  445.6 13.7 all-to-all-start.10
  451.6 141.1 %copy-start.204 = (f32[192]{0:T(256)}, f32[192]{0:T(256)S(1)}, u32[]{:S(2)}) copy-start(f32[192]{0:T(256)S(1)} %get-tuple-element.257) | copy-start | bytes 2308
  459.3 17.2 %all-to-all-start.9 = ((f32[8,4,16,192]{3,2,0,1:T(8,128)}), f32[8,4,16,192]{3,2,0,1:T(8,128)S(1)}, u32[]{:S(2)}, u32[]{:S(2)}) async-start(f32[8,4,16,192]{3,2,0,1:T(8,128)} %copy.361), calls=%async_computation.9 | async-start | bytes 1048576 | tf_op jit(solution)/shard_map/all_to_all | solution.py:82
  476.5 67.4 %all-to-all-start.11 = ((f32[8,4,16,192]{3,2,0,1:T(8,128)}), f32[8,4,16,192]{3,2,0,1:T(8,128)}, u32[]{:S(2)}, u32[]{:S(2)}) async-start(f32[8,4,16,192]{3,2,0,1:T(8,128)} %copy.368), calls=%async_computation.11 | async-start | bytes 1048576 | tf_op jit(solution)/shard_map/all_to_all | solution.py:82
  540.9 198.9 %copy-start.10 = (bf16[128,60,192]{0,2,1:T(8,128)(2,1)}, bf16[128,60,192]{0,2,1:T(8,128)(2,1)S(1)}, u32[]{:S(2)}) copy-start(bf16[128,60,192]{0,2,1:T(8,128)(2,1)S(1)} %get-tuple-element.303) | copy-start | bytes 8847364
  664.4 70.4 %all-to-all-start.16 = ((f32[8,4,16,192]{3,2,1,0:T(8,128)}), f32[8,4,16,192]{3,2,1,0:T(8,128)S(1)}, u32[]{:S(2)}, u32[]{:S(2)}) async-start(f32[8,4,16,192]{3,2,1,0:T(8,128)} %bitcast.540), calls=%async_computation.16 | async-start | bytes 1048576 | tf_op jit(solution)/shard_map/all_to_all | solution.py:124
  735.6 13.9 all-to-all-start.12
  749.6 17.2 %all-to-all-start.17 = ((f32[8,4,16,192]{3,2,0,1:T(8,128)}), f32[8,4,16,192]{3,2,0,1:T(8,128)S(1)}, u32[]{:S(2)}, u32[]{:S(2)}) async-start(f32[8,4,16,192]{3,2,0,1:T(8,128)} %copy.386), calls=%async_computation.17 | async-start | bytes 1048576 | tf_op jit(solution)/shard_map/all_to_all | solution.py:123
  754.7 410.8 %all-reduce.7.cloned.1.call-start = ((), (), s32[]{:S(2)}) async-start(), calls=%async_computation.33 | async-start | bytes 1572864
  766.8 25.1 %all-to-all-start.13 = ((f32[8,4,16,192]{3,2,0,1:T(8,128)}), f32[8,4,16,192]{3,2,0,1:T(8,128)S(1)}, u32[]{:S(2)}, u32[]{:S(2)}) async-start(f32[8,4,16,192]{3,2,0,1:T(8,128)} %copy.376), calls=%async_computation.13 | async-start | bytes 1048576 | tf_op jit(solution)/shard_map/all_to_all | solution.py:123
  770.3 496.4 %reduce-scatter.8.cloned.1.call-start = ((), (), s32[]{:S(2)}) async-start(), calls=%async_computation.29 | async-start | bytes 491520 | tf_op jit(solution)/shard_map/reduce_scatter | solution.py:387
  930.5 336.1 %reduce-scatter.14.cloned.1.call-start = ((), (), s32[]{:S(2)}) async-start(), calls=%async_computation.32 | async-start | bytes 983040 | tf_op jit(solution)/shard_map/reduce_scatter | solution.py:390
  939.7 327.0 %reduce-scatter.6.cloned.1.call-start = ((), (), s32[]{:S(2)}) async-start(), calls=%async_computation.28 | async-start | bytes 5242880 | tf_op jit(solution)/shard_map/reduce_scatter | solution.py:386
  951.0 315.7 %reduce-scatter.12.cloned.1.call-start = ((), (), s32[]{:S(2)}) async-start(), calls=%async_computation.31 | async-start | bytes 5242880 | tf_op jit(solution)/shard_map/reduce_scatter | solution.py:389
  955.7 311.0 %reduce-scatter.10.cloned.1.call-start = ((), (), s32[]{:S(2)}) async-start(), calls=%async_computation.30 | async-start | bytes 5242880 | tf_op jit(solution)/shard_map/reduce_scatter | solution.py:388
  1087.6 63.0 %all-to-all-start.14 = ((f32[8,4,16,512]{3,2,1,0:T(8,128)}), f32[8,4,16,512]{3,2,1,0:T(8,128)}, u32[]{:S(2)}, u32[]{:S(2)}) async-start(f32[8,4,16,512]{3,2,1,0:T(8,128)} %bitcast.539), calls=%async_computation.14 | async-start | bytes 2097152 | tf_op jit(solution)/shard_map/all_to_all | solution.py:100
  1150.6 22.4 %all-to-all-start.18 = ((f32[8,4,16,512]{3,2,1,0:T(8,128)}), f32[8,4,16,512]{3,2,1,0:T(8,128)}, u32[]{:S(2)}, u32[]{:S(2)}) async-start(f32[8,4,16,512]{3,2,1,0:T(8,128)} %bitcast.538), calls=%async_computation.18 | async-start | bytes 2097152 | tf_op jit(solution)/shard_map/all_to_all | solution.py:100
  1173.0 57.5 %all-to-all-start.15 = ((f32[8,4,16,512]{3,2,0,1:T(8,128)}), f32[8,4,16,512]{3,2,0,1:T(8,128)}, u32[]{:S(2)}, u32[]{:S(2)}) async-start(f32[8,4,16,512]{3,2,0,1:T(8,128)} %copy.379), calls=%async_computation.15 | async-start | bytes 2097152 | tf_op jit(solution)/shard_map/all_to_all | solution.py:99
  1230.5 30.6 %all-to-all-start.19 = ((f32[8,4,16,512]{3,2,0,1:T(8,128)}), f32[8,4,16,512]{3,2,0,1:T(8,128)}, u32[]{:S(2)}, u32[]{:S(2)}) async-start(f32[8,4,16,512]{3,2,0,1:T(8,128)} %copy.389), calls=%async_computation.19 | async-start | bytes 2097152 | tf_op jit(solution)/shard_map/all_to_all | solution.py:99
  1234.9 106.9 %all-reduce.9.cloned.1.call-start = ((), (), s32[]{:S(2)}) async-start(), calls=%async_computation.34 | async-start | bytes 7176192 | tf_op jit(solution)/shard_map/psum | solution.py:384
  1266.8 108.9 %copy-start.92 = (f32[3,48,192]{2,1,0:T(8,128)S(1)}, f32[3,48,192]{2,1,0:T(8,128)}, u32[]{:S(2)}) copy-start(f32[3,48,192]{2,1,0:T(8,128)} %param.42) | copy-start | bytes 331780
  1267.7 112.0 %copy-start.43 = (f32[512,512]{1,0:T(8,128)S(1)}, f32[512,512]{1,0:T(8,128)}, u32[]{:S(2)}) copy-start(f32[512,512]{1,0:T(8,128)} %param.40) | copy-start | bytes 3145732
  (221 other events, 2494.5 us)
Sparse Core Ops, SparseCore 0:
  10.2 49.6 all-gather.3
  62.0 47.8 all-gather.5
  112.0 56.8 all-gather.7
  760.0 52.4 all-reduce.6
  930.6 19.7 reduce-scatter.7
  953.3 21.5 reduce-scatter.13
  977.2 76.0 reduce-scatter.5
  1055.6 77.2 reduce-scatter.11
  1135.3 93.7 reduce-scatter.9
  1266.9 74.9 all-reduce.8
where the time goes:
time: 1410 us; the launch traced here: 1400 us
  local copies, waits for them, and re-layouts  391 us (28%)
  matrix products  373 us (26%)
  other arithmetic  277 us (20%)
  waiting for transfers between devices  125 us (9%)
  blocking collectives  117 us (8%)
  starting transfers between devices  86.8 us (6%)
  between operations  26.6 us (2%)
    dot_general x14, matrix products, mix_back(): jnp.einsum('nkh,dh->nkd', upstream, weight, preferred_element_type=jnp.fl...  140 us
    dot_general x14, matrix products, mix(): jnp.einsum('nkd,dh->nkh', left, weight, preferred_element_type=jnp.float32)  114 us
    scatter-add x2, other arithmetic, return_grads(): table_grad.at[slot_index.reshape(-1)].add(neigh_grad.reshape(-1, width))  94.2 us
    gather x6, local copies, waits for them, and re-layouts, run_batch(): first_neigh = fetch_rows(first_low, row_index)[slot_index]  92.3 us
    gather x6, local copies, waits for them, and re-layouts, run_batch(): tag_neigh = tag_table[slot_index]  90.8 us
    scatter-add x2, other arithmetic, return_sums(): table_grad.at[slot_index.reshape(-1)].add(neigh_grad.reshape(-1, width))  85.5 us
    dot_general x14, matrix products, weight_grad(): jnp.einsum('nkd,nkh->dh', left, upstream, preferred_element_type=jnp.floa...  76.2 us
    gather x6, local copies, waits for them, and re-layouts, run_batch(): neigh_term = fetch_projected(projected_local, row_index)[slot_index]  73.6 us
  transfers between devices with their start and end apart: 30, of which 12 were waited for; matrix products, arithmetic and copies ran while one was open for 63% of the time, Pallas kernels for 0%

commit v1 on v0

v1 whole, which is shorter than its diff:
```python
import functools

import jax
import jax.numpy as jnp
from jax import lax
from jax.experimental import pallas as pl
from jax.experimental.pallas import tpu as pltpu
from jax.sharding import PartitionSpec as P

D = 512
E = 192
F = 2048
STEP = 5

norm_eps = 1e-05
learn_rate = 0.03
vector_rate = 0.25
beta_first = 0.5
beta_second = 0.5
adam_eps = 1e-08
decay_rate = 0.01
clip_norm = 1.0

C0 = 0.7978845608028654
C1 = C0 * 0.044715
bf16 = jnp.bfloat16
f32 = jnp.float32
VMEM_LIMIT = 58 * 1024 * 1024


def gelu_pair(z):
    q = z * z
    t = jnp.tanh(z * (q * C1 + C0))
    s = 0.5 * t + 0.5
    p = z * s
    d = s + (p - p * s) * (q * (6.0 * C1) + 2.0 * C0)
    return p, d


def dot(a, b):
    return jnp.dot(a, b, preferred_element_type=f32)


def dot_t(a, b):
    return lax.dot_general(a, b, (((1,), (1,)), ((), ())), preferred_element_type=f32)


def tdot(a, b):
    return lax.dot_general(a, b, (((0,), (0,)), ((), ())), preferred_element_type=f32)


def turned(v):
    n = v.shape[1]
    eye = lax.broadcasted_iota(jnp.int32, (n, n), 0) == lax.broadcasted_iota(jnp.int32, (n, n), 1)
    return dot_t(jnp.where(eye, 1.0, 0.0).astype(bf16), v)


def split2(v):
    hi = v.astype(bf16)
    lo = (v - hi.astype(f32)).astype(bf16)
    return hi, lo


def normed(v):
    centred = v - jnp.mean(v, axis=-1, keepdims=True)
    spread = jnp.mean(centred * centred, axis=-1, keepdims=True)
    rs = lax.rsqrt(spread + norm_eps)
    return centred * rs, rs


def norm_back(xhat, rs, gain, grad):
    gn = grad * gain
    gx = rs * (
        gn
        - jnp.mean(gn, axis=-1, keepdims=True)
        - xhat * jnp.mean(gn * xhat, axis=-1, keepdims=True)
    )
    return gx, jnp.sum(grad * xhat, axis=0, keepdims=True), jnp.sum(grad, axis=0, keepdims=True)


def whole(*dims):
    zero = (0,) * len(dims)
    return pl.BlockSpec(dims, lambda i: zero)


def picked(m, *dims):
    index = (m,) + (0,) * len(dims)
    return pl.BlockSpec((1,) + dims, lambda i: index)


def one_hots(slot, m, k0, count, S):
    n = slot.shape[2]
    iota = lax.broadcasted_iota(jnp.int32, (S, n), 0)
    return jnp.concatenate(
        [
            jnp.where(iota == slot[k0 + j, m : m + 1, :], 1.0, 0.0).astype(bf16)
            for j in range(count)
        ],
        axis=1,
    )


def wide(ref3, k0, count):
    return jnp.concatenate([ref3[k0 + j] for j in range(count)], axis=1)


def msg_fwd_body(
    m, KB, sub, S, slot, own, ef, tab, u1, wnbr, wself, wedge, w2, rows,
    p1o, d1o, d2o, pso, cnto, vso, tt_s, zs_s, zc_s, we_s, w2_s, c2_s,
):
    step = pl.program_id(0)
    N = ef.shape[3]

    @pl.when(step == 0)
    def _():
        tt_s[0:D, :] = dot(tab[0, :, 0:D], wnbr[0]).T.astype(bf16)
        tt_s[D:, :] = tab[0, :, D : D + 128].astype(f32).T[0:16, :].astype(bf16)
        zs = dot(u1[0], wself[0]) + rows[6:7, :]
        zs_s[...] = zs.T
        zc_s[...] = (zs + rows[7:8, :]).T
        we_s[...] = wedge[...].astype(f32).T.astype(bf16)
        w2_s[...] = w2[0].astype(f32).T.astype(bf16)
        c2_s[...] = jnp.broadcast_to(rows[8:9, :], (N, D)).T
        pso[...] = jnp.zeros_like(pso)
        cnto[...] = jnp.zeros_like(cnto)

    own_row = own[m : m + 1, :]
    FC = 128
    for s in range(KB // sub):
        k0 = s * sub
        oht = one_hots(slot, m, k0, sub, S)
        z1 = dot(tt_s[...], oht)
        ze = dot(we_s[...], jnp.concatenate([ef[0, k0 + j] for j in range(sub)], axis=1))
        vals = []
        parts = []
        for j in range(sub):
            k = k0 + j
            lo, hi = j * N, (j + 1) * N
            tag = z1[D : D + 1, lo:hi]
            v = jnp.where((tag > 0.0) & (own_row > 0.0), 1.0, 0.0)
            same = tag == own_row
            vals.append(v)
            vso[k, 0:1, :] = v
            vso[k, 1:2, :] = jnp.where(same, 1.0, 0.0)
            cnto[0:1, :] += v
            for c in range(0, D, FC):
                base = jnp.where(same, zc_s[c : c + FC, :], zs_s[c : c + FC, :])
                p, d = gelu_pair(z1[c : c + FC, lo:hi] + ze[c : c + FC, lo:hi] + base)
                p1o[k, c : c + FC, :] = p.astype(bf16)
                d1o[k, c : c + FC, :] = d.astype(bf16)
        z2 = dot(w2_s[...], wide(p1o, k0, sub))
        for j in range(sub):
            k = k0 + j
            lo, hi = j * N, (j + 1) * N
            for c in range(0, D, FC):
                p, d = gelu_pair(z2[c : c + FC, lo:hi] + c2_s[c : c + FC, :])
                d2o[k, c : c + FC, :] = (d * vals[j]).astype(bf16)
                pso[c : c + FC, :] += p * vals[j]


def msg_fwd(m, slot, own, ef, tab, u1, square, wedge, rows, KB=12, sub=6):
    K, N = ef.shape[1], ef.shape[3]
    S = tab.shape[1]
    return pl.pallas_call(
        functools.partial(msg_fwd_body, m, KB, sub, S),
        grid=(K // KB,),
        in_specs=[
            pl.BlockSpec((KB, 2, N), lambda i: (i, 0, 0)),
            whole(2, N),
            pl.BlockSpec((1, KB, E, N), lambda i: (m, i, 0, 0)),
            picked(0, S, D + 128),
            picked(m, N, D),
            picked(1, D, D),
            picked(0, D, D),
            whole(E, D),
            picked(2, D, D),
            whole(16, D),
        ],
        out_specs=[
            pl.BlockSpec((KB, D, N), lambda i: (i, 0, 0)),
            pl.BlockSpec((KB, D, N), lambda i: (i, 0, 0)),
            pl.BlockSpec((KB, D, N), lambda i: (i, 0, 0)),
            whole(D, N),
            whole(8, N),
            pl.BlockSpec((KB, 2, N), lambda i: (i, 0, 0)),
        ],
        out_shape=[
            jax.ShapeDtypeStruct((K, D, N), bf16),
            jax.ShapeDtypeStruct((K, D, N), bf16),
            jax.ShapeDtypeStruct((K, D, N), bf16),
            jax.ShapeDtypeStruct((D, N), f32),
            jax.ShapeDtypeStruct((8, N), f32),
            jax.ShapeDtypeStruct((K, 2, N), f32),
        ],
        scratch_shapes=[
            pltpu.VMEM((D + 16, S), bf16),
            pltpu.VMEM((D, N), f32),
            pltpu.VMEM((D, N), f32),
            pltpu.VMEM((D, E), bf16),
            pltpu.VMEM((D, D), bf16),
            pltpu.VMEM((D, N), f32),
        ],
        compiler_params=pltpu.CompilerParams(vmem_limit_bytes=VMEM_LIMIT),
        name="msg_fwd",
        cost_estimate=pl.CostEstimate(
            flops=2 * N * K * 10 * 65536, bytes_accessed=N * K * D * 6, transcendentals=0
        ),
    )(slot, own, ef, tab, u1, square, square, wedge, square, rows)


def edge_body(m, KB, sub, S, first, slot, vs, ef, up, tab, ys, vsq, rows, *refs):
    refs, scr = refs[:-10], refs[-10:]
    (eo, gy1o, gyso, so, dvo, dbo) = refs[-6:]
    (nt_s, vt_s, b_s, oh_s, r1_s, r2_s, g3_s, g2_s, ef_s, acc_s) = scr
    step = pl.program_id(0)
    N = ef.shape[3]

    @pl.when(step == 0)
    def _():
        nt_s[...] = turned(tab[...]).astype(bf16)
        for i in range(3):
            vt_s[i] = turned(vsq[i]).astype(bf16)
        for i in range(2):
            b_s[i] = jnp.broadcast_to(rows[i + 1 : i + 2, :], (N, E)).T
        gyso[...] = jnp.zeros_like(gyso)
        acc_s[...] = jnp.zeros_like(acc_s)
        if first:
            dvo[...] = jnp.zeros_like(dvo)
            dbo[...] = jnp.zeros_like(dbo)
        else:
            dvo[...] = refs[0][...]
            dbo[...] = refs[1][...]

    w = sub * N
    for s in range(KB // sub):
        k0 = s * sub
        lo = s * w
        oht = one_hots(slot, m, k0, sub, S)
        oh_s[:, lo : lo + w] = oht
        eft = jnp.concatenate([ef[0, k0 + j] for j in range(sub)], axis=1)
        ef_s[:, lo : lo + w] = eft
        base = jnp.concatenate([ys[...]] * sub, axis=1)
        r1, e1 = gelu_pair(dot(nt_s[...], oht) + dot(vt_s[0], eft) + base)
        r1 = r1.astype(bf16)
        r1_s[:, lo : lo + w] = r1
        r2, e2 = gelu_pair(dot(vt_s[1], r1) + jnp.concatenate([b_s[0]] * sub, axis=1))
        r2 = r2.astype(bf16)
        r2_s[:, lo : lo + w] = r2
        y3 = dot(vt_s[2], r2)
        for j in range(sub):
            v = vs[k0 + j, 0:1, :]
            eo[0, k0 + j] = ef[0, k0 + j].astype(f32) + v * (y3[:, j * N : (j + 1) * N] + b_s[1])
            g3f = v * up[0, k0 + j].astype(f32)
            acc_s[1] += g3f
            g3_s[:, lo + j * N : lo + (j + 1) * N] = g3f.astype(bf16)
        g2 = (e2 * dot(vsq[2], g3_s[:, lo : lo + w])).astype(bf16)
        g2_s[:, lo : lo + w] = g2
        g1 = (e1 * dot(vsq[1], g2)).astype(bf16)
        for j in range(sub):
            acc_s[0] += g2[:, j * N : (j + 1) * N].astype(f32)
            gyso[...] += g1[:, j * N : (j + 1) * N].astype(f32)
            gy1o[k0 + j] = g1[:, j * N : (j + 1) * N]
    g1 = wide(gy1o, 0, KB)
    part = dot_t(oh_s[...], g1)

    @pl.when(step == 0)
    def _():
        so[...] = part

    @pl.when(step > 0)
    def _():
        so[...] += part

    dvo[2] += dot_t(r2_s[...], g3_s[...])
    dvo[1] += dot_t(r1_s[...], g2_s[...])
    dvo[0] += dot_t(ef_s[...], g1)

    @pl.when(step == pl.num_programs(0) - 1)
    def _():
        dbo[1:2, :] += jnp.sum(acc_s[0].T, axis=0, keepdims=True)
        dbo[2:3, :] += jnp.sum(acc_s[1].T, axis=0, keepdims=True)


def edge_net(m, slot, vs, ef, up, tab, ys, vsq, rows, before, KB=12, sub=6):
    K, N = ef.shape[1], ef.shape[3]
    S = tab.shape[0]
    first = before is None
    extra = [] if first else list(before)
    args = [slot, vs, ef, up, tab, ys, vsq, rows]
    specs = [
        pl.BlockSpec((KB, 2, N), lambda i: (i, 0, 0)),
        pl.BlockSpec((KB, 2, N), lambda i: (i, 0, 0)),
        pl.BlockSpec((1, KB, E, N), lambda i: (m, i, 0, 0)),
        pl.BlockSpec((1, KB, E, N), lambda i: (m, i, 0, 0)),
        whole(S, E),
        whole(E, N),
        whole(3, E, E),
        whole(8, E),
    ]
    aliases = {}
    if not first:
        specs += [whole(3, E, E), whole(8, E), pl.BlockSpec(memory_space=pl.ANY)]
        aliases = {len(args) + 2: 0}
    L = KB * N
    return pl.pallas_call(
        functools.partial(edge_body, m, KB, sub, S, first),
        grid=(K // KB,),
        in_specs=specs,
        out_specs=[
            pl.BlockSpec((1, KB, E, N), lambda i: (m, i, 0, 0)),
            pl.BlockSpec((KB, E, N), lambda i: (i, 0, 0)),
            whole(E, N),
            whole(S, E),
            whole(3, E, E),
            whole(8, E),
        ],
        out_shape=[
            jax.ShapeDtypeStruct(ef.shape, f32),
            jax.ShapeDtypeStruct((K, E, N), bf16),
            jax.ShapeDtypeStruct((E, N), f32),
            jax.ShapeDtypeStruct((S, E), f32),
            jax.ShapeDtypeStruct((3, E, E), f32),
            jax.ShapeDtypeStruct((8, E), f32),
        ],
        scratch_shapes=[
            pltpu.VMEM((E, S), bf16),
            pltpu.VMEM((3, E, E), bf16),
            pltpu.VMEM((2, E, N), f32),
            pltpu.VMEM((S, L), bf16),
            pltpu.VMEM((E, L), bf16),
            pltpu.VMEM((E, L), bf16),
            pltpu.VMEM((E, L), bf16),
            pltpu.VMEM((E, L), bf16),
            pltpu.VMEM((E, L), bf16),
            pltpu.VMEM((2, E, N), f32),
        ],
        input_output_aliases=aliases,
        compiler_params=pltpu.CompilerParams(vmem_limit_bytes=VMEM_LIMIT),
        name="edge_net",
        cost_estimate=pl.CostEstimate(
            flops=2 * N * K * 12 * 65536, bytes_accessed=N * K * E * 12, transcendentals=0
        ),
    )(*args, *extra)


def msg_bwd_body(
    m, KB, sub, S, first, slot, vs, ef, up, p1, d1, d2, gy1, h, w2, wedge, vsq, *refs
):
    refs, scr = refs[:-4], refs[-4:]
    (ego, gzso, so, dw2o, dweo, dbo) = refs[-6:]
    (oh_s, g2_s, g1_s, acc_s) = scr
    step = pl.program_id(0)
    N = ef.shape[3]

    @pl.when(step == 0)
    def _():
        gzso[...] = jnp.zeros_like(gzso)
        acc_s[...] = jnp.zeros_like(acc_s)
        if first:
            dw2o[...] = jnp.zeros_like(dw2o)
            dweo[...] = jnp.zeros_like(dweo)
            dbo[...] = jnp.zeros_like(dbo)
        else:
            dw2o[...] = refs[0][...]
            dweo[...] = refs[1][...]
            dbo[...] = refs[2][...]

    w = sub * N
    FC = 128
    for s in range(KB // sub):
        k0 = s * sub
        lo = s * w
        oh_s[:, lo : lo + w] = one_hots(slot, m, k0, sub, S)
        for j in range(sub):
            for c in range(0, D, FC):
                g = d2[k0 + j, c : c + FC, :].astype(f32) * h[c : c + FC, :]
                acc_s[0, c : c + FC, :] += g
                g2_s[c : c + FC, lo + j * N : lo + (j + 1) * N] = g.astype(bf16)
        back = dot(w2[0], g2_s[:, lo : lo + w])
        for j in range(sub):
            same = vs[k0 + j, 1:2, :]
            for c in range(0, D, FC):
                g = d1[k0 + j, c : c + FC, :].astype(f32) * back[c : c + FC, j * N : (j + 1) * N]
                gzso[c : c + FC, :] += g
                acc_s[1, c : c + FC, :] += g * same
                g1_s[c : c + FC, lo + j * N : lo + (j + 1) * N] = g.astype(bf16)
        back = dot(wedge[...], g1_s[:, lo : lo + w]) + dot(vsq[0], wide(gy1, k0, sub))
        for j in range(sub):
            ego[0, k0 + j] = up[0, k0 + j].astype(f32) + back[:, j * N : (j + 1) * N]
    g1 = g1_s[...]
    part = dot_t(oh_s[...], g1)

    @pl.when(step == 0)
    def _():
        so[...] = part

    @pl.when(step > 0)
    def _():
        so[...] += part

    dw2o[...] += dot_t(wide(p1, 0, KB), g2_s[...])
    dweo[...] += dot_t(jnp.concatenate([ef[0, j] for j in range(KB)], axis=1), g1)

    @pl.when(step == pl.num_programs(0) - 1)
    def _():
        dbo[0:1, :] += jnp.sum(acc_s[0].T, axis=0, keepdims=True)
        dbo[1:2, :] += jnp.sum(acc_s[1].T, axis=0, keepdims=True)


def msg_bwd(m, S, slot, vs, ef, up, p1, d1, d2, gy1, h, square, wedge, vsq, before, KB=12, sub=6):
    K, N = ef.shape[1], ef.shape[3]
    first = before is None
    extra = [] if first else list(before)
    args = [slot, vs, ef, up, p1, d1, d2, gy1, h, square, wedge, vsq]
    specs = [
        pl.BlockSpec((KB, 2, N), lambda i: (i, 0, 0)),
        pl.BlockSpec((KB, 2, N), lambda i: (i, 0, 0)),
        pl.BlockSpec((1, KB, E, N), lambda i: (m, i, 0, 0)),
        pl.BlockSpec((1, KB, E, N), lambda i: (m, i, 0, 0)),
        pl.BlockSpec((KB, D, N), lambda i: (i, 0, 0)),
        pl.BlockSpec((KB, D, N), lambda i: (i, 0, 0)),
        pl.BlockSpec((KB, D, N), lambda i: (i, 0, 0)),
        pl.BlockSpec((KB, E, N), lambda i: (i, 0, 0)),
        whole(D, N),
        picked(2, D, D),
        whole(E, D),
        picked(0, E, E),
    ]
    aliases = {}
    if not first:
        specs += [whole(D, D), whole(E, D), whole(8, D), pl.BlockSpec(memory_space=pl.ANY)]
        aliases = {len(args) + 3: 0}
    L = KB * N
    return pl.pallas_call(
        functools.partial(msg_bwd_body, m, KB, sub, S, first),
        grid=(K // KB,),
        in_specs=specs,
        out_specs=[
            pl.BlockSpec((1, KB, E, N), lambda i: (m, i, 0, 0)),
            whole(D, N),
            whole(S, D),
            whole(D, D),
            whole(E, D),
            whole(8, D),
        ],
        out_shape=[
            jax.ShapeDtypeStruct(ef.shape, f32),
            jax.ShapeDtypeStruct((D, N), f32),
            jax.ShapeDtypeStruct((S, D), f32),
            jax.ShapeDtypeStruct((D, D), f32),
            jax.ShapeDtypeStruct((E, D), f32),
            jax.ShapeDtypeStruct((8, D), f32),
        ],
        scratch_shapes=[
            pltpu.VMEM((S, L), bf16),
            pltpu.VMEM((D, L), bf16),
            pltpu.VMEM((D, L), bf16),
            pltpu.VMEM((2, D, N), f32),
        ],
        input_output_aliases=aliases,
        compiler_params=pltpu.CompilerParams(vmem_limit_bytes=VMEM_LIMIT),
        name="msg_bwd",
        cost_estimate=pl.CostEstimate(
            flops=2 * N * K * 16 * 65536, bytes_accessed=N * K * D * 10, transcendentals=0
        ),
    )(*args, *extra)


def picked_rows(srow, N, S):
    hit = lax.broadcasted_iota(jnp.int32, (N, S), 0) == srow
    return jnp.where(hit, 1.0, 0.0).astype(bf16)


def split_dot(v, w):
    hi, lo = split2(v)
    return dot(hi, w) + dot(lo, w)


def split_dot_t(v, w):
    hi, lo = split2(v)
    return dot_t(hi, w) + dot_t(lo, w)


def split_tdot(w, v):
    hi, lo = split2(v)
    return tdot(w, hi) + tdot(w, lo)


def scaled(v, row, shift):
    xhat, rs = normed(v)
    return xhat * row + shift, xhat, rs


def node_in_body(x, rows, srow, tags, u1o, sendo):
    _, N, _ = x.shape
    S = srow.shape[2]
    for m in range(x.shape[0]):
        u1 = scaled(x[m].astype(f32), rows[0:1, :], rows[1:2, :])[0].astype(bf16)
        u1o[m] = u1
        oh = picked_rows(srow[m], N, S)
        sendo[m, :, 0:D] = tdot(oh, u1).astype(bf16)
        sendo[m, :, D:] = tdot(oh, tags[m]).astype(bf16)


def node_in(x, rows, srow, tags):
    MB, N, _ = x.shape
    S = srow.shape[2]
    return pl.pallas_call(
        node_in_body,
        out_shape=[
            jax.ShapeDtypeStruct((MB, N, D), bf16),
            jax.ShapeDtypeStruct((MB, S, D + 128), bf16),
        ],
        compiler_params=pltpu.CompilerParams(vmem_limit_bytes=VMEM_LIMIT),
        name="node_in",
    )(x, rows, srow, tags)


def node_mid_body(
    ps, cnt, x, w3, wup, wdown, vin, rows, c4, rowe, srow,
    outo, x1o, a2o, qo, qdo, wo, yso, sendo,
):
    N = x.shape[1]
    S = srow.shape[2]
    cnt_col = cnt[...].T[:, 0:1]
    total = split_dot(ps[...].T, w3[0]) + cnt_col * rows[9:10, :]
    x1 = x[0].astype(f32) + total / jnp.maximum(cnt_col, 1.0)
    x1o[...] = x1
    a2 = scaled(x1, rows[2:3, :], rows[3:4, :])[0].astype(bf16)
    a2o[...] = a2
    out = x1 + rows[10:11, :]
    for c in range(0, F, 512):
        q, qd = gelu_pair(dot(a2, wup[:, c : c + 512]) + c4[0:1, c : c + 512])
        q = q.astype(bf16)
        qo[:, c : c + 512] = q
        qdo[:, c : c + 512] = qd
        out = out + dot(q, wdown[c : c + 512, :])
    outo[...] = out
    w = scaled(out, rows[4:5, :], rows[5:6, :])[0].astype(bf16)
    wo[...] = w
    yso[...] = (dot(w, vin[0]) + rowe[0:1, :]).T
    near = dot(w, vin[1]).astype(bf16)
    sendo[...] = tdot(picked_rows(srow[0], N, S), near).astype(bf16)


def node_mid(m, ps, cnt, x, square, wup, wdown, vin, rows, c4, rowe, srow):
    N = x.shape[1]
    S = srow.shape[2]
    shapes = [
        jax.ShapeDtypeStruct((N, D), f32),
        jax.ShapeDtypeStruct((N, D), f32),
        jax.ShapeDtypeStruct((N, D), bf16),
        jax.ShapeDtypeStruct((N, F), bf16),
        jax.ShapeDtypeStruct((N, F), f32),
        jax.ShapeDtypeStruct((N, D), bf16),
        jax.ShapeDtypeStruct((E, N), f32),
        jax.ShapeDtypeStruct((S, E), bf16),
    ]
    return pl.pallas_call(
        node_mid_body,
        grid=(1,),
        in_specs=[
            whole(D, N), whole(8, N), picked(m, N, D), picked(3, D, D), whole(D, F), whole(F, D),
            whole(2, D, E), whole(16, D), whole(8, F), whole(8, E), picked(m, 1, S),
        ],
        out_specs=[whole(*s.shape) for s in shapes],
        out_shape=shapes,
        compiler_params=pltpu.CompilerParams(vmem_limit_bytes=VMEM_LIMIT),
        name="node_mid",
        cost_estimate=pl.CostEstimate(flops=2 * N * D * F * 2, bytes_accessed=8 << 20, transcendentals=0),
    )(ps, cnt, x, square, wup, wdown, vin, rows, c4, rowe, srow)


def node_back_body(
    inc, srow, gys_t, vin, w, out, x1, a2, q, qd, up, wup, wdown, w3, rows, ps, cnt, *refs
):
    first = len(refs) == 8
    old, (ho, gx1o, dw3o, dupo, ddowno, dvino, vro, vwo) = refs[:-8], refs[-8:]
    N = w.shape[0]
    S = srow.shape[2]

    def put(i, ref, sl, v):
        ref[sl] = v if first else old[i][sl] + v

    picks = picked_rows(srow[0], N, S)
    near = dot(picks, inc[...])
    gys = gys_t[...].T
    wv = w[...]
    put(3, dvino, 0, split_tdot(wv, gys))
    put(3, dvino, 1, split_tdot(wv, near))
    gw = split_dot_t(gys, vin[0]) + split_dot_t(near, vin[1])
    xhat, rs = normed(out[...])
    gx, dg3, db3 = norm_back(xhat, rs, rows[4:5, :], gw)
    gx2 = up[0].astype(f32) + gx
    gy = gx2.astype(bf16)
    dc5 = jnp.sum(gy.astype(f32), axis=0, keepdims=True)
    ga2 = jnp.zeros((N, D), f32)
    for c in range(0, F, 512):
        sl = slice(c, c + 512)
        put(2, ddowno, (sl, slice(None)), tdot(q[:, sl], gy))
        gf = (qd[:, sl] * dot_t(gy, wdown[sl, :])).astype(bf16)
        put(1, dupo, (slice(None), sl), tdot(a2[...], gf))
        put(5, vwo, (slice(0, 1), sl), jnp.sum(gf.astype(f32), axis=0, keepdims=True))
        ga2 = ga2 + dot_t(gf, wup[:, sl])
    xhat, rs = normed(x1[...])
    gx, dg2, db2 = norm_back(xhat, rs, rows[2:3, :], ga2)
    gx1 = gx2 + gx
    gx1o[...] = gx1
    cnt_col = cnt[...].T[:, 0:1]
    g = (gx1 / jnp.maximum(cnt_col, 1.0)).astype(bf16)
    ho[...] = dot_t(g, w3[0]).T
    put(0, dw3o, slice(None), split_dot(ps[...], g))
    dc3 = jnp.sum(g.astype(f32) * cnt_col, axis=0, keepdims=True)
    dd1 = jnp.sum(gys, axis=0, keepdims=True)
    zero = jnp.zeros((1, D - E), f32)
    for i, v in enumerate((dg2, db2, dg3, db3, dc3, dc5, jnp.concatenate([dd1, zero], axis=1))):
        put(4, vro, (slice(i, i + 1), slice(None)), v)
    vro[7:8, :] = jnp.zeros((1, D), f32)
    vwo[1:8, :] = jnp.zeros((7, F), f32)


def node_back(m, inc, srow, gys_t, vin, kept, up, wup, wdown, square, rows, ps, cnt, before):
    out, x1, a2, q, qd, w = kept
    N = w.shape[0]
    S = srow.shape[2]
    shapes = [
        jax.ShapeDtypeStruct((D, N), f32),
        jax.ShapeDtypeStruct((N, D), f32),
        jax.ShapeDtypeStruct((D, D), f32),
        jax.ShapeDtypeStruct((D, F), f32),
        jax.ShapeDtypeStruct((F, D), f32),
        jax.ShapeDtypeStruct((2, D, E), f32),
        jax.ShapeDtypeStruct((8, D), f32),
        jax.ShapeDtypeStruct((8, F), f32),
    ]
    extra = [] if before is None else list(before)
    args = [inc, srow, gys_t, vin, w, out, x1, a2, q, qd, up, wup, wdown, square, rows, ps, cnt]
    aliases = {len(args) + i: 2 + i for i in range(len(extra))}
    return pl.pallas_call(
        node_back_body,
        grid=(1,),
        in_specs=[
            whole(S, E), picked(m, 1, S), whole(E, N), whole(2, D, E), whole(N, D), whole(N, D),
            whole(N, D), whole(N, D), whole(N, F), whole(N, F), picked(m, N, D), whole(D, F),
            whole(F, D), picked(3, D, D), whole(16, D), whole(D, N), whole(8, N),
        ]
        + [whole(*v.shape) for v in extra],
        out_specs=[whole(*s.shape) for s in shapes],
        out_shape=shapes,
        input_output_aliases=aliases,
        compiler_params=pltpu.CompilerParams(vmem_limit_bytes=VMEM_LIMIT),
        name="node_back",
        cost_estimate=pl.CostEstimate(flops=2 * N * D * F * 4, bytes_accessed=20 << 20, transcendentals=0),
    )(*args, *extra)


def node_end_body(inc, srow, gzs_t, u1, x, gx1, wself, wnbr, rows, *refs):
    first = len(refs) == 3
    old, (go, dwo, vro) = refs[:-3], refs[-3:]
    N = u1.shape[1]
    S = srow.shape[2]

    def put(i, ref, sl, v):
        ref[sl] = v if first else old[i][sl] + v

    near = dot(picked_rows(srow[0], N, S), inc[...])
    gzs = gzs_t[...].T
    put(0, dwo, 0, split_tdot(u1[0], gzs))
    put(0, dwo, 1, split_tdot(u1[0], near))
    gu1 = split_dot_t(gzs, wself[0]) + split_dot_t(near, wnbr[0])
    xhat, rs = normed(x[0].astype(f32))
    gx, dg1, db1 = norm_back(xhat, rs, rows[0:1, :], gu1)
    go[...] = gx1[...] + gx
    for i, v in enumerate((dg1, db1, jnp.sum(gzs, axis=0, keepdims=True))):
        put(1, vro, (slice(i, i + 1), slice(None)), v)
    vro[3:8, :] = jnp.zeros((5, D), f32)


def node_end(m, inc, srow, gzs_t, u1, x, gx1, square, rows, before):
    N = x.shape[1]
    S = srow.shape[2]
    shapes = [
        jax.ShapeDtypeStruct((N, D), f32),
        jax.ShapeDtypeStruct((2, D, D), f32),
        jax.ShapeDtypeStruct((8, D), f32),
    ]
    extra = [] if before is None else list(before)
    args = [inc, srow, gzs_t, u1, x, gx1, square, square, rows]
    return pl.pallas_call(
        node_end_body,
        grid=(1,),
        in_specs=[
            whole(S, D), picked(m, 1, S), whole(D, N), picked(m, N, D), picked(m, N, D),
            whole(N, D), picked(0, D, D), picked(1, D, D), whole(16, D),
        ]
        + [whole(*v.shape) for v in extra],
        out_specs=[whole(*s.shape) for s in shapes],
        out_shape=shapes,
        input_output_aliases={len(args) + i: 1 + i for i in range(len(extra))},
        compiler_params=pltpu.CompilerParams(vmem_limit_bytes=VMEM_LIMIT),
        name="node_end",
    )(*args, *extra)


def exchange(rows):
    return lax.all_to_all(rows, ("res", "tp"), split_axis=0, concat_axis=0, tiled=True)


def shards(
    node_feats, edge_feats, slot_index, send_rows, res_mask, chain_ids, node_upstream, edge_upstream,
    *state,
):
    masters, firsts, seconds = state[0:7], state[7:14], state[14:21]
    MB, N, K, _ = edge_feats.shape
    devs = send_rows.shape[2]
    S = devs * send_rows.shape[3]
    low = [v.astype(bf16) for v in masters]
    vec = lax.all_gather(low[6], "tp", axis=0, tiled=True)
    square = lax.all_gather(low[0], "tp", axis=1, tiled=True)
    wedge = lax.all_gather(low[1], "tp", axis=0, tiled=True)
    wup = lax.all_gather(low[2], "tp", axis=0, tiled=True)
    wdown = lax.all_gather(low[3], "tp", axis=0, tiled=True)
    vin = lax.all_gather(low[4], "tp", axis=1, tiled=True)
    vsq = lax.all_gather(low[5], "tp", axis=1, tiled=True)
    vec = vec.astype(f32)
    rows = jnp.pad(vec[: 11 * D].reshape(11, D), ((0, 5), (0, 0)))
    c4 = jnp.pad(vec[11 * D : 11 * D + F].reshape(1, F), ((0, 7), (0, 0)))
    rowe = jnp.pad(vec[11 * D + F :].reshape(3, E), ((0, 5), (0, 0)))

    ef = jnp.transpose(edge_feats, (0, 2, 3, 1))
    eup = jnp.transpose(edge_upstream, (0, 2, 3, 1))
    slot = jnp.transpose(slot_index, (2, 0, 1))
    srow = send_rows.reshape(MB, 1, S)
    own = (res_mask * (chain_ids + 1)).astype(f32)
    tags = jnp.broadcast_to(own.astype(bf16)[:, :, None], (MB, N, 128))

    u1, send = node_in(node_feats, rows, srow, tags)
    tabs = [exchange(send[m])[None] for m in range(MB)]

    mids, fwd, kept = [], [], []
    for m in range(MB):
        a = msg_fwd(0 if False else m, slot, own, ef, tabs[m], u1, square, wedge, rows)
        p1, d1, d2, ps, cnt, vs = a
        fwd.append(a)
        out, x1, a2, q, qd, w, ys, wsend = node_mid(
            m, ps, cnt, node_feats, square, wup, wdown, vin, rows, c4, rowe, srow
        )
        kept.append((out, x1, a2, q, qd, w))
        mids.append((ys, exchange(wsend)))
    before = None
    edges = []
    for m in range(MB):
        ys, tab = mids[m]
        eo, gy1, gys_t, sums, dv, db = edge_net(
            m, slot, fwd[m][5], ef, eup, tab, ys, vsq, rowe, before
        )
        before = (dv, db, eo)
        edges.append((gy1, gys_t, exchange(sums.astype(bf16))))
    dvsq, dbe, edge_out = before
    before = None
    backs = []
    for m in range(MB):
        gy1, gys_t, inc = edges[m]
        p1, d1, d2, ps, cnt, vs = fwd[m]
        ho, gx1, *before = node_back(
            m, inc, srow, gys_t, vin, kept[m], node_upstream, wup, wdown, square, rows, ps, cnt, before
        )
        backs.append((ho, gx1))
    dw3, dup, ddown, dvin, vr2, vw = before
    before = None
    last = []
    for m in range(MB):
        p1, d1, d2, ps, cnt, vs = fwd[m]
        ego, gzs_t, sums, dw2, dwe, dbm = msg_bwd(
            m, S, slot, vs, ef, eup, p1, d1, d2, edges[m][0], backs[m][0], square, wedge, vsq, before
        )
        before = (dw2, dwe, dbm, ego)
        last.append((gzs_t, exchange(sums.astype(bf16))))
    dw2, dwe, dbm, edge_grad = before
    before = None
    node_grads = []
    for m in range(MB):
        gzs_t, inc = last[m]
        ng, *before = node_end(m, inc, srow, gzs_t, u1, node_feats, backs[m][1], square, rows, before)
        node_grads.append(ng)
    dws, vr1 = before
    vec_grad = jnp.concatenate(
        [
            vr1[0], vr1[1], vr2[0], vr2[1], vr2[2], vr2[3], vr1[2], dbm[1], dbm[0], vr2[4], vr2[5],
            vw[0], vr2[6, :E], dbe[1], dbe[2],
        ]
    )
    locals_ = (
        jnp.stack([dws[0], dws[1], dw2, dw3]), dwe, dup, ddown, dvin, dvsq, vec_grad,
    )
    dims = (1, 0, 0, 0, 1, 1, 0)
    total = lax.psum(
        tuple(
            lax.psum_scatter(g, "tp", scatter_dimension=d, tiled=True) for g, d in zip(locals_, dims)
        ),
        "res",
    )
    square_sum = jnp.zeros((), f32)
    for part in total:
        square_sum = square_sum + jnp.sum(part * part)
    grad_norm = jnp.sqrt(lax.psum(square_sum, "tp"))
    scale = clip_norm / jnp.maximum(grad_norm, clip_norm)
    first_fix = 1.0 - beta_first**STEP
    second_fix = 1.0 - beta_second**STEP
    new_w, new_f, new_s = [], [], []
    for i in range(7):
        decay, rate = (decay_rate, learn_rate) if i < 6 else (0.0, vector_rate)
        clipped = total[i] * scale
        nf = beta_first * firsts[i] + (1.0 - beta_first) * clipped
        ns = beta_second * seconds[i] + (1.0 - beta_second) * clipped * clipped
        step = nf / first_fix / (jnp.sqrt(ns / second_fix) + adam_eps)
        new_w.append(masters[i] - rate * (step + decay * masters[i]))
        new_f.append(nf)
        new_s.append(ns)
    return (
        jnp.stack([k[0] for k in kept]),
        jnp.transpose(edge_out, (0, 3, 1, 2)),
        jnp.stack(node_grads),
        jnp.transpose(edge_grad, (0, 3, 1, 2)),
        grad_norm.reshape(1),
        *new_w,
        *new_f,
        *new_s,
    )


def solution(mesh):
    lead = ("res", "tp")
    feats = (
        P(None, lead, None),
        P(None, lead, None, None),
        P(None, lead, None),
        P(None, lead, None, None),
        P(None, lead),
        P(None, lead),
        P(None, lead, None),
        P(None, lead, None, None),
    )
    params = (
        P(None, "tp", None),
        P("tp", None),
        P("tp", None),
        P("tp", None),
        P(None, "tp", None),
        P(None, "tp", None),
        P("tp"),
    )
    node, edge = P(None, lead, None), P(None, lead, None, None)
    return jax.shard_map(
        shards,
        mesh=mesh,
        in_specs=feats + params * 3,
        out_specs=(node, edge, node, edge, P()) + params * 3,
        check_vma=False,
    )
```

time: 1410 us -> 838 us (0.59)
  local copies, waits for them, and re-layouts: 391 us -> 16.3 us
  matrix products: 373 us -> 0 us
  other arithmetic: 277 us -> 43.8 us
  Pallas kernels: 0 us -> 216 us
  waiting for transfers between devices: 125 us -> 335 us
  starting transfers between devices: 86.8 us -> 39 us
  blocking collectives: 117 us -> 156 us
    dot_general x72 -> x0, matrix products: 373 us -> none  [the longest x14 140 us: mix_back(): jnp.einsum('nkh,dh->nkd', upstream, weight, preferred_element_type=jnp.fl...]
    gather x24 -> x0, local copies, waits for them, and re-layouts: 273 us -> none  [the longest x6 92.3 us: run_batch(): first_neigh = fetch_rows(first_low, row_index)[slot_index]]
    reduce_scatter x5 -> x6, waiting for transfers between devices: 0.09 us -> 235 us  [shards(): lax.psum_scatter(g, 'tp', scatter_dimension=d, tiled=True)]
    pallas_call x0 -> x13, Pallas kernels: none -> 216 us  [the longest x2 57.2 us: msg_bwd(): pl.pallas_call(functools.partial(msg_bwd_body, m, KB, sub, S, first), gri...]
    scatter-add x8 -> x0, other arithmetic: 195 us -> none  [the longest x2 94.2 us: return_grads(): table_grad.at[slot_index.reshape(-1)].add(neigh_grad.reshape(-1, width))]
    all_to_all x20 -> x8, starting transfers between devices: 85.7 us -> 38.4 us  [exchange(): lax.all_to_all(rows, ('res', 'tp'), split_axis=0, concat_axis=0, tiled=True)]
    convert_element_type x6 -> x1, local copies, waits for them, and re-layouts: 37.2 us -> 0.11 us  [shards(): low = [v.astype(bf16) for v in masters]]
    all_gather x3, blocking collectives: 44.8 us -> 80.8 us  [the longest x1 44.7 us: shards(): wedge = lax.all_gather(low[1], 'tp', axis=0, tiled=True)]
  transfers between devices with their start and end apart: 30 -> 18, of which waited for: 12 -> 8; matrix products, arithmetic and copies ran while one was open for 63% -> 3% of each run, Pallas kernels for 0% -> 26%
where the time goes in v1:
time: 838 us; the launch traced here: 829 us
  waiting for transfers between devices  335 us (40%)
  Pallas kernels  216 us (26%)
  blocking collectives  156 us (19%)
  other arithmetic  43.8 us (5%)
  starting transfers between devices  39 us (5%)
  between operations  23 us (3%)
  local copies, waits for them, and re-layouts  16.3 us (2%)
    reduce_scatter x6, waiting for transfers between devices, shards(): lax.psum_scatter(g, 'tp', scatter_dimension=d, tiled=True)  235 us
    all_to_all x8, waiting for transfers between devices, exchange(): lax.all_to_all(rows, ('res', 'tp'), split_axis=0, concat_axis=0, tiled=True)  63.8 us
    pallas_call x2, Pallas kernels, msg_bwd(): pl.pallas_call(functools.partial(msg_bwd_body, m, KB, sub, S, first), gri...  57.2 us
    pallas_call x2, Pallas kernels, msg_fwd(): pl.pallas_call(functools.partial(msg_fwd_body, m, KB, sub, S), grid=(K //...  55.4 us
    pallas_call x2, Pallas kernels, edge_net(): pl.pallas_call(functools.partial(edge_body, m, KB, sub, S, first), grid=(...  54.1 us
    all_gather x1, blocking collectives, shards(): wedge = lax.all_gather(low[1], 'tp', axis=0, tiled=True)  44.7 us
    unnamed x2, blocking collectives  40.1 us
    all_to_all x8, starting transfers between devices, exchange(): lax.all_to_all(rows, ('res', 'tp'), split_axis=0, concat_axis=0, tiled=True)  38.4 us
  transfers between devices with their start and end apart: 18, of which 8 were waited for; matrix products, arithmetic and copies ran while one was open for 3% of the time, Pallas kernels for 26%

profile of v1, /device:TPU:0, one launch (start us, length us, event | category | flops | bytes accessed | tf_op | source)
XLA Modules:
  0.0 828.6 jit_solution(1503988383371071971)
XLA Ops:
  7.3 2.2 convert_element_type.52
  9.6 2.1 convert_element_type.54
  14.2 21.5 %all-reduce.3 = bf16[8256]{0:T(1024)(128)(2,1)S(1)} all-reduce(bf16[8256]{0:T(1024)(128)(2,1)S(1)} %dynamic-update-slice), channel_id=1, replica_groups=mesh['res'=8,'tp'=4] {'tp'}, use_global_device_ids=true, to_apply=%add.3 | all-reduce | flops 8256 | bytes 33024
  38.5 2.8 node_in.1
  41.3 2.5 fusion.15
  43.8 2.9 all-to-all-start
  48.2 24.5 %all-to-all-done = bf16[32,16,640]{2,1,0:T(8,128)(2,1)S(1)} async-done(((bf16[32,16,640]{2,1,0:T(8,128)(2,1)}), bf16[32,16,640]{2,1,0:T(8,128)(2,1)S(1)}, u32[]{:S(2)}, u32[]{:S(2)}) %all-to-all-start) | async-done | bytes 655392 | tf_op jit(solution)/shard_map/all_to_all | solution.py:706
  72.7 3.8 all-to-all-start.1
  76.5 44.7 %all_gather.23.wedge = bf16[192,512]{1,0:T(8,128)(2,1)} all-gather(bf16[48,512]{1,0:T(8,128)(2,1)S(1)} %convert_element_type.53), channel_id=1, replica_groups=mesh['res'=8,'tp'=4] {'tp'}, dimensions={0}, use_global_device_ids=true | all-gather | bytes 245760 | tf_op jit(solution)/shard_map/all_gather | solution.py:720
  121.2 17.8 %all_gather.27.vsq = bf16[3,192,192]{2,1,0:T(8,128)(2,1)} all-gather(bf16[3,48,192]{2,1,0:T(8,128)(2,1)S(1)} %convert_element_type.57), channel_id=1, replica_groups=mesh['res'=8,'tp'=4] {'tp'}, dimensions={1}, use_global_device_ids=true | all-gather | bytes 276480 | tf_op jit(solution)/shard_map/all_gather | solution.py:724
  139.0 18.4 %all_gather.26.vin = bf16[2,512,192]{2,1,0:T(8,128)(2,1)} all-gather(bf16[2,128,192]{2,1,0:T(8,128)(2,1)S(1)} %copy.108), channel_id=1, replica_groups=mesh['res'=8,'tp'=4] {'tp'}, dimensions={1}, use_global_device_ids=true | all-gather | bytes 491520 | tf_op jit(solution)/shard_map/all_gather | solution.py:723
  157.4 27.7 %msg_fwd.2 = (bf16[60,512,128]{2,1,0:T(8,128)(2,1)}, bf16[60,512,128]{2,1,0:T(8,128)(2,1)}, bf16[60,512,128]{2,1,0:T(8,128)(2,1)}, f32[512,128]{1,0:T(8,128)}, f32[8,128]{1,0:T(8,128)}, /*index=5*/f32[60,2,128]{2,1,0:T(2,128)}) custom-call(s32[60,2,128]{2,1,0:T(2,128)} %bitcast.92, f32[2,128]{1,0:T(2,128)} %get-tuple-element.310.own, ...), custom_call_target="tpu_custom_call" | custom-call | flops 10066329600 | bytes 23592960 | tf_op jit(solution)/shard_map/msg_fwd/pallas_call | solution.py:164
  185.4 6.0 node_mid.2
  191.4 4.4 all-to-all-start.3
  195.8 27.7 %msg_fwd.3 = (bf16[60,512,128]{2,1,0:T(8,128)(2,1)}, bf16[60,512,128]{2,1,0:T(8,128)(2,1)}, bf16[60,512,128]{2,1,0:T(8,128)(2,1)}, f32[512,128]{1,0:T(8,128)}, f32[8,128]{1,0:T(8,128)}, /*index=5*/f32[60,2,128]{2,1,0:T(2,128)}) custom-call(s32[60,2,128]{2,1,0:T(2,128)} %bitcast.93, f32[2,128]{1,0:T(2,128)} %get-tuple-element.310.own, ...), custom_call_target="tpu_custom_call" | custom-call | flops 10066329600 | bytes 23592960 | tf_op jit(solution)/shard_map/msg_fwd/pallas_call | solution.py:164
  223.5 6.0 node_mid.3
  229.5 5.9 all-to-all-start.2
  235.5 27.0 %edge_net.2 = (f32[2,60,192,128]{3,2,1,0:T(8,128)}, bf16[60,192,128]{2,1,0:T(8,128)(2,1)}, f32[192,128]{1,0:T(8,128)}, f32[512,192]{1,0:T(8,128)}, f32[3,192,192]{2,1,0:T(8,128)}, /*index=5*/f32[8,192]{1,0:T(8,128)}) custom-call(s32[60,2,128]{2,1,0:T(2,128)} %bitcast.94, f32[60,2,128]{2,1,0:T(2,128)} %get-tuple-element.113.vs, ...), custom_call_target="tpu_custom_call" | custom-call | flops 12079595520 | bytes 17694720 | tf_op jit(solution)/shard_map/edge_net/pallas_call | solution.py:305
  262.4 1.8 convert_element_type.58
  264.2 5.8 all-to-all-start.4
  270.3 27.2 %edge_net.3 = (f32[2,60,192,128]{3,2,1,0:T(8,128)}, bf16[60,192,128]{2,1,0:T(8,128)(2,1)}, f32[192,128]{1,0:T(8,128)}, f32[512,192]{1,0:T(8,128)}, f32[3,192,192]{2,1,0:T(8,128)}, /*index=5*/f32[8,192]{1,0:T(8,128)}) custom-call(s32[60,2,128]{2,1,0:T(2,128)} %bitcast.95, f32[60,2,128]{2,1,0:T(2,128)} %get-tuple-element.110.vs, ...), custom_call_target="tpu_custom_call", output_to_operand_aliasing={{0}: (10, {})} | custom-call | flops 12079595520 | bytes 17694720 | tf_op jit(solution)/shard_map/edge_net/pallas_call | solution.py:305
  299.3 5.8 all-to-all-start.6
  305.2 11.2 %node_back.2 = (f32[512,128]{1,0:T(8,128)}, f32[128,512]{1,0:T(8,128)}, f32[512,512]{1,0:T(8,128)}, f32[512,2048]{1,0:T(8,128)}, f32[2048,512]{1,0:T(8,128)}, /*...) custom-call(bf16[512,192]{1,0:T(8,128)(2,1)} %bitcast.55, s32[2,1,512]{2,1,0:T(1,128)} %reshape.104.srow, ...), custom_call_target="tpu_custom_call" | custom-call | flops 1073741824 | bytes 20971520 | tf_op jit(solution)/shard_map/node_back/pallas_call | solution.py:639
  316.4 28.5 %msg_bwd.2 = (f32[2,60,192,128]{3,2,1,0:T(8,128)}, f32[512,128]{1,0:T(8,128)}, f32[512,512]{1,0:T(8,128)}, f32[512,512]{1,0:T(8,128)}, f32[192,512]{1,0:T(8,128)}, /*index=5*/f32[8,512]{1,0:T(8,128)}) custom-call(s32[60,2,128]{2,1,0:T(2,128)} %bitcast.96, f32[60,2,128]{2,1,0:T(2,128)} %get-tuple-element.113.vs, bf16[2,60,192,128]{3,2,1,0:T(8,128)(2,1)} %bitcast.86, ...), custom_call_target="tpu_custom_call" | custom-call | flops 16106127360 | bytes 39321600 | tf_op jit(solution)/shard_map/msg_bwd/pallas_call | solution.py:434
  345.6 14.1 %node_back.3 = (f32[512,128]{1,0:T(8,128)}, f32[128,512]{1,0:T(8,128)}, f32[512,512]{1,0:T(8,128)}, f32[512,2048]{1,0:T(8,128)}, f32[2048,512]{1,0:T(8,128)}, /*...) custom-call(bf16[512,192]{1,0:T(8,128)(2,1)} %bitcast.53, ...), custom_call_target="tpu_custom_call", output_to_operand_aliasing={{2}: (17, {}), {3}: (18, {}), {4}: (19, {}), {5}: (20, {}),... | custom-call | flops 1073741824 | bytes 20971520 | tf_op jit(solution)/shard_map/node_back/pallas_call | solution.py:639
  359.7 28.7 %msg_bwd.3 = (f32[2,60,192,128]{3,2,1,0:T(8,128)}, f32[512,128]{1,0:T(8,128)}, f32[512,512]{1,0:T(8,128)}, f32[512,512]{1,0:T(8,128)}, f32[192,512]{1,0:T(8,128)}, /*index=5*/f32[8,512]{1,0:T(8,128)}) custom-call(s32[60,2,128]{2,1,0:T(2,128)} %bitcast.97, f32[60,2,128]{2,1,0:T(2,128)} %get-tuple-element.110.vs, ...), custom_call_target="tpu_custom_call", output_to_operand_aliasing={{0}: (15, {})} | custom-call | flops 16106127360 | bytes 39321600 | tf_op jit(solution)/shard_map/msg_bwd/pallas_call | solution.py:434
  391.4 6.1 all-to-all-start.5
  398.4 18.1 %all-to-all-done.5 = bf16[32,16,512]{2,1,0:T(8,128)(2,1)S(1)} async-done(((bf16[32,16,512]{2,1,0:T(8,128)(2,1)}), bf16[32,16,512]{2,1,0:T(8,128)(2,1)S(1)}, u32[]{:S(2)}, u32[]{:S(2)}) %all-to-all-start.5) | async-done | bytes 524320 | tf_op jit(solution)/shard_map/all_to_all | solution.py:706
  416.5 3.7 all-to-all-start.7
  420.2 4.1 node_end.2
  424.3 21.2 %all-to-all-done.7 = bf16[32,16,512]{2,1,0:T(8,128)(2,1)S(1)} async-done(((bf16[32,16,512]{2,1,0:T(8,128)(2,1)}), bf16[32,16,512]{2,1,0:T(8,128)(2,1)S(1)}, u32[]{:S(2)}, u32[]{:S(2)}) %all-to-all-start.7) | async-done | bytes 524320 | tf_op jit(solution)/shard_map/all_to_all | solution.py:706
  446.3 4.6 node_end.3
  450.9 4.2 pad_maximum_fusion
  455.3 75.3 %reduce-scatter.11.cloned.1.call-done = f32[128,2048]{1,0:T(8,128)} async-done(((f32[512,2048]{1,0:T(8,128)}), f32[128,2048]{1,0:T(8,128)}) %reduce-scatter.11.cloned.1.call-update) | async-done | bytes 1048592 | tf_op jit(solution)/shard_map/reduce_scatter | solution.py:799
  530.6 79.7 %reduce-scatter.13.cloned.1.call-done = f32[512,512]{1,0:T(8,128)} async-done(((f32[2048,512]{1,0:T(8,128)}), f32[512,512]{1,0:T(8,128)}) %reduce-scatter.13.cloned.1.call-update) | async-done | bytes 1048592 | tf_op jit(solution)/shard_map/reduce_scatter | solution.py:799
  610.3 79.6 %reduce-scatter.7.cloned.1.call-done = f32[4,128,512]{2,1,0:T(8,128)} async-done(((f32[4,512,512]{2,1,0:T(8,128)}), f32[4,128,512]{2,1,0:T(8,128)}) %reduce-scatter.7.cloned.1.call-update) | async-done | bytes 1048592 | tf_op jit(solution)/shard_map/reduce_scatter | solution.py:799
  695.2 18.6 %all-reduce.4 = f32[8256]{0:T(1024)S(1)} all-reduce(f32[8256]{0:T(1024)S(1)} %concatenate.3), channel_id=8, replica_groups=mesh['res'=8,'tp'=4] {'tp'}, use_global_device_ids=true, to_apply=%region_18.19.clone | all-reduce | flops 8256 | bytes 66048
  713.8 22.5 %psum.62 = f32[2064]{0:T(1024)S(1)} all-reduce(f32[2064]{0:T(1024)S(1)} %dynamic-slice.2), channel_id=1, replica_groups=mesh['res'=8,'tp'=4] {'res'}, use_global_device_ids=true, to_apply=%region_19.20 | all-reduce | flops 2064 | bytes 16512 | tf_op jit(solution)/shard_map/psum | solution.py:797
  736.9 34.5 %all-reduce.8.cloned.1.call-done = (f32[4,128,512]{2,1,0:T(8,128)}, f32[48,512]{1,0:T(8,128)}, f32[128,2048]{1,0:T(8,128)}, f32[512,512]{1,0:T(8,128)}, f32[2,128,192]{2,1,0:T(8,128)}, /*index=5*/f32[3,48,192]{2,1,0:T(8,128)}) async-done(((f32[4,128,512]{2,1,0:T(8,128)}, f32[48,512]{1,0:T(8,128)}, f32[128,2048]{1,0:T(8,128)}, f32[512,512]{1,0:T(8,128)}, f32[2,128,192]{2,1,0:T(8,128)}, ...) | async-done | bytes 3551248 | tf_op jit(solution)/shard_map/psum | solution.py:797
  771.4 2.1 multiply_reduce_fusion.2
  775.1 2.1 multiply_reduce_fusion.1
  777.2 2.1 multiply_reduce_fusion
  788.8 12.2 %psum.63 = f32[]{:T(128)} all-reduce(f32[]{:T(128)S(6)} %add.172), channel_id=1, replica_groups=mesh['res'=8,'tp'=4] {'tp'}, use_global_device_ids=true, to_apply=%region_21.22 | all-reduce | flops 1 | bytes 8 | tf_op jit(solution)/shard_map/psum | solution.py:806
  801.8 1.9 multiply_subtract_fusion.3
  808.4 2.0 multiply_subtract_fusion.4
  810.4 3.8 multiply_subtract_fusion
  814.4 2.3 multiply_subtract_fusion.1
  817.9 2.3 multiply_subtract_fusion.2
  (159 shorter events, 31.9 us)
Async XLA Ops:
  7.2 5.5 copy-start.38
  7.2 4.5 copy-start
  7.2 5.4 copy-start.36
  7.2 28.6 %copy-start.37 = (s32[2,1,32,16]{2,3,1,0:T(8,128)S(1)}, s32[2,1,32,16]{2,3,1,0:T(8,128)}, u32[]{:S(2)}) copy-start(s32[2,1,32,16]{2,3,1,0:T(8,128)} %param.32) | copy-start | bytes 12292
  7.2 29.9 %copy-start.39 = (s32[2,128]{1,0:T(2,128)S(1)}, s32[2,128]{1,0:T(2,128)}, u32[]{:S(2)}) copy-start(s32[2,128]{1,0:T(2,128)} %param.33) | copy-start | bytes 3076
  7.3 29.9 %copy-start.40 = (s32[2,128]{1,0:T(2,128)S(1)}, s32[2,128]{1,0:T(2,128)}, u32[]{:S(2)}) copy-start(s32[2,128]{1,0:T(2,128)} %param.34) | copy-start | bytes 3076
  7.3 150.1 %all-gather.4.cloned.1.call-start = ((), (), s32[]{:S(2)}) async-start(), calls=%async_computation.14 | async-start | bytes 2621440 | tf_op jit(solution)/shard_map/all_gather | solution.py:719
  9.5 37.1 %copy-start.24 = (f32[48,512]{1,0:T(8,128)S(1)}, f32[48,512]{1,0:T(8,128)}, u32[]{:S(2)}) copy-start(f32[48,512]{1,0:T(8,128)} %param.38) | copy-start | bytes 294916
  9.5 175.6 %all-gather.6.cloned.1.call-start = ((), (), s32[]{:S(2)}) async-start(), calls=%async_computation.15 | async-start | bytes 2621440 | tf_op jit(solution)/shard_map/all_gather | solution.py:721
  11.6 36.3 %copy-start.20 = (f32[2,128,192]{1,2,0:T(8,128)S(1)}, f32[2,128,192]{1,2,0:T(8,128)}, u32[]{:S(2)}) copy-start(f32[2,128,192]{1,2,0:T(8,128)} %param.41) | copy-start | bytes 589828
  11.6 36.5 %copy-start.23 = (f32[3,48,192]{2,1,0:T(8,128)S(1)}, f32[3,48,192]{2,1,0:T(8,128)}, u32[]{:S(2)}) copy-start(f32[3,48,192]{2,1,0:T(8,128)} %param.42) | copy-start | bytes 331780
  11.7 173.7 %all-gather.8.cloned.1.call-start = ((), (), s32[]{:S(2)}) async-start(), calls=%async_computation.16 | async-start | bytes 2621440 | tf_op jit(solution)/shard_map/all_gather | solution.py:722
  43.8 28.9 %all-to-all-start = ((bf16[32,16,640]{2,1,0:T(8,128)(2,1)}), bf16[32,16,640]{2,1,0:T(8,128)(2,1)S(1)}, u32[]{:S(2)}, u32[]{:S(2)}) async-start(bf16[32,16,640]{2,1,0:T(8,128)(2,1)} %bitcast.3), calls=%async_computation | async-start | bytes 1310720 | tf_op jit(solution)/shard_map/all_to_all | solution.py:706
  72.7 84.7 %copy-start.22 = (bf16[32,16,640]{2,1,0:T(8,128)(2,1)}, bf16[32,16,640]{2,1,0:T(8,128)(2,1)S(1)}, u32[]{:S(2)}) copy-start(bf16[32,16,640]{2,1,0:T(8,128)(2,1)S(1)} %all-to-all-done) | copy-start | bytes 1966084
  72.7 118.7 %all-to-all-start.1 = ((bf16[32,16,640]{2,1,0:T(8,128)(2,1)}), bf16[32,16,640]{2,1,0:T(8,128)(2,1)S(1)}, u32[]{:S(2)}, u32[]{:S(2)}) async-start(bf16[32,16,640]{2,1,0:T(8,128)(2,1)} %bitcast.7), calls=%async_computation.1 | async-start | bytes 1310720 | tf_op jit(solution)/shard_map/all_to_all | solution.py:706
  191.4 4.4 copy-start.21
  191.4 38.1 %all-to-all-start.3 = ((bf16[32,16,192]{2,1,0:T(8,128)(2,1)}), bf16[32,16,192]{2,1,0:T(8,128)(2,1)S(1)}, u32[]{:S(2)}, u32[]{:S(2)}) async-start(bf16[32,16,192]{2,1,0:T(8,128)(2,1)} %bitcast.61), calls=%async_computation.3 | async-start | bytes 524288 | tf_op jit(solution)/shard_map/all_to_all | solution.py:706
  229.5 6.0 copy-start.27
  229.5 34.7 %all-to-all-start.2 = ((bf16[32,16,192]{2,1,0:T(8,128)(2,1)}), bf16[32,16,192]{2,1,0:T(8,128)(2,1)S(1)}, u32[]{:S(2)}, u32[]{:S(2)}) async-start(bf16[32,16,192]{2,1,0:T(8,128)(2,1)} %bitcast.63), calls=%async_computation.2 | async-start | bytes 524288 | tf_op jit(solution)/shard_map/all_to_all | solution.py:706
  264.2 6.1 copy-start.28
  264.2 35.0 %all-to-all-start.4 = ((bf16[32,16,192]{2,1,0:T(8,128)(2,1)}), bf16[32,16,192]{2,1,0:T(8,128)(2,1)S(1)}, u32[]{:S(2)}, u32[]{:S(2)}) async-start(bf16[32,16,192]{2,1,0:T(8,128)(2,1)} %bitcast.16), calls=%async_computation.4 | async-start | bytes 524288 | tf_op jit(solution)/shard_map/all_to_all | solution.py:706
  270.1 185.1 %reduce-scatter.17.cloned.1.call-start = ((), (), s32[]{:S(2)}) async-start(), calls=%async_computation.22 | async-start | bytes 737280 | tf_op jit(solution)/shard_map/reduce_scatter | solution.py:799
  299.3 5.9 copy-start.11
  299.3 45.6 %all-to-all-start.6 = ((bf16[32,16,192]{2,1,0:T(8,128)(2,1)}), bf16[32,16,192]{2,1,0:T(8,128)(2,1)S(1)}, u32[]{:S(2)}, u32[]{:S(2)}) async-start(bf16[32,16,192]{2,1,0:T(8,128)(2,1)} %bitcast.21), calls=%async_computation.6 | async-start | bytes 524288 | tf_op jit(solution)/shard_map/all_to_all | solution.py:706
  305.1 150.1 %reduce-scatter.9.cloned.1.call-start = ((), (), s32[]{:S(2)}) async-start(), calls=%async_computation.18 | async-start | bytes 491520 | tf_op jit(solution)/shard_map/reduce_scatter | solution.py:799
  388.5 66.8 %reduce-scatter.15.cloned.1.call-start = ((), (), s32[]{:S(2)}) async-start(), calls=%async_computation.21 | async-start | bytes 1310720 | tf_op jit(solution)/shard_map/reduce_scatter | solution.py:799
  389.0 141.5 %reduce-scatter.11.cloned.1.call-start = ((), (), s32[]{:S(2)}) async-start(), calls=%async_computation.19 | async-start | bytes 5242880 | tf_op jit(solution)/shard_map/reduce_scatter | solution.py:799
  389.8 7.7 copy-start.13
  389.8 220.5 %reduce-scatter.13.cloned.1.call-start = ((), (), s32[]{:S(2)}) async-start(), calls=%async_computation.20 | async-start | bytes 5242880 | tf_op jit(solution)/shard_map/reduce_scatter | solution.py:799
  391.4 25.0 %all-to-all-start.5 = ((bf16[32,16,512]{2,1,0:T(8,128)(2,1)}), bf16[32,16,512]{2,1,0:T(8,128)(2,1)S(1)}, u32[]{:S(2)}, u32[]{:S(2)}) async-start(bf16[32,16,512]{2,1,0:T(8,128)(2,1)} %bitcast.18), calls=%async_computation.5 | async-start | bytes 1048576 | tf_op jit(solution)/shard_map/all_to_all | solution.py:706
  416.5 3.8 copy-start.8
  416.5 29.1 %all-to-all-start.7 = ((bf16[32,16,512]{2,1,0:T(8,128)(2,1)}), bf16[32,16,512]{2,1,0:T(8,128)(2,1)S(1)}, u32[]{:S(2)}, u32[]{:S(2)}) async-start(bf16[32,16,512]{2,1,0:T(8,128)(2,1)} %bitcast.23), calls=%async_computation.7 | async-start | bytes 1048576 | tf_op jit(solution)/shard_map/all_to_all | solution.py:706
  420.2 269.7 %reduce-scatter.7.cloned.1.call-start = ((), (), s32[]{:S(2)}) async-start(), calls=%async_computation.17 | async-start | bytes 5242880 | tf_op jit(solution)/shard_map/reduce_scatter | solution.py:799
  424.3 26.6 %copy-start.6 = (f32[512,512]{1,0:T(8,128)S(1)}, f32[512,512]{1,0:T(8,128)}, u32[]{:S(2)}) copy-start(f32[512,512]{1,0:T(8,128)} %get-tuple-element.167) | copy-start | bytes 3145732
  445.5 5.4 copy-start.19
  455.1 234.9 %copy-start.30 = (f32[2,128,192]{1,2,0:T(8,128)S(1)}, f32[2,128,192]{1,2,0:T(8,128)}, u32[]{:S(2)}) copy-start(f32[2,128,192]{1,2,0:T(8,128)} %param.48) | copy-start | bytes 589828
  455.1 235.1 %copy-start.31 = (f32[2,128,192]{1,2,0:T(8,128)S(1)}, f32[2,128,192]{1,2,0:T(8,128)}, u32[]{:S(2)}) copy-start(f32[2,128,192]{1,2,0:T(8,128)} %param.55) | copy-start | bytes 589828
  455.1 235.9 %copy-start.10 = (f32[128,512]{1,0:T(8,128)S(1)}, f32[128,512]{1,0:T(8,128)}, u32[]{:S(2)}) copy-start(f32[128,512]{1,0:T(8,128)} %get-tuple-element.109.out) | copy-start | bytes 786436
  455.1 235.9 %copy-start.14 = (f32[128,512]{1,0:T(8,128)S(1)}, f32[128,512]{1,0:T(8,128)}, u32[]{:S(2)}) copy-start(f32[128,512]{1,0:T(8,128)} %get-tuple-element.106.out) | copy-start | bytes 786436
  455.1 238.3 %copy-start.35 = (f32[8,512]{1,0:T(8,128)S(1)}, f32[8,512]{1,0:T(8,128)}, u32[]{:S(2)}) copy-start(f32[8,512]{1,0:T(8,128)} %get-tuple-element.174) | copy-start | bytes 49156
  455.1 316.3 %all-reduce.8.cloned.1.call-start = ((), (), s32[]{:S(2)}) async-start(), calls=%async_computation.23 | async-start | bytes 7307264 | tf_op jit(solution)/shard_map/psum | solution.py:797
  689.9 97.2 %copy-start.29 = (f32[128,512]{1,0:T(8,128)S(1)}, f32[128,512]{1,0:T(8,128)}, u32[]{:S(2)}) copy-start(f32[128,512]{1,0:T(8,128)} %get-tuple-element.135) | copy-start | bytes 786436
  736.3 65.4 %copy-start.32 = (f32[2064]{0:T(1024)}, f32[2064]{0:T(1024)S(1)}, u32[]{:S(2)}) copy-start(f32[2064]{0:T(1024)S(1)} %psum.62) | copy-start | bytes 24772
  773.5 36.9 %copy-start.5 = (f32[512,512]{1,0:T(8,128)S(1)}, f32[512,512]{1,0:T(8,128)}, u32[]{:S(2)}) copy-start(f32[512,512]{1,0:T(8,128)} %get-tuple-element.285) | copy-start | bytes 3145732
  808.4 5.9 copy-start.1
  808.4 5.9 copy-start.4
  808.4 5.9 copy-start.15
  808.4 5.9 copy-start.16
  (11 other events, 25.3 us)
Sparse Core Ops, SparseCore 0:
  10.2 61.0 all-gather.3
  73.5 62.6 all-gather.5
  138.4 46.9 all-gather.7
  299.4 25.5 reduce-scatter.16
  388.6 24.3 reduce-scatter.8
  415.8 36.1 reduce-scatter.14
  454.4 76.1 reduce-scatter.10
  533.0 77.2 reduce-scatter.12
  612.6 77.2 reduce-scatter.6
  694.3 77.0 all-reduce.7

commit v2 on v1

--- a/solution.py
+++ b/solution.py
@@ -104,8 +104,20 @@
     return jnp.concatenate([ref3[k0 + j] for j in range(count)], axis=1)
 
 
+def stacked(ref, lo=0, n=None, c0=0, cols=D):
+    n = ref.shape[1] if n is None else n
+    if n % 16 == 0:
+        return ref[:, lo : lo + n, c0 : c0 + cols].reshape(ref.shape[0] * n, cols)
+    parts = [ref[t, :, c0 : c0 + cols].astype(f32)[lo : lo + n] for t in range(ref.shape[0])]
+    return jnp.concatenate(parts, axis=0).astype(bf16)
+
+
+def unit(T, n, index):
+    return pl.BlockSpec((T, n, D), lambda i: (0, index, 0))
+
+
 def msg_fwd_body(
-    m, KB, sub, S, slot, own, ef, tab, u1, wnbr, wself, wedge, w2, rows,
+    m, KB, sub, S, slot, own, ef, tab, x, wnbr, wself, wedge, w2, rows,
     p1o, d1o, d2o, pso, cnto, vso, tt_s, zs_s, zc_s, we_s, w2_s, c2_s,
 ):
     step = pl.program_id(0)
@@ -113,13 +125,19 @@
 
     @pl.when(step == 0)
     def _():
-        tt_s[0:D, :] = dot(tab[0, :, 0:D], wnbr[0]).T.astype(bf16)
-        tt_s[D:, :] = tab[0, :, D : D + 128].astype(f32).T[0:16, :].astype(bf16)
-        zs = dot(u1[0], wself[0]) + rows[6:7, :]
+        g1, b1 = rows[0:1, :], rows[1:2, :]
+        wn = stacked(wnbr)
+        for c in range(0, S, 512):
+            near = (normed(tab[c : c + 512, 0:D].astype(f32))[0] * g1 + b1).astype(bf16)
+            tt_s[0:D, c : c + 512] = dot(near, wn).T.astype(bf16)
+            tags = tab[c : c + 512, D : D + 128].astype(f32).T
+            tt_s[D:, c : c + 512] = tags[0:16, :].astype(bf16)
+        u1 = (normed(x[0].astype(f32))[0] * g1 + b1).astype(bf16)
+        zs = dot(u1, stacked(wself)) + rows[6:7, :]
         zs_s[...] = zs.T
         zc_s[...] = (zs + rows[7:8, :]).T
-        we_s[...] = wedge[...].astype(f32).T.astype(bf16)
-        w2_s[...] = w2[0].astype(f32).T.astype(bf16)
+        we_s[...] = stacked(wedge, 0, E // wedge.shape[0]).astype(f32).T.astype(bf16)
+        w2_s[...] = stacked(w2).astype(f32).T.astype(bf16)
         c2_s[...] = jnp.broadcast_to(rows[8:9, :], (N, D)).T
         pso[...] = jnp.zeros_like(pso)
         cnto[...] = jnp.zeros_like(cnto)
@@ -158,9 +176,11 @@
                 pso[c : c + FC, :] += p * vals[j]
 
 
-def msg_fwd(m, slot, own, ef, tab, u1, square, wedge, rows, KB=12, sub=6):
+def msg_fwd(m, slot, own, ef, tab, x, l0, l1, rows, KB=12, sub=6):
     K, N = ef.shape[1], ef.shape[3]
-    S = tab.shape[1]
+    S = tab.shape[0]
+    T = l0.shape[0]
+    U = D // T
     return pl.pallas_call(
         functools.partial(msg_fwd_body, m, KB, sub, S),
         grid=(K // KB,),
@@ -168,12 +188,12 @@
             pl.BlockSpec((KB, 2, N), lambda i: (i, 0, 0)),
             whole(2, N),
             pl.BlockSpec((1, KB, E, N), lambda i: (m, i, 0, 0)),
-            picked(0, S, D + 128),
+            whole(S, D + 128),
             picked(m, N, D),
-            picked(1, D, D),
-            picked(0, D, D),
-            whole(E, D),
-            picked(2, D, D),
+            unit(T, U, 1),
+            unit(T, U, 0),
+            unit(T, U // 2, 2),
+            unit(T, U, 0),
             whole(16, D),
         ],
         out_specs=[
@@ -205,20 +225,22 @@
         cost_estimate=pl.CostEstimate(
             flops=2 * N * K * 10 * 65536, bytes_accessed=N * K * D * 6, transcendentals=0
         ),
-    )(slot, own, ef, tab, u1, square, square, wedge, square, rows)
-
-
-def edge_body(m, KB, sub, S, first, slot, vs, ef, up, tab, ys, vsq, rows, *refs):
-    refs, scr = refs[:-10], refs[-10:]
+    )(slot, own, ef, tab, x, l0, l0, l1, l1, rows)
+
+
+def edge_body(m, KB, sub, S, first, slot, vs, ef, up, tab, ys, strips, rows, *refs):
+    refs, scr = refs[:-11], refs[-11:]
     (eo, gy1o, gyso, so, dvo, dbo) = refs[-6:]
-    (nt_s, vt_s, b_s, oh_s, r1_s, r2_s, g3_s, g2_s, ef_s, acc_s) = scr
+    (nt_s, vsq, vt_s, b_s, oh_s, r1_s, r2_s, g3_s, g2_s, ef_s, acc_s) = scr
     step = pl.program_id(0)
     N = ef.shape[3]
 
     @pl.when(step == 0)
     def _():
         nt_s[...] = turned(tab[...]).astype(bf16)
-        for i in range(3):
+        EP, SP = E // strips.shape[0], strips.shape[1] // 2
+        for i, (lo, c0) in enumerate(((0, 0), (0, 256), (SP, 0))):
+            vsq[i] = stacked(strips, lo, EP, c0, E)
             vt_s[i] = turned(vsq[i]).astype(bf16)
         for i in range(2):
             b_s[i] = jnp.broadcast_to(rows[i + 1 : i + 2, :], (N, E)).T
@@ -281,12 +303,13 @@
         dbo[2:3, :] += jnp.sum(acc_s[1].T, axis=0, keepdims=True)
 
 
-def edge_net(m, slot, vs, ef, up, tab, ys, vsq, rows, before, KB=12, sub=6):
+def edge_net(m, slot, vs, ef, up, tab, ys, m1, rows, before, KB=12, sub=6):
     K, N = ef.shape[1], ef.shape[3]
     S = tab.shape[0]
     first = before is None
     extra = [] if first else list(before)
-    args = [slot, vs, ef, up, tab, ys, vsq, rows]
+    args = [slot, vs, ef, up, tab, ys, m1, rows]
+    T = m1.shape[0]
     specs = [
         pl.BlockSpec((KB, 2, N), lambda i: (i, 0, 0)),
         pl.BlockSpec((KB, 2, N), lambda i: (i, 0, 0)),
@@ -294,7 +317,7 @@
         pl.BlockSpec((1, KB, E, N), lambda i: (m, i, 0, 0)),
         whole(S, E),
         whole(E, N),
-        whole(3, E, E),
+        unit(T, D // T, 5),
         whole(8, E),
     ]
     aliases = {}
@@ -325,6 +348,7 @@
         scratch_shapes=[
             pltpu.VMEM((E, S), bf16),
             pltpu.VMEM((3, E, E), bf16),
+            pltpu.VMEM((3, E, E), bf16),
             pltpu.VMEM((2, E, N), f32),
             pltpu.VMEM((S, L), bf16),
             pltpu.VMEM((E, L), bf16),
@@ -344,16 +368,19 @@
 
 
 def msg_bwd_body(
-    m, KB, sub, S, first, slot, vs, ef, up, p1, d1, d2, gy1, h, w2, wedge, vsq, *refs
+    m, KB, sub, S, first, slot, vs, ef, up, p1, d1, d2, gy1, h, w2u, strip, strips, *refs
 ):
-    refs, scr = refs[:-4], refs[-4:]
+    refs, scr = refs[:-7], refs[-7:]
     (ego, gzso, so, dw2o, dweo, dbo) = refs[-6:]
-    (oh_s, g2_s, g1_s, acc_s) = scr
+    (oh_s, g2_s, g1_s, acc_s, w2, wedge, ve) = scr
     step = pl.program_id(0)
     N = ef.shape[3]
 
     @pl.when(step == 0)
     def _():
+        w2[...] = stacked(w2u)
+        wedge[...] = stacked(strip, 0, E // strip.shape[0])
+        ve[...] = stacked(strips, 0, E // strip.shape[0], 0, E)
         gzso[...] = jnp.zeros_like(gzso)
         acc_s[...] = jnp.zeros_like(acc_s)
         if first:
@@ -376,7 +403,7 @@
                 g = d2[k0 + j, c : c + FC, :].astype(f32) * h[c : c + FC, :]
                 acc_s[0, c : c + FC, :] += g
                 g2_s[c : c + FC, lo + j * N : lo + (j + 1) * N] = g.astype(bf16)
-        back = dot(w2[0], g2_s[:, lo : lo + w])
+        back = dot(w2[...], g2_s[:, lo : lo + w])
         for j in range(sub):
             same = vs[k0 + j, 1:2, :]
             for c in range(0, D, FC):
@@ -384,7 +411,7 @@
                 gzso[c : c + FC, :] += g
                 acc_s[1, c : c + FC, :] += g * same
                 g1_s[c : c + FC, lo + j * N : lo + (j + 1) * N] = g.astype(bf16)
-        back = dot(wedge[...], g1_s[:, lo : lo + w]) + dot(vsq[0], wide(gy1, k0, sub))
+        back = dot(wedge[...], g1_s[:, lo : lo + w]) + dot(ve[...], wide(gy1, k0, sub))
         for j in range(sub):
             ego[0, k0 + j] = up[0, k0 + j].astype(f32) + back[:, j * N : (j + 1) * N]
     g1 = g1_s[...]
@@ -407,11 +434,13 @@
         dbo[1:2, :] += jnp.sum(acc_s[1].T, axis=0, keepdims=True)
 
 
-def msg_bwd(m, S, slot, vs, ef, up, p1, d1, d2, gy1, h, square, wedge, vsq, before, KB=12, sub=6):
+def msg_bwd(m, S, slot, vs, ef, up, p1, d1, d2, gy1, h, l1, m1, before, KB=12, sub=6):
     K, N = ef.shape[1], ef.shape[3]
     first = before is None
     extra = [] if first else list(before)
-    args = [slot, vs, ef, up, p1, d1, d2, gy1, h, square, wedge, vsq]
+    args = [slot, vs, ef, up, p1, d1, d2, gy1, h, l1, l1, m1]
+    T = l1.shape[0]
+    U = D // T
     specs = [
         pl.BlockSpec((KB, 2, N), lambda i: (i, 0, 0)),
         pl.BlockSpec((KB, 2, N), lambda i: (i, 0, 0)),
@@ -422,9 +451,9 @@
         pl.BlockSpec((KB, D, N), lambda i: (i, 0, 0)),
         pl.BlockSpec((KB, E, N), lambda i: (i, 0, 0)),
         whole(D, N),
-        picked(2, D, D),
-        whole(E, D),
-        picked(0, E, E),
+        unit(T, U, 0),
+        unit(T, U // 2, 2),
+        unit(T, U // 2, 10),
     ]
     aliases = {}
     if not first:
@@ -456,6 +485,9 @@
             pltpu.VMEM((D, L), bf16),
             pltpu.VMEM((D, L), bf16),
             pltpu.VMEM((2, D, N), f32),
+            pltpu.VMEM((D, D), bf16),
+            pltpu.VMEM((E, D), bf16),
+            pltpu.VMEM((E, E), bf16),
         ],
         input_output_aliases=aliases,
         compiler_params=pltpu.CompilerParams(vmem_limit_bytes=VMEM_LIMIT),
@@ -491,61 +523,60 @@
     return xhat * row + shift, xhat, rs
 
 
-def node_in_body(x, rows, srow, tags, u1o, sendo):
+def node_in_body(x, srow, tags, sendo):
     _, N, _ = x.shape
     S = srow.shape[2]
     for m in range(x.shape[0]):
-        u1 = scaled(x[m].astype(f32), rows[0:1, :], rows[1:2, :])[0].astype(bf16)
-        u1o[m] = u1
         oh = picked_rows(srow[m], N, S)
-        sendo[m, :, 0:D] = tdot(oh, u1).astype(bf16)
+        sendo[m, :, 0:D] = tdot(oh, x[m]).astype(bf16)
         sendo[m, :, D:] = tdot(oh, tags[m]).astype(bf16)
 
 
-def node_in(x, rows, srow, tags):
+def node_in(x, srow, tags):
     MB, N, _ = x.shape
     S = srow.shape[2]
     return pl.pallas_call(
         node_in_body,
-        out_shape=[
-            jax.ShapeDtypeStruct((MB, N, D), bf16),
-            jax.ShapeDtypeStruct((MB, S, D + 128), bf16),
-        ],
+        out_shape=jax.ShapeDtypeStruct((MB, S, D + 128), bf16),
         compiler_params=pltpu.CompilerParams(vmem_limit_bytes=VMEM_LIMIT),
         name="node_in",
-    )(x, rows, srow, tags)
+    )(x, srow, tags)
 
 
 def node_mid_body(
-    ps, cnt, x, w3, wup, wdown, vin, rows, c4, rowe, srow,
+    ps, cnt, x, w3, wup, wdown, vinu, rows, c4, rowe, srow,
     outo, x1o, a2o, qo, qdo, wo, yso, sendo,
 ):
     N = x.shape[1]
     S = srow.shape[2]
+    U = vinu.shape[1]
     cnt_col = cnt[...].T[:, 0:1]
-    total = split_dot(ps[...].T, w3[0]) + cnt_col * rows[9:10, :]
+    total = split_dot(ps[...].T, stacked(w3)) + cnt_col * rows[9:10, :]
     x1 = x[0].astype(f32) + total / jnp.maximum(cnt_col, 1.0)
     x1o[...] = x1
     a2 = scaled(x1, rows[2:3, :], rows[3:4, :])[0].astype(bf16)
     a2o[...] = a2
     out = x1 + rows[10:11, :]
+    wd = stacked(wdown)
     for c in range(0, F, 512):
-        q, qd = gelu_pair(dot(a2, wup[:, c : c + 512]) + c4[0:1, c : c + 512])
+        q, qd = gelu_pair(dot(a2, stacked(wup, c // 512 * U, U)) + c4[0:1, c : c + 512])
         q = q.astype(bf16)
         qo[:, c : c + 512] = q
         qdo[:, c : c + 512] = qd
-        out = out + dot(q, wdown[c : c + 512, :])
+        out = out + dot(q, wd[c : c + 512, :])
     outo[...] = out
     w = scaled(out, rows[4:5, :], rows[5:6, :])[0].astype(bf16)
     wo[...] = w
-    yso[...] = (dot(w, vin[0]) + rowe[0:1, :]).T
-    near = dot(w, vin[1]).astype(bf16)
+    yso[...] = (dot(w, stacked(vinu, 0, U, 0, E)) + rowe[0:1, :]).T
+    near = dot(w, stacked(vinu, 0, U, 256, E)).astype(bf16)
     sendo[...] = tdot(picked_rows(srow[0], N, S), near).astype(bf16)
 
 
-def node_mid(m, ps, cnt, x, square, wup, wdown, vin, rows, c4, rowe, srow):
+def node_mid(m, ps, cnt, x, m0, m1, rows, c4, rowe, srow):
     N = x.shape[1]
     S = srow.shape[2]
+    T = m0.shape[0]
+    U = D // T
     shapes = [
         jax.ShapeDtypeStruct((N, D), f32),
         jax.ShapeDtypeStruct((N, D), f32),
@@ -560,24 +591,26 @@
         node_mid_body,
         grid=(1,),
         in_specs=[
-            whole(D, N), whole(8, N), picked(m, N, D), picked(3, D, D), whole(D, F), whole(F, D),
-            whole(2, D, E), whole(16, D), whole(8, F), whole(8, E), picked(m, 1, S),
+            whole(D, N), whole(8, N), picked(m, N, D), unit(T, U, 4), unit(T, 4 * U, 0),
+            unit(T, 4 * U, 0), unit(T, U, 4), whole(16, D), whole(8, F), whole(8, E), picked(m, 1, S),
         ],
         out_specs=[whole(*s.shape) for s in shapes],
         out_shape=shapes,
         compiler_params=pltpu.CompilerParams(vmem_limit_bytes=VMEM_LIMIT),
         name="node_mid",
         cost_estimate=pl.CostEstimate(flops=2 * N * D * F * 2, bytes_accessed=8 << 20, transcendentals=0),
-    )(ps, cnt, x, square, wup, wdown, vin, rows, c4, rowe, srow)
+    )(ps, cnt, x, m0, m1, m0, m1, rows, c4, rowe, srow)
 
 
 def node_back_body(
-    inc, srow, gys_t, vin, w, out, x1, a2, q, qd, up, wup, wdown, w3, rows, ps, cnt, *refs
+    inc, srow, gys_t, vinu, w, out, x1, a2, q, qd, up, wup, wdown, w3, rows, ps, cnt, *refs
 ):
     first = len(refs) == 8
     old, (ho, gx1o, dw3o, dupo, ddowno, dvino, vro, vwo) = refs[:-8], refs[-8:]
     N = w.shape[0]
     S = srow.shape[2]
+    U = vinu.shape[1]
+    w3v, wd = stacked(w3), stacked(wdown)
 
     def put(i, ref, sl, v):
         ref[sl] = v if first else old[i][sl] + v
@@ -588,7 +621,9 @@
     wv = w[...]
     put(3, dvino, 0, split_tdot(wv, gys))
     put(3, dvino, 1, split_tdot(wv, near))
-    gw = split_dot_t(gys, vin[0]) + split_dot_t(near, vin[1])
+    gw = split_dot_t(gys, stacked(vinu, 0, U, 0, E)) + split_dot_t(
+        near, stacked(vinu, 0, U, 256, E)
+    )
     xhat, rs = normed(out[...])
     gx, dg3, db3 = norm_back(xhat, rs, rows[4:5, :], gw)
     gx2 = up[0].astype(f32) + gx
@@ -598,17 +633,17 @@
     for c in range(0, F, 512):
         sl = slice(c, c + 512)
         put(2, ddowno, (sl, slice(None)), tdot(q[:, sl], gy))
-        gf = (qd[:, sl] * dot_t(gy, wdown[sl, :])).astype(bf16)
+        gf = (qd[:, sl] * dot_t(gy, wd[sl, :])).astype(bf16)
         put(1, dupo, (slice(None), sl), tdot(a2[...], gf))
         put(5, vwo, (slice(0, 1), sl), jnp.sum(gf.astype(f32), axis=0, keepdims=True))
-        ga2 = ga2 + dot_t(gf, wup[:, sl])
+        ga2 = ga2 + dot_t(gf, stacked(wup, c // 512 * U, U))
     xhat, rs = normed(x1[...])
     gx, dg2, db2 = norm_back(xhat, rs, rows[2:3, :], ga2)
     gx1 = gx2 + gx
     gx1o[...] = gx1
     cnt_col = cnt[...].T[:, 0:1]
     g = (gx1 / jnp.maximum(cnt_col, 1.0)).astype(bf16)
-    ho[...] = dot_t(g, w3[0]).T
+    ho[...] = dot_t(g, w3v).T
     put(0, dw3o, slice(None), split_dot(ps[...], g))
     dc3 = jnp.sum(g.astype(f32) * cnt_col, axis=0, keepdims=True)
     dd1 = jnp.sum(gys, axis=0, keepdims=True)
@@ -619,7 +654,7 @@
     vwo[1:8, :] = jnp.zeros((7, F), f32)
 
 
-def node_back(m, inc, srow, gys_t, vin, kept, up, wup, wdown, square, rows, ps, cnt, before):
+def node_back(m, inc, srow, gys_t, kept, up, m0, m1, rows, ps, cnt, before):
     out, x1, a2, q, qd, w = kept
     N = w.shape[0]
     S = srow.shape[2]
@@ -634,15 +669,17 @@
         jax.ShapeDtypeStruct((8, F), f32),
     ]
     extra = [] if before is None else list(before)
-    args = [inc, srow, gys_t, vin, w, out, x1, a2, q, qd, up, wup, wdown, square, rows, ps, cnt]
+    args = [inc, srow, gys_t, m1, w, out, x1, a2, q, qd, up, m1, m0, m0, rows, ps, cnt]
+    T = m0.shape[0]
+    U = D // T
     aliases = {len(args) + i: 2 + i for i in range(len(extra))}
     return pl.pallas_call(
         node_back_body,
         grid=(1,),
         in_specs=[
-            whole(S, E), picked(m, 1, S), whole(E, N), whole(2, D, E), whole(N, D), whole(N, D),
-            whole(N, D), whole(N, D), whole(N, F), whole(N, F), picked(m, N, D), whole(D, F),
-            whole(F, D), picked(3, D, D), whole(16, D), whole(D, N), whole(8, N),
+            whole(S, E), picked(m, 1, S), whole(E, N), unit(T, U, 4), whole(N, D), whole(N, D),
+            whole(N, D), whole(N, D), whole(N, F), whole(N, F), picked(m, N, D), unit(T, 4 * U, 0),
+            unit(T, 4 * U, 0), unit(T, U, 4), whole(16, D), whole(D, N), whole(8, N),
         ]
         + [whole(*v.shape) for v in extra],
         out_specs=[whole(*s.shape) for s in shapes],
@@ -654,21 +691,22 @@
     )(*args, *extra)
 
 
-def node_end_body(inc, srow, gzs_t, u1, x, gx1, wself, wnbr, rows, *refs):
+def node_end_body(inc, srow, gzs_t, x, gx1, wself, wnbr, rows, *refs):
     first = len(refs) == 3
     old, (go, dwo, vro) = refs[:-3], refs[-3:]
-    N = u1.shape[1]
+    N = x.shape[1]
     S = srow.shape[2]
+    xhat, rs = normed(x[0].astype(f32))
+    u1 = (xhat * rows[0:1, :] + rows[1:2, :]).astype(bf16)
 
     def put(i, ref, sl, v):
         ref[sl] = v if first else old[i][sl] + v
 
     near = dot(picked_rows(srow[0], N, S), inc[...])
     gzs = gzs_t[...].T
-    put(0, dwo, 0, split_tdot(u1[0], gzs))
-    put(0, dwo, 1, split_tdot(u1[0], near))
-    gu1 = split_dot_t(gzs, wself[0]) + split_dot_t(near, wnbr[0])
-    xhat, rs = normed(x[0].astype(f32))
+    put(0, dwo, 0, split_tdot(u1, gzs))
+    put(0, dwo, 1, split_tdot(u1, near))
+    gu1 = split_dot_t(gzs, stacked(wself)) + split_dot_t(near, stacked(wnbr))
     gx, dg1, db1 = norm_back(xhat, rs, rows[0:1, :], gu1)
     go[...] = gx1[...] + gx
     for i, v in enumerate((dg1, db1, jnp.sum(gzs, axis=0, keepdims=True))):
@@ -676,7 +714,9 @@
     vro[3:8, :] = jnp.zeros((5, D), f32)
 
 
-def node_end(m, inc, srow, gzs_t, u1, x, gx1, square, rows, before):
+def node_end(m, inc, srow, gzs_t, x, gx1, l0, rows, before):
+    T = l0.shape[0]
+    U = D // T
     N = x.shape[1]
     S = srow.shape[2]
     shapes = [
@@ -685,13 +725,13 @@
         jax.ShapeDtypeStruct((8, D), f32),
     ]
     extra = [] if before is None else list(before)
-    args = [inc, srow, gzs_t, u1, x, gx1, square, square, rows]
+    args = [inc, srow, gzs_t, x, gx1, l0, l0, rows]
     return pl.pallas_call(
         node_end_body,
         grid=(1,),
         in_specs=[
-            whole(S, D), picked(m, 1, S), whole(D, N), picked(m, N, D), picked(m, N, D),
-            whole(N, D), picked(0, D, D), picked(1, D, D), whole(16, D),
+            whole(S, D), picked(m, 1, S), whole(D, N), picked(m, N, D),
+            whole(N, D), unit(T, U, 0), unit(T, U, 1), whole(16, D),
         ]
         + [whole(*v.shape) for v in extra],
         out_specs=[whole(*s.shape) for s in shapes],
@@ -702,6 +742,336 @@
     )(*args, *extra)
 
 
+def place(R, T):
+    U = D // T
+    lift = lambda rows: -(-rows // (16 * R)) * 16 * R
+    sizes = (lift(2 * U), lift(U + U // 2 + 16), lift(5 * U), lift(6 * U))
+    return U, U // 2, E // T, sizes
+
+
+def bit(r, b):
+    return (r // (1 << b)) % 2
+
+
+def flip(r, b):
+    return r + (1 - 2 * bit(r, b)) * (1 << b)
+
+
+def orders(R):
+    high = list(range(1, R.bit_length() - 1))
+    return (high, high[::-1])
+
+
+def subsets(bits):
+    out = [0]
+    for b in bits:
+        out = out + [v + (1 << b) for v in out]
+    return out
+
+
+def greet(R, T, r, t):
+    barrier = pltpu.get_barrier_semaphore()
+    peers = [(flip(r, b), t) for b in range(R.bit_length() - 1)]
+    peers += [(r, (t + j) % T) for j in range(1, T)]
+    for peer in peers:
+        pl.semaphore_signal(barrier, inc=1, device_id=peer, device_id_type=pl.DeviceIdType.MESH)
+    pl.semaphore_wait(barrier, len(peers))
+
+
+class Sender:
+    def __init__(self, send_sem, recv_sem):
+        self.send_sem, self.recv_sem, self.used, self.started = send_sem, recv_sem, 0, []
+
+    def start(self, src, dst, peer):
+        copy = pltpu.make_async_remote_copy(
+            src_ref=src,
+            dst_ref=dst,
+            send_sem=self.send_sem.at[self.used],
+            recv_sem=self.recv_sem.at[self.used],
+            device_id=peer,
+            device_id_type=pl.DeviceIdType.MESH,
+        )
+        copy.start()
+        self.used += 1
+        self.started.append(copy)
+        return copy
+
+    def finish(self):
+        for copy in self.started:
+            copy.wait_send()
+
+
+def at_slice(index, h):
+    return pl.ds(pl.multiple_of(index * h, 16), h)
+
+
+def rest_of(r, bits):
+    total = 0
+    for b in bits:
+        total = total + bit(r, b) * (1 << b)
+    return total
+
+
+def pack_weights(which, U, SP, refs, outs):
+    EP = refs["wedge"].shape[0] if which == 0 else refs["vsq"].shape[1]
+    a, b = outs
+    if which == 0:
+        a[0:U, :] = refs["square"][0].astype(bf16)
+        a[U : 2 * U, :] = refs["square"][1].astype(bf16)
+        b[0:U, :] = refs["square"][2].astype(bf16)
+        b[U : U + SP, :] = pad_rows(refs["wedge"][...], SP).astype(bf16)
+        b[U + SP : U + SP + 16, :] = refs["vec"][...].astype(bf16)
+    else:
+        F4 = 4 * U
+        a[0:F4, :] = refs["down"][...].astype(bf16)
+        a[F4 : F4 + U, :] = refs["square"][3].astype(bf16)
+        for c in range(4):
+            b[c * U : (c + 1) * U, :] = refs["up"][:, c * D : (c + 1) * D].astype(bf16)
+        zero = jnp.zeros((SP - EP, E), f32)
+        for lo, row, n, v in (
+            (0, F4, U, refs["vin"][0]),
+            (256, F4, U, refs["vin"][1]),
+            (0, F4 + U, SP, jnp.concatenate([refs["vsq"][0], zero], axis=0)),
+            (256, F4 + U, SP, jnp.concatenate([refs["vsq"][1], zero], axis=0)),
+            (0, F4 + U + SP, SP, jnp.concatenate([refs["vsq"][2], zero], axis=0)),
+        ):
+            b[row : row + n, lo : lo + E] = v.astype(bf16)
+
+
+def pad_rows(v, n):
+    return jnp.concatenate([v, jnp.zeros((n - v.shape[0], v.shape[1]), v.dtype)], axis=0)
+
+
+def gather_body(which, R, T, names, *refs):
+    n = len(names)
+    ins = dict(zip(names, refs[:n]))
+    outs = refs[n : n + 2]
+    packs = refs[n + 2 : n + 4]
+    own_sem, send_sem, recv_sem = refs[n + 4 :]
+    U, SP, _, _ = place(R, T)
+    r, t = lax.axis_index("res"), lax.axis_index("tp")
+    greet(R, T, r, t)
+    for p in packs:
+        p[...] = jnp.zeros_like(p)
+    pack_weights(which, U, SP, ins, packs)
+    own = []
+    for i in range(2):
+        copy = pltpu.make_async_copy(packs[i], outs[i].at[t], own_sem.at[i])
+        copy.start()
+        own.append(copy)
+    sender = Sender(send_sem, recv_sem)
+    others = [(t + j) % T for j in range(1, T)]
+    hs = [p.shape[0] // R for p in packs]
+    waiting = []
+    for i in range(2):
+        mine = at_slice(r, hs[i])
+        waiting.append(
+            [sender.start(packs[i].at[mine], outs[i].at[t, mine], (r, o)) for o in others]
+        )
+    paths = [order + [0] for order in orders(R)]
+    nbits = R.bit_length() - 1
+    for step in range(nbits):
+        for i in range(2):
+            for copy in waiting[i]:
+                copy.wait_recv()
+            b = paths[i][step]
+            have = paths[i][:step]
+            fixed = rest_of(r, [c for c in range(nbits) if c not in have])
+            peer = (flip(r, b), t)
+            for s in subsets(have):
+                where = at_slice(fixed + s, hs[i])
+                for o in others:
+                    place_ = outs[i].at[o, where]
+                    waiting[i].append(sender.start(place_, place_, peer))
+            waiting[i] = waiting[i][-len(subsets(have)) * len(others) :]
+    for i in range(2):
+        for copy in waiting[i]:
+            copy.wait_recv()
+    sender.finish()
+    for copy in own:
+        copy.wait()
+
+
+def gather_weights(which, R, T, ins):
+    names = sorted(ins)
+    _, _, _, sizes = place(R, T)
+    sizes = sizes[2 * which : 2 * which + 2]
+    count = 2 * (T - 1) * R
+    return pl.pallas_call(
+        functools.partial(gather_body, which, R, T, names),
+        in_specs=[pl.BlockSpec(memory_space=pltpu.VMEM)] * len(names),
+        out_specs=[pl.BlockSpec(memory_space=pl.ANY)] * 2,
+        out_shape=[jax.ShapeDtypeStruct((T, n, D), bf16) for n in sizes],
+        scratch_shapes=[pltpu.VMEM((n, D), bf16) for n in sizes]
+        + [
+            pltpu.SemaphoreType.DMA((2,)),
+            pltpu.SemaphoreType.DMA((count,)),
+            pltpu.SemaphoreType.DMA((count,)),
+        ],
+        compiler_params=pltpu.CompilerParams(
+            vmem_limit_bytes=VMEM_LIMIT, collective_id=1 + which, has_side_effects=True
+        ),
+        name="gather_weights",
+        cost_estimate=pl.CostEstimate(flops=0, bytes_accessed=60 << 20, transcendentals=0),
+    )(*[ins[k] for k in names])
+
+
+def pack_grads(which, U, SP, T, refs, outs):
+    a, b = outs
+    for t in range(T):
+        sl = slice(t * U, (t + 1) * U)
+        EP = E // T
+        se = slice(t * EP, (t + 1) * EP)
+        if which == 0:
+            a[t, 0:U, :] = refs["dws"][0, sl, :].astype(bf16)
+            a[t, U : 2 * U, :] = refs["dws"][1, sl, :].astype(bf16)
+            b[t, 0:U, :] = refs["dw2"][sl, :].astype(bf16)
+            b[t, U : U + SP, :] = pad_rows(refs["dwe"][se, :], SP).astype(bf16)
+            b[t, U + SP : U + SP + 16, :] = refs["vec"][t].astype(bf16)
+        else:
+            F4 = 4 * U
+            a[t, 0:F4, :] = refs["ddown"][t * F4 : (t + 1) * F4, :].astype(bf16)
+            a[t, F4 : F4 + U, :] = refs["dw3"][sl, :].astype(bf16)
+            for c in range(4):
+                b[t, c * U : (c + 1) * U, :] = refs["dup"][sl, c * D : (c + 1) * D].astype(bf16)
+            zero = jnp.zeros((SP - EP, E), f32)
+            for lo, row, n, v in (
+                (0, F4, U, refs["dvin"][0, sl, :]),
+                (256, F4, U, refs["dvin"][1, sl, :]),
+                (0, F4 + U, SP, jnp.concatenate([refs["dvsq"][0, se, :], zero], axis=0)),
+                (256, F4 + U, SP, jnp.concatenate([refs["dvsq"][1, se, :], zero], axis=0)),
+                (0, F4 + U + SP, SP, jnp.concatenate([refs["dvsq"][2, se, :], zero], axis=0)),
+            ):
+                b[t, row : row + n, lo : lo + E] = v.astype(bf16)
+
+
+def reduce_body(which, R, T, names, *refs):
+    n = len(names)
+    ins = dict(zip(names, refs[:n]))
+    outs = refs[n : n + 2]
+    sqo = refs[n + 2]
+    bufs = refs[n + 3 : n + 5]
+    lands = refs[n + 5 : n + 7]
+    zlands = refs[n + 7 : n + 9]
+    sq_land, send_sem, recv_sem = refs[n + 9 :]
+    U, SP, _, _ = place(R, T)
+    r, t = lax.axis_index("res"), lax.axis_index("tp")
+    greet(R, T, r, t)
+    for p in bufs:
+        p[...] = jnp.zeros_like(p)
+    pack_grads(which, U, SP, T, ins, bufs)
+    sender = Sender(send_sem, recv_sem)
+    nbits = R.bit_length() - 1
+    hs = [p.shape[1] // R for p in bufs]
+    paths = [[0] + order for order in orders(R)]
+    used = [0, 0]
+    waiting = [[], []]
+
+    def halve(i, step):
+        b, done = paths[i][step], paths[i][:step]
+        left = [c for c in range(nbits) if c not in done and c != b]
+        fixed = rest_of(r, done)
+        peer = (flip(r, b), t)
+        waiting[i] = []
+        for s in subsets(left):
+            land = lands[i].at[used[i]]
+            give = at_slice(fixed + (1 - bit(r, b)) * (1 << b) + s, hs[i])
+            keep = at_slice(fixed + bit(r, b) * (1 << b) + s, hs[i])
+            copy = sender.start(bufs[i].at[:, give, :], land, peer)
+            waiting[i].append((copy, used[i], keep))
+            used[i] += 1
+
+    def take(i):
+        for copy, slot, keep in waiting[i]:
+            copy.wait_recv()
+            bufs[i][:, keep, :] = (
+                bufs[i][:, keep, :].astype(f32) + lands[i][slot].astype(f32)
+            ).astype(bf16)
+
+    for step in range(nbits):
+        for i in range(2):
+            if step:
+                take(i)
+            halve(i, step)
+    for i in range(2):
+        take(i)
+        mine = at_slice(r, hs[i])
+        waiting[i] = [
+            sender.start(bufs[i].at[(t + j) % T, mine, :], zlands[i].at[j], (r, (t + j) % T))
+            for j in range(1, T)
+        ]
+    for i in range(2):
+        mine = at_slice(r, hs[i])
+        total = bufs[i][t, mine, :].astype(f32)
+        for j, copy in enumerate(waiting[i]):
+            copy.wait_recv()
+            total = total + zlands[i][j + 1].astype(f32)
+        outs[i][mine, :] = total.astype(bf16)
+        waiting[i] = []
+    paths = [p[::-1] for p in paths]
+    for step in range(nbits):
+        for i in range(2):
+            for copy in waiting[i]:
+                copy.wait_recv()
+            b, have = paths[i][step], paths[i][:step]
+            fixed = rest_of(r, [c for c in range(nbits) if c not in have])
+            waiting[i] = []
+            for s in subsets(have):
+                spot = outs[i].at[at_slice(fixed + s, hs[i]), :]
+                waiting[i].append(sender.start(spot, spot, (flip(r, b), t)))
+    squares = jnp.zeros((8, 128), f32)
+    for i in range(2):
+        for copy in waiting[i]:
+            copy.wait_recv()
+        for c in range(0, outs[i].shape[0], 128):
+            v = outs[i][c : c + 128, :].astype(f32)
+            v = jnp.sum((v * v).reshape(16, 8, D), axis=0)
+            squares = squares + sum(v[:, k : k + 128] for k in range(0, D, 128))
+    if which == 0:
+        squares = squares + ins["sq"][...]
+        sq_land[0] = squares
+        copies = [
+            sender.start(sq_land.at[0], sq_land.at[j], (r, (t + j) % T)) for j in range(1, T)
+        ]
+        for copy in copies:
+            copy.wait_recv()
+        total = 0.0
+        for k in range(T):
+            slot = (t + T - k) % T
+            total = total + jnp.sum(sq_land[slot])
+        squares = jnp.full((8, 128), jnp.sqrt(total), f32)
+    sqo[...] = squares
+    sender.finish()
+
+
+def reduce_grads(which, R, T, ins):
+    names = sorted(ins)
+    _, _, _, sizes = place(R, T)
+    sizes = sizes[2 * which : 2 * which + 2]
+    count = 2 * (2 * (R - 1) + T - 1) + T
+    vm = pl.BlockSpec(memory_space=pltpu.VMEM)
+    return pl.pallas_call(
+        functools.partial(reduce_body, which, R, T, names),
+        in_specs=[vm] * len(names),
+        out_specs=[vm] * 3,
+        out_shape=[jax.ShapeDtypeStruct((n, D), bf16) for n in sizes]
+        + [jax.ShapeDtypeStruct((8, 128), f32)],
+        scratch_shapes=[pltpu.VMEM((T, n, D), bf16) for n in sizes]
+        + [pltpu.VMEM((R - 1, T, n // R, D), bf16) for n in sizes]
+        + [pltpu.VMEM((T, n // R, D), bf16) for n in sizes]
+        + [
+            pltpu.VMEM((T, 8, 128), f32),
+            pltpu.SemaphoreType.DMA((count,)),
+            pltpu.SemaphoreType.DMA((count,)),
+        ],
+        compiler_params=pltpu.CompilerParams(
+            vmem_limit_bytes=VMEM_LIMIT, collective_id=3 + which, has_side_effects=True
+        ),
+        name="reduce_grads",
+        cost_estimate=pl.CostEstimate(flops=0, bytes_accessed=60 << 20, transcendentals=0),
+    )(*[ins[k] for k in names])
+
+
 def exchange(rows):
     return lax.all_to_all(rows, ("res", "tp"), split_axis=0, concat_axis=0, tiled=True)
 
@@ -714,15 +1084,14 @@
     MB, N, K, _ = edge_feats.shape
     devs = send_rows.shape[2]
     S = devs * send_rows.shape[3]
-    low = [v.astype(bf16) for v in masters]
-    vec = lax.all_gather(low[6], "tp", axis=0, tiled=True)
-    square = lax.all_gather(low[0], "tp", axis=1, tiled=True)
-    wedge = lax.all_gather(low[1], "tp", axis=0, tiled=True)
-    wup = lax.all_gather(low[2], "tp", axis=0, tiled=True)
-    wdown = lax.all_gather(low[3], "tp", axis=0, tiled=True)
-    vin = lax.all_gather(low[4], "tp", axis=1, tiled=True)
-    vsq = lax.all_gather(low[5], "tp", axis=1, tiled=True)
-    vec = vec.astype(f32)
+    R, T = lax.axis_size("res"), lax.axis_size("tp")
+    U, SP, EP, _ = place(R, T)
+    named = dict(zip(("square", "wedge", "up", "down", "vin", "vsq", "vec"), masters))
+    part = masters[6].shape[0]
+    named["vec"] = jnp.pad(masters[6], (0, 16 * D - part)).reshape(16, D)
+    l0, l1 = gather_weights(0, R, T, {k: named[k] for k in ("square", "wedge", "vec")})
+    m0, m1 = gather_weights(1, R, T, {k: named[k] for k in ("square", "up", "down", "vin", "vsq")})
+    vec = l1[:, U + SP : U + SP + 16, :].reshape(T, 16 * D)[:, :part].reshape(-1).astype(f32)
     rows = jnp.pad(vec[: 11 * D].reshape(11, D), ((0, 5), (0, 0)))
     c4 = jnp.pad(vec[11 * D : 11 * D + F].reshape(1, F), ((0, 7), (0, 0)))
     rowe = jnp.pad(vec[11 * D + F :].reshape(3, E), ((0, 5), (0, 0)))
@@ -734,16 +1103,16 @@
     own = (res_mask * (chain_ids + 1)).astype(f32)
     tags = jnp.broadcast_to(own.astype(bf16)[:, :, None], (MB, N, 128))
 
-    u1, send = node_in(node_feats, rows, srow, tags)
-    tabs = [exchange(send[m])[None] for m in range(MB)]
+    send = node_in(node_feats, srow, tags)
+    tabs = [exchange(send[m]) for m in range(MB)]
 
     mids, fwd, kept = [], [], []
     for m in range(MB):
-        a = msg_fwd(0 if False else m, slot, own, ef, tabs[m], u1, square, wedge, rows)
+        a = msg_fwd(m, slot, own, ef, tabs[m], node_feats, l0, l1, rows)
         p1, d1, d2, ps, cnt, vs = a
         fwd.append(a)
         out, x1, a2, q, qd, w, ys, wsend = node_mid(
-            m, ps, cnt, node_feats, square, wup, wdown, vin, rows, c4, rowe, srow
+            m, ps, cnt, node_feats, m0, m1, rows, c4, rowe, srow
         )
         kept.append((out, x1, a2, q, qd, w))
         mids.append((ys, exchange(wsend)))
@@ -752,7 +1121,7 @@
     for m in range(MB):
         ys, tab = mids[m]
         eo, gy1, gys_t, sums, dv, db = edge_net(
-            m, slot, fwd[m][5], ef, eup, tab, ys, vsq, rowe, before
+            m, slot, fwd[m][5], ef, eup, tab, ys, m1, rowe, before
         )
         before = (dv, db, eo)
         edges.append((gy1, gys_t, exchange(sums.astype(bf16))))
@@ -763,16 +1132,19 @@
         gy1, gys_t, inc = edges[m]
         p1, d1, d2, ps, cnt, vs = fwd[m]
         ho, gx1, *before = node_back(
-            m, inc, srow, gys_t, vin, kept[m], node_upstream, wup, wdown, square, rows, ps, cnt, before
+            m, inc, srow, gys_t, kept[m], node_upstream, m0, m1, rows, ps, cnt, before
         )
         backs.append((ho, gx1))
     dw3, dup, ddown, dvin, vr2, vw = before
+    gm0, gm1, sq = reduce_grads(
+        1, R, T, {"ddown": ddown, "dw3": dw3, "dup": dup, "dvin": dvin, "dvsq": dvsq}
+    )
     before = None
     last = []
     for m in range(MB):
         p1, d1, d2, ps, cnt, vs = fwd[m]
         ego, gzs_t, sums, dw2, dwe, dbm = msg_bwd(
-            m, S, slot, vs, ef, eup, p1, d1, d2, edges[m][0], backs[m][0], square, wedge, vsq, before
+            m, S, slot, vs, ef, eup, p1, d1, d2, edges[m][0], backs[m][0], l1, m1, before
         )
         before = (dw2, dwe, dbm, ego)
         last.append((gzs_t, exchange(sums.astype(bf16))))
@@ -781,7 +1153,7 @@
     node_grads = []
     for m in range(MB):
         gzs_t, inc = last[m]
-        ng, *before = node_end(m, inc, srow, gzs_t, u1, node_feats, backs[m][1], square, rows, before)
+        ng, *before = node_end(m, inc, srow, gzs_t, node_feats, backs[m][1], l0, rows, before)
         node_grads.append(ng)
     dws, vr1 = before
     vec_grad = jnp.concatenate(
@@ -790,27 +1162,34 @@
             vw[0], vr2[6, :E], dbe[1], dbe[2],
         ]
     )
-    locals_ = (
-        jnp.stack([dws[0], dws[1], dw2, dw3]), dwe, dup, ddown, dvin, dvsq, vec_grad,
+    vec_grad = jnp.pad(vec_grad.reshape(T, part), ((0, 0), (0, 16 * D - part))).reshape(T, 16, D)
+    gl0, gl1, norm = reduce_grads(
+        0, R, T, {"dws": dws, "dw2": dw2, "dwe": dwe, "vec": vec_grad, "sq": sq}
     )
-    dims = (1, 0, 0, 0, 1, 1, 0)
-    total = lax.psum(
-        tuple(
-            lax.psum_scatter(g, "tp", scatter_dimension=d, tiled=True) for g, d in zip(locals_, dims)
+    F4 = 4 * U
+    total = (
+        jnp.stack([gl0[0:U], gl0[U : 2 * U], gl1[0:U], gm0[F4 : F4 + U]]),
+        gl1[U : U + EP],
+        gm1[0:F4].reshape(4, U, D).transpose(1, 0, 2).reshape(U, F),
+        gm0[0:F4],
+        jnp.stack([gm1[F4 : F4 + U, 0:E], gm1[F4 : F4 + U, 256 : 256 + E]]),
+        jnp.stack(
+            [
+                gm1[F4 + U : F4 + U + EP, 0:E],
+                gm1[F4 + U : F4 + U + EP, 256 : 256 + E],
+                gm1[F4 + U + SP : F4 + U + SP + EP, 0:E],
+            ]
         ),
-        "res",
+        gl1[U + SP : U + SP + 16].reshape(-1)[:part],
     )
-    square_sum = jnp.zeros((), f32)
-    for part in total:
-        square_sum = square_sum + jnp.sum(part * part)
-    grad_norm = jnp.sqrt(lax.psum(square_sum, "tp"))
+    grad_norm = norm[0, 0]
     scale = clip_norm / jnp.maximum(grad_norm, clip_norm)
     first_fix = 1.0 - beta_first**STEP
     second_fix = 1.0 - beta_second**STEP
     new_w, new_f, new_s = [], [], []
     for i in range(7):
         decay, rate = (decay_rate, learn_rate) if i < 6 else (0.0, vector_rate)
-        clipped = total[i] * scale
+        clipped = total[i].astype(f32) * scale
         nf = beta_first * firsts[i] + (1.0 - beta_first) * clipped
         ns = beta_second * seconds[i] + (1.0 - beta_second) * clipped * clipped
         step = nf / first_fix / (jnp.sqrt(ns / second_fix) + adam_eps)

time: 838 us -> 527 us (0.63)
  waiting for transfers between devices: 335 us -> 0.02 us
  Pallas kernels: 216 us -> 410 us
  blocking collectives: 156 us -> 0 us
  between operations: 23 us -> 2.35 us
  other arithmetic: 43.8 us -> 24.4 us
  local copies, waits for them, and re-layouts: 16.3 us -> 34.9 us
    reduce_scatter x6 -> x0, waiting for transfers between devices: 235 us -> none  [shards(): lax.psum_scatter(g, 'tp', scatter_dimension=d, tiled=True)]
    pallas_call x1 -> x5, Pallas kernels: 2.8 us -> 197 us  [the longest x2 106 us: reduce_grads(): pl.pallas_call(functools.partial(reduce_body, which, R, T, names), in_spe...]
    all_gather x3 -> x0, blocking collectives: 80.8 us -> none  [the longest x1 44.7 us: shards(): wedge = lax.all_gather(low[1], 'tp', axis=0, tiled=True)]
    all_to_all x8, waiting for transfers between devices: 63.8 us -> 0.02 us  [exchange(): lax.all_to_all(rows, ('res', 'tp'), split_axis=0, concat_axis=0, tiled=True)]
    unnamed x2 -> x0, blocking collectives: 40.1 us -> none
    psum x2 -> x0, blocking collectives: 34.7 us -> none  [the longest x1 22.5 us: shards(): lax.psum(tuple((lax.psum_scatter(g, 'tp', scatter_dimension=d, tiled=True...]
    psum x1 -> x0, waiting for transfers between devices: 34.5 us -> none  [shards(): lax.psum(tuple((lax.psum_scatter(g, 'tp', scatter_dimension=d, tiled=True...]
    reduce_sum x7 -> x0, other arithmetic: 11.7 us -> none  [shards(): square_sum = square_sum + jnp.sum(part * part)]
  transfers between devices with their start and end apart: 18 -> 8, of which waited for: 8 -> 0; matrix products, arithmetic and copies ran while one was open for 3% -> 4% of each run, Pallas kernels for 26% -> 70%
where the time goes in v2:
time: 527 us; the launch traced here: 517 us
  Pallas kernels  410 us (78%)
  starting transfers between devices  45.5 us (9%)
  local copies, waits for them, and re-layouts  34.9 us (7%)
  other arithmetic  24.4 us (5%)
    pallas_call x2, Pallas kernels, reduce_grads(): pl.pallas_call(functools.partial(reduce_body, which, R, T, names), in_spe...  106 us
    pallas_call x2, Pallas kernels, gather_weights(): pl.pallas_call(functools.partial(gather_body, which, R, T, names), in_spe...  88.5 us
    pallas_call x2, Pallas kernels, msg_fwd(): pl.pallas_call(functools.partial(msg_fwd_body, m, KB, sub, S), grid=(K //...  56.3 us
    pallas_call x2, Pallas kernels, msg_bwd(): pl.pallas_call(functools.partial(msg_bwd_body, m, KB, sub, S, first), gri...  56.2 us
    pallas_call x2, Pallas kernels, edge_net(): pl.pallas_call(functools.partial(edge_body, m, KB, sub, S, first), grid=(...  54.3 us
    all_to_all x8, starting transfers between devices, exchange(): lax.all_to_all(rows, ('res', 'tp'), split_axis=0, concat_axis=0, tiled=True)  45.5 us
    pallas_call x2, Pallas kernels, node_back(): pl.pallas_call(node_back_body, grid=(1,), in_specs=[whole(S, E), picked(m...  25.6 us
    sub x7, other arithmetic, shards(): new_w.append(masters[i] - rate * (step + decay * masters[i]))  13.8 us
  transfers between devices with their start and end apart: 8, of which 0 were waited for; matrix products, arithmetic and copies ran while one was open for 4% of the time, Pallas kernels for 70%

profile of v2, /device:TPU:0, one launch (start us, length us, event | category | flops | bytes accessed | tf_op | source)
XLA Modules:
  0.0 517.5 jit_solution(13080559197782032028)
XLA Ops:
  2.2 1.3 fusion.14
  4.2 2.5 node_in.1
  6.8 2.4 fusion.15
  9.2 7.3 %all-to-all-start = ((bf16[32,16,640]{2,1,0:T(8,128)(2,1)}), bf16[32,16,640]{2,1,0:T(8,128)(2,1)S(1)}, u32[]{:S(2)}, u32[]{:S(2)}) async-start(bf16[32,16,640]{2,1,0:T(8,128)(2,1)} %bitcast.2), calls=%async_computation | async-start | bytes 1310720 | tf_op jit(solution)/shard_map/all_to_all | solution.py:1076
  17.9 35.2 %gather_weights.2 = (bf16[4,256,512]{2,1,0:T(8,128)(2,1)}, bf16[4,256,512]{2,1,0:T(8,128)(2,1)}) custom-call(f32[4,128,512]{2,1,0:T(8,128)} %refs_1_.1, f32[16,512]{1,0:T(8,128)} %reshape.116.refs_1_, f32[48,512]{1,0:T(8,128)} %refs_2_.2), custom_call_target="tpu_custom_call" | custom-call | bytes 62914560 | tf_op jit(solution)/shard_map/gather_weights/pallas_call | solution.py:900
  54.0 2.6 all-to-all-start.1
  60.7 53.3 %gather_weights.3 = (bf16[4,640,512]{2,1,0:T(8,128)(2,1)}, bf16[4,768,512]{2,1,0:T(8,128)(2,1)}) custom-call(f32[512,512]{1,0:T(8,128)} %refs_0_.3, f32[4,128,512]{2,1,0:T(8,128)} %refs_1_.1, f32[128,2048]{1,0:T(8,128)} %refs_2_.3, f32[2,128,192]{2,1,0:T(8,128)} %copy.94.refs_3_, f32[3,48,192]{2,1,0:T(8,128)} %refs_4_.1), custom_call_target="tpu_custom_call" | custom-call | bytes 62914560 | tf_op jit(solution)/shard_map/gather_weights/pallas_call | solution.py:900
  114.6 28.2 %msg_fwd.2 = (bf16[60,512,128]{2,1,0:T(8,128)(2,1)}, bf16[60,512,128]{2,1,0:T(8,128)(2,1)}, bf16[60,512,128]{2,1,0:T(8,128)(2,1)}, f32[512,128]{1,0:T(8,128)}, f32[8,128]{1,0:T(8,128)}, /*index=5*/f32[60,2,128]{2,1,0:T(2,128)}) custom-call(s32[60,2,128]{2,1,0:T(2,128)} %bitcast.126, f32[2,128]{1,0:T(2,128)} %get-tuple-element.294.own, ...), custom_call_target="tpu_custom_call" | custom-call | flops 10066329600 | bytes 23592960 | tf_op jit(solution)/shard_map/msg_fwd/pallas_call | solution.py:184
  142.8 6.0 %node_mid.2 = (f32[128,512]{1,0:T(8,128)}, f32[128,512]{1,0:T(8,128)}, bf16[128,512]{1,0:T(8,128)(2,1)}, bf16[128,2048]{1,0:T(8,128)(2,1)}, f32[128,2048]{1,0:T(...) custom-call(f32[512,128]{1,0:T(8,128)} %get-tuple-element.112.ps, ...), custom_call_target="tpu_custom_call" | custom-call | flops 536870912 | bytes 8388608 | tf_op jit(solution)/shard_map/node_mid/pallas_call | solution.py:590
  148.8 5.4 %all-to-all-start.3 = ((bf16[32,16,192]{2,1,0:T(8,128)(2,1)}), bf16[32,16,192]{2,1,0:T(8,128)(2,1)S(1)}, u32[]{:S(2)}, u32[]{:S(2)}) async-start(bf16[32,16,192]{2,1,0:T(8,128)(2,1)} %bitcast.93), calls=%async_computation.3 | async-start | bytes 524288 | tf_op jit(solution)/shard_map/all_to_all | solution.py:1076
  154.2 28.2 %msg_fwd.3 = (bf16[60,512,128]{2,1,0:T(8,128)(2,1)}, bf16[60,512,128]{2,1,0:T(8,128)(2,1)}, bf16[60,512,128]{2,1,0:T(8,128)(2,1)}, f32[512,128]{1,0:T(8,128)}, f32[8,128]{1,0:T(8,128)}, /*index=5*/f32[60,2,128]{2,1,0:T(2,128)}) custom-call(s32[60,2,128]{2,1,0:T(2,128)} %bitcast.127, f32[2,128]{1,0:T(2,128)} %get-tuple-element.294.own, ...), custom_call_target="tpu_custom_call" | custom-call | flops 10066329600 | bytes 23592960 | tf_op jit(solution)/shard_map/msg_fwd/pallas_call | solution.py:184
  182.4 6.0 %node_mid.3 = (f32[128,512]{1,0:T(8,128)}, f32[128,512]{1,0:T(8,128)}, bf16[128,512]{1,0:T(8,128)(2,1)}, bf16[128,2048]{1,0:T(8,128)(2,1)}, f32[128,2048]{1,0:T(...) custom-call(f32[512,128]{1,0:T(8,128)} %get-tuple-element.117.ps, ...), custom_call_target="tpu_custom_call" | custom-call | flops 536870912 | bytes 8388608 | tf_op jit(solution)/shard_map/node_mid/pallas_call | solution.py:590
  188.4 5.9 %all-to-all-start.2 = ((bf16[32,16,192]{2,1,0:T(8,128)(2,1)}), bf16[32,16,192]{2,1,0:T(8,128)(2,1)S(1)}, u32[]{:S(2)}, u32[]{:S(2)}) async-start(bf16[32,16,192]{2,1,0:T(8,128)(2,1)} %bitcast.95), calls=%async_computation.2 | async-start | bytes 524288 | tf_op jit(solution)/shard_map/all_to_all | solution.py:1076
  194.3 27.0 %edge_net.2 = (f32[2,60,192,128]{3,2,1,0:T(8,128)}, bf16[60,192,128]{2,1,0:T(8,128)(2,1)}, f32[192,128]{1,0:T(8,128)}, f32[512,192]{1,0:T(8,128)}, f32[3,192,192]{2,1,0:T(8,128)}, /*index=5*/f32[8,192]{1,0:T(8,128)}) custom-call(s32[60,2,128]{2,1,0:T(2,128)} %bitcast.128, f32[60,2,128]{2,1,0:T(2,128)} %get-tuple-element.123.vs, ...), custom_call_target="tpu_custom_call" | custom-call | flops 12079595520 | bytes 17694720 | tf_op jit(solution)/shard_map/edge_net/pallas_call | solution.py:328
  221.4 1.8 convert_element_type.67
  223.2 6.0 %all-to-all-start.4 = ((bf16[32,16,192]{2,1,0:T(8,128)(2,1)}), bf16[32,16,192]{2,1,0:T(8,128)(2,1)S(1)}, u32[]{:S(2)}, u32[]{:S(2)}) async-start(bf16[32,16,192]{2,1,0:T(8,128)(2,1)} %bitcast.15), calls=%async_computation.4 | async-start | bytes 524288 | tf_op jit(solution)/shard_map/all_to_all | solution.py:1076
  229.2 27.2 %edge_net.3 = (f32[2,60,192,128]{3,2,1,0:T(8,128)}, bf16[60,192,128]{2,1,0:T(8,128)(2,1)}, f32[192,128]{1,0:T(8,128)}, f32[512,192]{1,0:T(8,128)}, f32[3,192,192]{2,1,0:T(8,128)}, /*index=5*/f32[8,192]{1,0:T(8,128)}) custom-call(s32[60,2,128]{2,1,0:T(2,128)} %bitcast.129, f32[60,2,128]{2,1,0:T(2,128)} %get-tuple-element.120.vs, ...), custom_call_target="tpu_custom_call", output_to_operand_aliasing={{0}: (10, {})} | custom-call | flops 12079595520 | bytes 17694720 | tf_op jit(solution)/shard_map/edge_net/pallas_call | solution.py:328
  256.4 1.8 convert_element_type.69
  258.2 1.4 fusion.20
  259.6 5.9 %all-to-all-start.6 = ((bf16[32,16,192]{2,1,0:T(8,128)(2,1)}), bf16[32,16,192]{2,1,0:T(8,128)(2,1)S(1)}, u32[]{:S(2)}, u32[]{:S(2)}) async-start(bf16[32,16,192]{2,1,0:T(8,128)(2,1)} %bitcast.20), calls=%async_computation.6 | async-start | bytes 524288 | tf_op jit(solution)/shard_map/all_to_all | solution.py:1076
  265.6 11.4 %node_back.2 = (f32[512,128]{1,0:T(8,128)}, f32[128,512]{1,0:T(8,128)}, f32[512,512]{1,0:T(8,128)}, f32[512,2048]{1,0:T(8,128)}, f32[2048,512]{1,0:T(8,128)}, /*...) custom-call(bf16[512,192]{1,0:T(8,128)(2,1)} %bitcast.85, s32[2,1,512]{2,1,0:T(1,128)} %reshape.124.srow, ...), custom_call_target="tpu_custom_call" | custom-call | flops 1073741824 | bytes 20971520 | tf_op jit(solution)/shard_map/node_back/pallas_call | solution.py:676
  277.0 27.8 %msg_bwd.2 = (f32[2,60,192,128]{3,2,1,0:T(8,128)}, f32[512,128]{1,0:T(8,128)}, f32[512,512]{1,0:T(8,128)}, f32[512,512]{1,0:T(8,128)}, f32[192,512]{1,0:T(8,128)}, /*index=5*/f32[8,512]{1,0:T(8,128)}) custom-call(s32[60,2,128]{2,1,0:T(2,128)} %bitcast.130, f32[60,2,128]{2,1,0:T(2,128)} %get-tuple-element.123.vs, bf16[2,60,192,128]{3,2,1,0:T(8,128)(2,1)} %bitcast.120, ...), custom_call_target="tpu_custom_call" | custom-call | flops 16106127360 | bytes 39321600 | tf_op jit(solution)/shard_map/msg_bwd/pallas_call | solution.py:463
  304.8 2.1 convert_element_type.68
  306.9 6.0 %all-to-all-start.5 = ((bf16[32,16,512]{2,1,0:T(8,128)(2,1)}), bf16[32,16,512]{2,1,0:T(8,128)(2,1)S(1)}, u32[]{:S(2)}, u32[]{:S(2)}) async-start(bf16[32,16,512]{2,1,0:T(8,128)(2,1)} %bitcast.17), calls=%async_computation.5 | async-start | bytes 1048576 | tf_op jit(solution)/shard_map/all_to_all | solution.py:1076
  313.0 14.2 %node_back.3 = (f32[512,128]{1,0:T(8,128)}, f32[128,512]{1,0:T(8,128)}, f32[512,512]{1,0:T(8,128)}, f32[512,2048]{1,0:T(8,128)}, f32[2048,512]{1,0:T(8,128)}, /*...) custom-call(bf16[512,192]{1,0:T(8,128)(2,1)} %bitcast.84, ...), custom_call_target="tpu_custom_call", output_to_operand_aliasing={{2}: (17, {}), {3}: (18, {}), {4}: (19, {}), {5}: (20, {}),... | custom-call | flops 1073741824 | bytes 20971520 | tf_op jit(solution)/shard_map/node_back/pallas_call | solution.py:676
  327.2 28.3 %msg_bwd.3 = (f32[2,60,192,128]{3,2,1,0:T(8,128)}, f32[512,128]{1,0:T(8,128)}, f32[512,512]{1,0:T(8,128)}, f32[512,512]{1,0:T(8,128)}, f32[192,512]{1,0:T(8,128)}, /*index=5*/f32[8,512]{1,0:T(8,128)}) custom-call(s32[60,2,128]{2,1,0:T(2,128)} %bitcast.131, f32[60,2,128]{2,1,0:T(2,128)} %get-tuple-element.120.vs, ...), custom_call_target="tpu_custom_call", output_to_operand_aliasing={{0}: (15, {})} | custom-call | flops 16106127360 | bytes 39321600 | tf_op jit(solution)/shard_map/msg_bwd/pallas_call | solution.py:463
  355.5 2.1 convert_element_type.70
  357.6 6.2 %all-to-all-start.7 = ((bf16[32,16,512]{2,1,0:T(8,128)(2,1)}), bf16[32,16,512]{2,1,0:T(8,128)(2,1)S(1)}, u32[]{:S(2)}, u32[]{:S(2)}) async-start(bf16[32,16,512]{2,1,0:T(8,128)(2,1)} %bitcast.22), calls=%async_computation.7 | async-start | bytes 1048576 | tf_op jit(solution)/shard_map/all_to_all | solution.py:1076
  363.8 1.4 fusion.18
  366.6 67.0 %reduce_grads.2 = (bf16[640,512]{1,0:T(8,128)(2,1)}, bf16[768,512]{1,0:T(8,128)(2,1)}, f32[8,128]{1,0:T(8,128)}) custom-call(f32[2048,512]{1,0:T(8,128)} %get-tuple-element.178.refs_0_, f32[512,2048]{1,0:T(8,128)} %get-tuple-element.179.refs_1_, f32[2,512,192]{2,1,0:T(8,128)} %get-tuple-element.180.refs_2_, f32[3,192,192]{2,1,0:T(8,128)} %get-tuple-element.181.refs_3_, ...), custom_call_target="tpu_custom_call" | custom-call | bytes 62914560 | tf_op jit(solution)/shard_map/reduce_grads/pallas_call | solution.py:1053
  434.2 1.4 slice_bitcast_fusion.9
  435.6 1.5 slice_bitcast_fusion.5
  438.0 4.0 node_end.2
  442.9 4.9 node_end.3
  447.8 1.4 fusion.19
  449.2 1.5 concatenate.3
  450.7 1.5 reshape.120
  453.6 39.1 %reduce_grads.3 = (bf16[256,512]{1,0:T(8,128)(2,1)}, bf16[256,512]{1,0:T(8,128)(2,1)}, f32[8,128]{1,0:T(8,128)}) custom-call(f32[512,512]{1,0:T(8,128)} %get-tuple-element.175.refs_0_, f32[192,512]{1,0:T(8,128)} %get-tuple-element.176.refs_1_, f32[2,512,512]{2,1,0:T(8,128)} %get-tuple-element.177.refs_2_, f32[8,128]{1,0:T(8,128)} %get-tuple-element.183.refs_3_, ...), custom_call_target="tpu_custom_call" | custom-call | bytes 62914560 | tf_op jit(solution)/shard_map/reduce_grads/pallas_call | solution.py:1053
  493.4 1.2 slice.135
  495.3 2.1 multiply_subtract_fusion.3
  497.5 1.8 copy.109
  499.2 1.8 copy.110
  501.0 1.8 copy.111
  502.8 3.7 multiply_subtract_fusion
  506.8 1.2 slice_bitcast_fusion.3
  508.0 2.0 multiply_subtract_fusion.5
  510.6 2.2 multiply_subtract_fusion.1
  514.8 2.3 multiply_subtract_fusion.2
  (110 shorter events, 17.8 us)
Async XLA Ops:
  0.7 56.8 %copy-start.23 = (f32[2,128,192]{1,2,0:T(8,128)S(1)}, f32[2,128,192]{1,2,0:T(8,128)}, u32[]{:S(2)}) copy-start(f32[2,128,192]{1,2,0:T(8,128)} %param.41) | copy-start | bytes 589828
  0.7 58.3 %copy-start.24 = (f32[2,128,192]{1,2,0:T(8,128)S(1)}, f32[2,128,192]{1,2,0:T(8,128)}, u32[]{:S(2)}) copy-start(f32[2,128,192]{1,2,0:T(8,128)} %param.48) | copy-start | bytes 589828
  0.7 59.2 %copy-start.25 = (f32[2,128,192]{1,2,0:T(8,128)S(1)}, f32[2,128,192]{1,2,0:T(8,128)}, u32[]{:S(2)}) copy-start(f32[2,128,192]{1,2,0:T(8,128)} %param.55) | copy-start | bytes 589828
  9.2 44.8 %all-to-all-start = ((bf16[32,16,640]{2,1,0:T(8,128)(2,1)}), bf16[32,16,640]{2,1,0:T(8,128)(2,1)S(1)}, u32[]{:S(2)}, u32[]{:S(2)}) async-start(bf16[32,16,640]{2,1,0:T(8,128)(2,1)} %bitcast.2), calls=%async_computation | async-start | bytes 1310720 | tf_op jit(solution)/shard_map/all_to_all | solution.py:1076
  54.0 60.6 %copy-start.17 = (bf16[32,16,640]{2,1,0:T(8,128)(2,1)}, bf16[32,16,640]{2,1,0:T(8,128)(2,1)S(1)}, u32[]{:S(2)}) copy-start(bf16[32,16,640]{2,1,0:T(8,128)(2,1)S(1)} %all-to-all-done) | copy-start | bytes 1966084
  54.0 94.8 %all-to-all-start.1 = ((bf16[32,16,640]{2,1,0:T(8,128)(2,1)}), bf16[32,16,640]{2,1,0:T(8,128)(2,1)S(1)}, u32[]{:S(2)}, u32[]{:S(2)}) async-start(bf16[32,16,640]{2,1,0:T(8,128)(2,1)} %bitcast.6), calls=%async_computation.1 | async-start | bytes 1310720 | tf_op jit(solution)/shard_map/all_to_all | solution.py:1076
  148.8 5.4 %copy-start.16 = (bf16[32,16,640]{2,1,0:T(8,128)(2,1)}, bf16[32,16,640]{2,1,0:T(8,128)(2,1)S(1)}, u32[]{:S(2)}) copy-start(bf16[32,16,640]{2,1,0:T(8,128)(2,1)S(1)} %all-to-all-done.1) | copy-start | bytes 1966084
  148.8 39.6 %all-to-all-start.3 = ((bf16[32,16,192]{2,1,0:T(8,128)(2,1)}), bf16[32,16,192]{2,1,0:T(8,128)(2,1)S(1)}, u32[]{:S(2)}, u32[]{:S(2)}) async-start(bf16[32,16,192]{2,1,0:T(8,128)(2,1)} %bitcast.93), calls=%async_computation.3 | async-start | bytes 524288 | tf_op jit(solution)/shard_map/all_to_all | solution.py:1076
  188.4 6.0 %copy-start.19 = (bf16[32,16,192]{2,1,0:T(8,128)(2,1)}, bf16[32,16,192]{2,1,0:T(8,128)(2,1)S(1)}, u32[]{:S(2)}) copy-start(bf16[32,16,192]{2,1,0:T(8,128)(2,1)S(1)} %all-to-all-done.3) | copy-start | bytes 589828
  188.4 34.8 %all-to-all-start.2 = ((bf16[32,16,192]{2,1,0:T(8,128)(2,1)}), bf16[32,16,192]{2,1,0:T(8,128)(2,1)S(1)}, u32[]{:S(2)}, u32[]{:S(2)}) async-start(bf16[32,16,192]{2,1,0:T(8,128)(2,1)} %bitcast.95), calls=%async_computation.2 | async-start | bytes 524288 | tf_op jit(solution)/shard_map/all_to_all | solution.py:1076
  223.2 6.0 %copy-start.20 = (bf16[32,16,192]{2,1,0:T(8,128)(2,1)}, bf16[32,16,192]{2,1,0:T(8,128)(2,1)S(1)}, u32[]{:S(2)}) copy-start(bf16[32,16,192]{2,1,0:T(8,128)(2,1)S(1)} %all-to-all-done.2) | copy-start | bytes 589828
  223.2 36.4 %all-to-all-start.4 = ((bf16[32,16,192]{2,1,0:T(8,128)(2,1)}), bf16[32,16,192]{2,1,0:T(8,128)(2,1)S(1)}, u32[]{:S(2)}, u32[]{:S(2)}) async-start(bf16[32,16,192]{2,1,0:T(8,128)(2,1)} %bitcast.15), calls=%async_computation.4 | async-start | bytes 524288 | tf_op jit(solution)/shard_map/all_to_all | solution.py:1076
  259.6 6.0 %copy-start.7 = (bf16[32,16,192]{2,1,0:T(8,128)(2,1)}, bf16[32,16,192]{2,1,0:T(8,128)(2,1)S(1)}, u32[]{:S(2)}) copy-start(bf16[32,16,192]{2,1,0:T(8,128)(2,1)S(1)} %all-to-all-done.4) | copy-start | bytes 589828
  259.6 47.3 %all-to-all-start.6 = ((bf16[32,16,192]{2,1,0:T(8,128)(2,1)}), bf16[32,16,192]{2,1,0:T(8,128)(2,1)S(1)}, u32[]{:S(2)}, u32[]{:S(2)}) async-start(bf16[32,16,192]{2,1,0:T(8,128)(2,1)} %bitcast.20), calls=%async_computation.6 | async-start | bytes 524288 | tf_op jit(solution)/shard_map/all_to_all | solution.py:1076
  306.9 6.1 %copy-start.6 = (bf16[32,16,192]{2,1,0:T(8,128)(2,1)}, bf16[32,16,192]{2,1,0:T(8,128)(2,1)S(1)}, u32[]{:S(2)}) copy-start(bf16[32,16,192]{2,1,0:T(8,128)(2,1)S(1)} %all-to-all-done.6) | copy-start | bytes 589828
  306.9 50.7 %all-to-all-start.5 = ((bf16[32,16,512]{2,1,0:T(8,128)(2,1)}), bf16[32,16,512]{2,1,0:T(8,128)(2,1)S(1)}, u32[]{:S(2)}, u32[]{:S(2)}) async-start(bf16[32,16,512]{2,1,0:T(8,128)(2,1)} %bitcast.17), calls=%async_computation.5 | async-start | bytes 1048576 | tf_op jit(solution)/shard_map/all_to_all | solution.py:1076
  327.2 38.9 %copy-start.31 = (f32[8,512]{1,0:T(8,128)S(1)}, f32[8,512]{1,0:T(8,128)}, u32[]{:S(2)}) copy-start(f32[8,512]{1,0:T(8,128)} %get-tuple-element.185) | copy-start | bytes 49156
  357.6 76.0 %copy-start.5 = (bf16[32,16,512]{2,1,0:T(8,128)(2,1)}, bf16[32,16,512]{2,1,0:T(8,128)(2,1)S(1)}, u32[]{:S(2)}) copy-start(bf16[32,16,512]{2,1,0:T(8,128)(2,1)S(1)} %all-to-all-done.5) | copy-start | bytes 1572868
  357.6 84.5 %all-to-all-start.7 = ((bf16[32,16,512]{2,1,0:T(8,128)(2,1)}), bf16[32,16,512]{2,1,0:T(8,128)(2,1)S(1)}, u32[]{:S(2)}, u32[]{:S(2)}) async-start(bf16[32,16,512]{2,1,0:T(8,128)(2,1)} %bitcast.22), calls=%async_computation.7 | async-start | bytes 1048576 | tf_op jit(solution)/shard_map/all_to_all | solution.py:1076
  438.0 57.3 %copy-start.3 = (f32[2,128,192]{2,1,0:T(8,128)S(1)}, f32[2,128,192]{2,1,0:T(8,128)}, u32[]{:S(2)}) copy-start(f32[2,128,192]{2,1,0:T(8,128)} %copy.94.refs_3_) | copy-start | bytes 589828
  442.1 0.8 copy-start.4
  442.9 59.9 %copy-start.1 = (f32[512,512]{1,0:T(8,128)S(1)}, f32[512,512]{1,0:T(8,128)}, u32[]{:S(2)}) copy-start(f32[512,512]{1,0:T(8,128)} %refs_0_.3) | copy-start | bytes 3145732
  442.9 59.9 %copy-start.10 = (f32[512,512]{1,0:T(8,128)S(1)}, f32[512,512]{1,0:T(8,128)}, u32[]{:S(2)}) copy-start(f32[512,512]{1,0:T(8,128)} %param.47) | copy-start | bytes 3145732
  447.8 55.0 %copy-start.11 = (f32[512,512]{1,0:T(8,128)S(1)}, f32[512,512]{1,0:T(8,128)}, u32[]{:S(2)}) copy-start(f32[512,512]{1,0:T(8,128)} %param.54) | copy-start | bytes 3145732
  502.8 7.2 %copy-start.32 = (f32[2064]{0:T(1024)S(1)}, f32[2064]{0:T(1024)}, u32[]{:S(2)}) copy-start(f32[2064]{0:T(1024)} %param.43) | copy-start | bytes 24772
  502.8 7.2 %copy-start.33 = (f32[2064]{0:T(1024)S(1)}, f32[2064]{0:T(1024)}, u32[]{:S(2)}) copy-start(f32[2064]{0:T(1024)} %param.50) | copy-start | bytes 24772
  502.8 7.2 %copy-start.34 = (f32[2064]{0:T(1024)S(1)}, f32[2064]{0:T(1024)}, u32[]{:S(2)}) copy-start(f32[2064]{0:T(1024)} %param.57) | copy-start | bytes 24772
  502.8 7.8 %copy-start.2 = (f32[128,2048]{1,0:T(8,128)S(1)}, f32[128,2048]{1,0:T(8,128)}, u32[]{:S(2)}) copy-start(f32[128,2048]{1,0:T(8,128)} %refs_2_.3) | copy-start | bytes 3145732
  502.8 7.8 %copy-start.12 = (f32[128,2048]{1,0:T(8,128)S(1)}, f32[128,2048]{1,0:T(8,128)}, u32[]{:S(2)}) copy-start(f32[128,2048]{1,0:T(8,128)} %param.46) | copy-start | bytes 3145732
  502.8 7.8 %copy-start.13 = (f32[128,2048]{1,0:T(8,128)S(1)}, f32[128,2048]{1,0:T(8,128)}, u32[]{:S(2)}) copy-start(f32[128,2048]{1,0:T(8,128)} %param.53) | copy-start | bytes 3145732
  506.6 6.3 %copy-start.8 = (f32[128,512]{1,0:T(8,128)S(1)}, f32[128,512]{1,0:T(8,128)}, u32[]{:S(2)}) copy-start(f32[128,512]{1,0:T(8,128)} %get-tuple-element.116.out) | copy-start | bytes 786436
  506.6 6.3 %copy-start.9 = (f32[128,512]{1,0:T(8,128)S(1)}, f32[128,512]{1,0:T(8,128)}, u32[]{:S(2)}) copy-start(f32[128,512]{1,0:T(8,128)} %get-tuple-element.119.out) | copy-start | bytes 786436
  506.6 6.3 %copy-start.21 = (f32[128,512]{1,0:T(8,128)S(1)}, f32[128,512]{1,0:T(8,128)}, u32[]{:S(2)}) copy-start(f32[128,512]{1,0:T(8,128)} %get-tuple-element.145) | copy-start | bytes 786436
  506.6 6.3 %copy-start.22 = (f32[128,512]{1,0:T(8,128)S(1)}, f32[128,512]{1,0:T(8,128)}, u32[]{:S(2)}) copy-start(f32[128,512]{1,0:T(8,128)} %get-tuple-element.173) | copy-start | bytes 786436
  506.7 7.2 %copy-start.18 = (f32[3,48,192]{2,1,0:T(8,128)S(1)}, f32[3,48,192]{2,1,0:T(8,128)}, u32[]{:S(2)}) copy-start(f32[3,48,192]{2,1,0:T(8,128)} %refs_4_.1) | copy-start | bytes 331780
  506.7 7.2 %copy-start.26 = (f32[3,48,192]{2,1,0:T(8,128)S(1)}, f32[3,48,192]{2,1,0:T(8,128)}, u32[]{:S(2)}) copy-start(f32[3,48,192]{2,1,0:T(8,128)} %param.49) | copy-start | bytes 331780
  506.7 7.2 %copy-start.27 = (f32[3,48,192]{2,1,0:T(8,128)S(1)}, f32[3,48,192]{2,1,0:T(8,128)}, u32[]{:S(2)}) copy-start(f32[3,48,192]{2,1,0:T(8,128)} %param.56) | copy-start | bytes 331780
  506.7 7.2 %copy-start.28 = (bf16[1,48,192]{2,1,0:T(8,128)(2,1)S(1)}, bf16[1,48,192]{2,1,0:T(8,128)(2,1)}, u32[]{:S(2)}) copy-start(bf16[1,48,192]{2,1,0:T(8,128)(2,1)} %get-tuple-element.297) | copy-start | bytes 55300
  506.7 7.2 %copy-start.29 = (bf16[1,48,192]{2,1,0:T(8,128)(2,1)S(1)}, bf16[1,48,192]{2,1,0:T(8,128)(2,1)}, u32[]{:S(2)}) copy-start(bf16[1,48,192]{2,1,0:T(8,128)(2,1)} %get-tuple-element.298) | copy-start | bytes 55300
  506.7 7.2 %copy-start.30 = (bf16[1,48,192]{2,1,0:T(8,128)(2,1)S(1)}, bf16[1,48,192]{2,1,0:T(8,128)(2,1)}, u32[]{:S(2)}) copy-start(bf16[1,48,192]{2,1,0:T(8,128)(2,1)} %get-tuple-element.299) | copy-start | bytes 55300
  506.7 8.0 %copy-start = (f32[4,128,512]{2,1,0:T(8,128)S(1)}, f32[4,128,512]{2,1,0:T(8,128)}, u32[]{:S(2)}) copy-start(f32[4,128,512]{2,1,0:T(8,128)} %refs_1_.1) | copy-start | bytes 3145732
  506.7 8.0 %copy-start.14 = (f32[4,128,512]{2,1,0:T(8,128)S(1)}, f32[4,128,512]{2,1,0:T(8,128)}, u32[]{:S(2)}) copy-start(f32[4,128,512]{2,1,0:T(8,128)} %param.44) | copy-start | bytes 3145732
  506.8 8.0 %copy-start.15 = (f32[4,128,512]{2,1,0:T(8,128)S(1)}, f32[4,128,512]{2,1,0:T(8,128)}, u32[]{:S(2)}) copy-start(f32[4,128,512]{2,1,0:T(8,128)} %param.51) | copy-start | bytes 3145732
